TPU v7x, 256 devices: a whole 4x4x8 slice. The times are simulated.
256 devices in a mesh: tensor: 4 (over y), prompt: 16 (over x_lo, z), cand: 4 (over x_hi, core).
Axes of the slice: x: 4 (x_hi: 2, x_lo: 2; x = x_hi * 2 + x_lo), y: 4, z: 8, core: 2. Of those that a mesh axis runs over, the one named last changes fastest.
Arguments:
- q_step: bfloat16 [512, 2, 4096], P(('prompt', 'cand'), None, 'tensor')
- step_k: bfloat16 [512, 2, 512], P(('prompt', 'cand'), None, 'tensor')
- step_values: bfloat16 [512, 2, 512], P(('prompt', 'cand'), None, 'tensor'), may hold values from -6 to 6
- prefix_k: bfloat16 [32, 4096, 512], P('prompt', 'cand', 'tensor'), may hold values from -13 to 13
- prefix_v: bfloat16 [32, 4096, 512], P('prompt', 'cand', 'tensor'), may hold values from -6 to 6
- suffix_k: bfloat16 [512, 2048, 512], P(('prompt', 'cand'), None, 'tensor')
- suffix_values: bfloat16 [512, 2048, 512], P(('prompt', 'cand'), None, 'tensor'), may hold values from -6 to 6
- lengths: int32 [512], P(('prompt', 'cand')), may hold values from 256 to 2048, as said below
- placement: int32 [16, 32], P('prompt'), may hold values from 0 to 31, each once within a row
- output_weight: bfloat16 [4096, 8192], P(('tensor', 'cand')), may hold values from -0.5 to 0.5
Outputs:
- projected: bfloat16 [512, 2, 8192], P('prompt', None, ('tensor', 'cand'))
Inputs may be any that keep to these rules, and one draw needn't show every extreme that they name: Each row is a permutation; the slot in column r of row p holds a candidate of prompt placement[p, r], so every prompt index holds 1 candidates of every prompt. `lengths`: some slot has exactly 2048 live positions and some slot exactly 256.
All inputs are finite; a program needn't handle non-finite values.
Results may differ from a plain program's by a relative error of at most 0.019.
Values may be sent and summed in bfloat16 or wider, within the bound.
No kernel may reach another device: no remote copies, remote signals or barrier semaphores. Data moves between devices by JAX's collectives and lax.ppermute only.
A program may use at most 128 MiB of HBM per device.

v0:
```python
import math

import jax
import jax.numpy as jnp
from jax import lax
from jax.sharding import PartitionSpec as P

HEAD_WIDTH = 128
BLOCK = 512


hidden_mask = -1e30


def joined(array, axis, combine):
    everything = jax.tree.map(lambda part: lax.all_gather(part, axis), array)
    first = jax.tree.map(lambda part: part[0], everything)

    def hop(k, so_far):
        return combine(so_far, jax.tree.map(lambda part: part[k], everything))

    return lax.fori_loop(1, lax.axis_size(axis), hop, first)


def combine_parts(part_one, part_two):
    max_one, total_one, sum_one = part_one
    max_two, total_two, sum_two = part_two
    highest = jnp.maximum(max_one, max_two)
    scale_one = jnp.exp(max_one - highest)
    scale_two = jnp.exp(max_two - highest)
    width_ratio = sum_one.shape[-1] // max_one.shape[-1]
    merged_sum = sum_one * jnp.repeat(scale_one, width_ratio, axis=-1) + sum_two * jnp.repeat(
        scale_two, width_ratio, axis=-1
    )
    return (highest, total_one * scale_one + total_two * scale_two, merged_sum)


def prefix_partial(query_rows, key_rows, value_rows, kv_heads):
    outer_count, prompt_count, inner_count, token_count, query_width = query_rows.shape
    row_length = key_rows.shape[1]
    group_size = query_width // (kv_heads * HEAD_WIDTH)
    shaped = query_rows.reshape(
        outer_count, prompt_count, inner_count, token_count, kv_heads, group_size, HEAD_WIDTH
    )
    key_view = key_rows.reshape(prompt_count, row_length, kv_heads, HEAD_WIDTH)
    value_view = value_rows.reshape(prompt_count, row_length, kv_heads, HEAD_WIDTH)
    scores = jnp.einsum(
        "apbtkgd,plkd->apbtkgl", shaped, key_view, preferred_element_type=jnp.float32
    ) * (1.0 / math.sqrt(HEAD_WIDTH))
    maxima = jnp.max(scores, axis=-1)
    weights = jnp.exp(scores - maxima[..., None])
    totals = jnp.sum(weights, axis=-1)
    numerators = jnp.einsum(
        "apbtkgl,plkd->apbtkgd",
        weights.astype(jnp.bfloat16),
        value_view,
        preferred_element_type=jnp.float32,
    )
    row_count = outer_count * prompt_count * inner_count
    head_total = kv_heads * group_size
    return (
        maxima.reshape(row_count, token_count, head_total),
        totals.reshape(row_count, token_count, head_total),
        numerators.reshape(row_count, token_count, query_width),
    )


def slot_partial(shaped, key_rows, value_rows, visible, kv_heads):
    slot_count, token_count = (shaped.shape[0], shaped.shape[1])
    row_count = key_rows.shape[1]
    key_view = key_rows.reshape(slot_count, row_count, kv_heads, HEAD_WIDTH)
    value_view = value_rows.reshape(slot_count, row_count, kv_heads, HEAD_WIDTH)
    scores = jnp.einsum(
        "stkgd,slkd->stkgl", shaped, key_view, preferred_element_type=jnp.float32
    ) * (1.0 / math.sqrt(HEAD_WIDTH))
    scores = jnp.where(visible[:, :, None, None, :], scores, hidden_mask)
    maxima = jnp.max(scores, axis=-1)
    weights = jnp.exp(scores - maxima[..., None])
    totals = jnp.sum(weights, axis=-1)
    numerators = jnp.einsum(
        "stkgl,slkd->stkgd",
        weights.astype(jnp.bfloat16),
        value_view,
        preferred_element_type=jnp.float32,
    )
    head_total = maxima.shape[2] * maxima.shape[3]
    return (
        maxima.reshape(slot_count, token_count, head_total),
        totals.reshape(slot_count, token_count, head_total),
        numerators.reshape(slot_count, token_count, head_total * HEAD_WIDTH),
    )


def body(
    q_step,
    step_k,
    step_values,
    prefix_k,
    prefix_v,
    suffix_k,
    suffix_values,
    lengths,
    placement,
    output_weight,
):
    slot_count, token_count, query_width = q_step.shape
    kv_heads = step_k.shape[2] // HEAD_WIDTH
    head_count = query_width // HEAD_WIDTH
    group_size = head_count // kv_heads
    slots_here = placement.shape[1]
    local_prompts = prefix_k.shape[0]
    spread = slots_here // (local_prompts * lax.axis_size("prompt"))
    gathered = lax.all_gather(q_step, "cand", axis=0, tiled=True)
    lookup = placement[0][None, :] == jnp.arange(slots_here, dtype=jnp.int32)[:, None]
    ordered = jnp.einsum(
        "us,sx->ux",
        lookup.astype(jnp.bfloat16),
        gathered.reshape(slots_here, token_count * query_width),
        preferred_element_type=jnp.float32,
    )
    ordered = ordered.astype(jnp.bfloat16).reshape(slots_here, token_count, query_width)
    key_piece = lax.all_gather(prefix_k, "prompt", axis=0, tiled=True)
    value_piece = lax.all_gather(prefix_v, "prompt", axis=0, tiled=True)
    piece_count = key_piece.shape[0]
    shaped = ordered.reshape(1, piece_count, spread, token_count, query_width)
    fresh = prefix_partial(shaped, key_piece, value_piece, kv_heads)
    prefix_max, prefix_total, prefix_sum = tuple((fresh_rows for fresh_rows in fresh))
    reverse_map = lookup.astype(jnp.float32)

    def to_slot_order(values_in):
        return jnp.einsum("us,u...->s...", reverse_map, values_in, precision=lax.Precision.HIGHEST)

    cand_index = lax.axis_index("cand")
    merged = joined((prefix_max, prefix_total, prefix_sum), "cand", combine_parts)
    own_prefix = tuple(
        (
            lax.dynamic_slice_in_dim(to_slot_order(member), cand_index * slot_count, slot_count, 0)
            for member in merged
        )
    )
    token_order = jnp.arange(token_count, dtype=jnp.int32)
    causal = token_order[None, :] <= token_order[:, None]
    shaped_all = q_step.reshape(slot_count, token_count, kv_heads, group_size, HEAD_WIDTH)
    causal_all = jnp.broadcast_to(causal[None], (slot_count, token_count, token_count))
    running = slot_partial(shaped_all, step_k, step_values, causal_all, kv_heads)
    block_order = jnp.arange(BLOCK, dtype=jnp.int32)
    block_total = suffix_k.shape[1] // BLOCK

    def add_block(block_index, current):
        block_start = block_index * BLOCK
        key_block = lax.dynamic_slice_in_dim(suffix_k, block_start, BLOCK, 1)
        value_block = lax.dynamic_slice_in_dim(suffix_values, block_start, BLOCK, 1)
        live = (block_start + block_order)[None, :] < lengths[:, None]
        visible = jnp.broadcast_to(live[:, None, :], (slot_count, token_count, BLOCK))
        return combine_parts(
            current, slot_partial(shaped_all, key_block, value_block, visible, kv_heads)
        )

    local_parts = lax.fori_loop(0, block_total, add_block, running)
    final_max, final_total, final_sum = combine_parts(own_prefix, local_parts)
    attention_output = (final_sum / jnp.repeat(final_total, HEAD_WIDTH, axis=-1)).astype(
        jnp.bfloat16
    )
    projected = jnp.einsum(
        "stx,xd->std",
        lax.all_to_all(attention_output, "cand", split_axis=2, concat_axis=0, tiled=True),
        output_weight,
        preferred_element_type=jnp.float32,
    )
    return lax.psum_scatter(
        projected.astype(jnp.bfloat16), ("tensor", "cand"), scatter_dimension=2, tiled=True
    )


def solution(mesh):
    return jax.shard_map(
        body,
        mesh=mesh,
        in_specs=(
            P(("prompt", "cand"), None, "tensor"),
            P(("prompt", "cand"), None, "tensor"),
            P(("prompt", "cand"), None, "tensor"),
            P("prompt", "cand", "tensor"),
            P("prompt", "cand", "tensor"),
            P(("prompt", "cand"), None, "tensor"),
            P(("prompt", "cand"), None, "tensor"),
            P(("prompt", "cand")),
            P("prompt", None),
            P(("tensor", "cand"), None),
        ),
        out_specs=P("prompt", None, ("tensor", "cand")),
        check_vma=False,
    )
```

profile of v0, /device:TPU:1, one launch (start us, length us, event | category | flops | bytes accessed | tf_op | source)
XLA Modules:
  0.0 351.2 jit_solution(1695366697476104631)
XLA Ops:
  6.5 0.7 all-gather.6.cloned.1.call-update
  7.3 0.7 all-gather.8.cloned.1.call-update
  8.1 0.8 reshape.164
  8.8 0.8 reshape.167
  9.6 10.2 %all_gather.18 = bf16[32,2,1024]{2,1,0:T(2,128)(2,1)S(1)} all-gather(bf16[8,2,1024]{2,1,0:T(2,128)(2,1)} %param.14), channel_id=1, replica_groups=mesh['tensor'=4,'prompt'=16,'cand'=4] {'cand'}, dimensions={0}, use_global_device_ids=true | all-gather | bytes 163840 | tf_op jit(solution)/shard_map/all_gather | solution.py:113
  19.9 0.9 fusion.32
  20.9 1.0 fusion.69
  21.8 0.2 convolution_bitcast_fusion.1
  22.1 91.8 %all-gather.6.cloned.1.call-done = bf16[32,1024,128]{2,1,0:T(8,128)(2,1)} async-done(((bf16[2,1024,128]{2,1,0:T(8,128)(2,1)}), bf16[32,1024,128]{2,1,0:T(8,128)(2,1)}) %all-gather.6.cloned.1.call-update) | async-done | bytes 8388624 | tf_op jit(solution)/shard_map/all_gather | solution.py:122
  114.0 5.8 %bitcast_reduce_fusion = (f32[32,2,8]{2,1,0:T(2,128)S(1)}, f32[32,2,8,1024]{3,2,1,0:T(8,128)S(1)}) fusion(bf16[32,2,8,128]{3,2,1,0:T(8,128)(2,1)S(1)} %bitcast.251, bf16[32,1024,128]{2,1,0:T(8,128)(2,1)} %all-gather.6.cloned.1.call-done), kind=kOutput, calls=%fused_computation.42 | convolution fusion | flops 135265792 | bytes 10618880 | tf_op jit(solution)/shard_map/apbtkgd,plkd->apbtkgl/dot_general | solution.py:47
  119.7 94.7 %all-gather.8.cloned.1.call-done = bf16[32,1024,128]{2,1,0:T(8,128)(2,1)} async-done(((bf16[2,1024,128]{2,1,0:T(8,128)(2,1)}), bf16[32,1024,128]{2,1,0:T(8,128)(2,1)}) %all-gather.8.cloned.1.call-update) | async-done | bytes 8388624 | tf_op jit(solution)/shard_map/all_gather | solution.py:123
  214.5 4.8 %fusion.29 = f32[1,32,1,2,1,8,128]{6,5,3,1,2,0,4:T(8,128)S(1)} fusion(bf16[32,1024,128]{2,1,0:T(8,128)(2,1)} %all-gather.8.cloned.1.call-done, f32[32,2,8,1024]{3,2,1,0:T(8,128)S(1)} %get-tuple-element.423, f32[32,2,8]{2,1,0:T(2,128)S(1)} %get-tuple-element.422), kind=kOutput, calls=%fused_computation.46 | convolution fusion | flops 135790592 | bytes 10749952 | tf_op jit(solution)/shard_map/apbtkgl,plkd->apbtkgd/dot_general | solution.py:53
  219.5 0.8 copy.39
  220.3 15.6 %while.38 = (s32[]{:T(128)}, f32[8,2,8]{2,1,0:T(2,128)S(1)}, f32[8,2,8]{2,1,0:T(2,128)S(1)}, f32[8,2,1024]{2,1,0:T(2,128)S(1)}, s32[8]{0:T(128)S(1)}, /*index=5*...) while((s32[]{:T(128)}, f32[8,2,8]{2,1,0:T(2,128)S(1)}, ...), condition=%wide.region_9.10_spmd.clone, body=%wide.region_6.9_spmd.clone.sunk | while | flops 34067460 | bytes 3853519 | solution.py:159
  220.4 1.7 fusion.85
  222.1 1.5 convolution_bitcast_fusion.3
  223.7 0.2 fusion.86
  224.3 1.7 fusion.85
  226.0 1.5 convolution_bitcast_fusion.3
  227.6 0.2 fusion.86
  228.2 1.7 fusion.85
  229.9 1.6 convolution_bitcast_fusion.3
  231.6 0.2 fusion.86
  232.2 1.7 fusion.85
  233.9 1.5 convolution_bitcast_fusion.3
  236.0 0.6 fusion.28
  236.6 7.4 %all-gather.1 = f32[128,2,8]{2,1,0:T(2,128)S(1)} all-gather(f32[32,2,8]{2,1,0:T(2,128)S(1)} %fusion.28), channel_id=3, replica_groups=mesh['tensor'=4,'prompt'=16,'cand'=4] {'cand'}, dimensions={0}, use_global_device_ids=true | all-gather | bytes 10240 | tf_op jit(solution)/shard_map/all_gather | solution.py:16
  244.2 6.9 %all-gather = f32[128,2,8]{2,1,0:T(2,128)S(1)} all-gather(f32[32,2,8]{2,1,0:T(2,128)S(1)} %get-tuple-element.422), channel_id=2, replica_groups=mesh['tensor'=4,'prompt'=16,'cand'=4] {'cand'}, dimensions={0}, use_global_device_ids=true | all-gather | bytes 10240 | tf_op jit(solution)/shard_map/all_gather | solution.py:16
  251.3 1.0 slice_bitcast_fusion
  252.3 0.2 copy.44
  252.5 6.4 %while.37 = (s32[]{:T(128)}, f32[32,2,8]{0,2,1:T(8,128)S(1)}, f32[32,2,8]{0,2,1:T(8,128)S(1)}, f32[32,2,1024]{2,1,0:T(2,128)S(1)}, f32[4,32,2,8]{1,3,2,0:T(8,128...) while((s32[]{:T(128)}, f32[32,2,8]{0,2,1:T(8,128)S(1)}, ...), condition=%wide.region_3.0_spmd, body=%wide.region_2.0_spmd.sunk | while | flops 199685 | bytes 3436695 | solution.py:22
  253.3 1.0 constant_dynamic-slice_fusion.2
  254.2 0.4 fusion.82
  255.4 1.0 constant_dynamic-slice_fusion.2
  256.4 0.4 fusion.82
  257.5 1.0 constant_dynamic-slice_fusion.2
  258.5 0.4 fusion.82
  258.9 0.2 fusion.45
  259.2 0.2 fusion.47
  259.6 0.3 fusion.39
  260.1 0.4 copy.56
  260.5 0.5 reshape.190
  261.0 8.6 %all_to_all.18 = bf16[4,2,2048]{2,1,0:T(2,128)(2,1)S(1)} all-to-all(bf16[4,2,2048]{2,1,0:T(2,128)(2,1)S(1)} %reshape.190), channel_id=1, replica_groups=mesh['tensor'=4,'prompt'=16,'cand'=4] {'cand'}, dimensions={0} | all-to-all | bytes 65536 | tf_op jit(solution)/shard_map/all_to_all | solution.py:166
  269.6 0.6 reshape.191
  270.2 0.3 copy.57
  270.6 4.0 %convolution_convert_fusion = bf16[32,2,8192]{2,0,1:T(8,128)(2,1)} fusion(bf16[256,8192]{1,0:T(8,128)(2,1)} %param.23, bf16[8,2,4,256]{3,0,2,1:T(8,128)(2,1)S(1)} %copy.57), kind=kOutput, calls=%fused_computation.34 | convolution fusion | flops 268959744 | bytes 5275648 | tf_op jit(solution)/shard_map/stx,xd->std/dot_general | solution.py:164
  274.6 68.6 %reduce-scatter.2.cloned.1.call-done = bf16[32,2,512]{2,0,1:T(8,128)(2,1)} async-done(((bf16[32,2,8192]{2,0,1:T(8,128)(2,1)}), bf16[32,2,512]{2,0,1:T(8,128)(2,1)}) %reduce-scatter.2.cloned.1.call-update) | async-done | bytes 65552 | tf_op jit(solution)/shard_map/reduce_scatter | solution.py:170
  343.2 1.5 copy.58
  (88 shorter events, 5.1 us)
Async XLA Ops:
  6.5 15.3 %copy-start = (bf16[8,2,128]{2,1,0:T(2,128)(2,1)S(1)}, bf16[8,2,128]{2,1,0:T(2,128)(2,1)}, u32[]{:S(2)}) copy-start(bf16[8,2,128]{2,1,0:T(2,128)(2,1)} %param.16) | copy-start | bytes 12292
  6.5 107.4 %all-gather.6.cloned.1.call-start = ((), (), s32[]{:S(2)}) async-start(), calls=%async_computation.2 | async-start | bytes 8912896 | tf_op jit(solution)/shard_map/all_gather | solution.py:122
  7.3 207.2 %all-gather.8.cloned.1.call-start = ((), (), s32[]{:S(2)}) async-start(), calls=%async_computation.3 | async-start | bytes 8912896 | tf_op jit(solution)/shard_map/all_gather | solution.py:123
  8.0 243.3 %all-gather.10.cloned.1.call-start = ((), (), s32[]{:S(2)}) async-start(), calls=%async_computation.4 | async-start | bytes 1310720 | tf_op jit(solution)/shard_map/all_gather | solution.py:16
  214.5 5.8 %copy-start.1 = (s32[8]{0:T(128)S(1)}, s32[8]{0:T(128)}, u32[]{:S(2)}) copy-start(s32[8]{0:T(128)} %param.21) | copy-start | bytes 100
  220.3 122.9 %reduce-scatter.2.cloned.1.call-start = ((), (), s32[]{:S(2)}) async-start(), calls=%async_computation.5 | async-start | bytes 1114112 | tf_op jit(solution)/shard_map/reduce_scatter | solution.py:170
  252.5 6.5 %copy-start.2 = (s32[1,32]{1,0:T(1,128)S(1)}, s32[1,32]{1,0:T(1,128)}, u32[]{:S(2)}) copy-start(s32[1,32]{1,0:T(1,128)} %param.22) | copy-start | bytes 388
Sparse Core Ops, SparseCore 0:
  9.1 104.7 all-gather.5
  115.8 98.6 all-gather.7
  220.4 21.4 all-gather.9
  274.7 68.3 reduce-scatter.1
where the time goes:
time: 353 us; the launch traced here: 351 us
  waiting for transfers between devices  257 us (73%)
  blocking collectives  33.2 us (9%)
  matrix products  30.5 us (9%)
  local copies, waits for them, and re-layouts  13.8 us (4%)
  between operations  13.3 us (4%)
    all_gather x1, waiting for transfers between devices, body(): value_piece = lax.all_gather(prefix_v, 'prompt', axis=0, tiled=True)  94.7 us
    all_gather x1, waiting for transfers between devices, body(): key_piece = lax.all_gather(prefix_k, 'prompt', axis=0, tiled=True)  91.8 us
    reduce_scatter x1, waiting for transfers between devices, body(): lax.psum_scatter(projected.astype(jnp.bfloat16), ('tensor', 'cand'), scat...  68.6 us
    all_gather x2, blocking collectives, joined(): everything = jax.tree.map(lambda part: lax.all_gather(part, axis), array)  14.4 us
    all_gather x1, blocking collectives, body(): gathered = lax.all_gather(q_step, 'cand', axis=0, tiled=True)  10.2 us
    all_to_all x1, blocking collectives, body(): lax.all_to_all(attention_output, 'cand', split_axis=2, concat_axis=0, til...  8.59 us
    dot_general x5, matrix products, slot_partial(): jnp.einsum('stkgd,slkd->stkgl', shaped, key_view, preferred_element_type=...  7.74 us
  transfers between devices with their start and end apart: 4, of which 3 were waited for; matrix products, arithmetic and copies ran while one was open for 7% of the time, Pallas kernels for 0%

commit v1 on v0

v1 whole, which is shorter than its diff:
```python
import math

import jax
import jax.numpy as jnp
from jax import lax
from jax.experimental import pallas as pl
from jax.experimental.pallas import tpu as pltpu
from jax.sharding import PartitionSpec as P

D = 128
LOG2E = 1.4426950408889634
SCALE2 = LOG2E / math.sqrt(D)
HIDDEN = -1e30
F32 = jnp.float32
BF16 = jnp.bfloat16
VMEM_LIMIT = 48 * 1024 * 1024


def split_stat(level, rows):
    high = level.astype(BF16).astype(F32)
    rest = level - high
    middle = rest.astype(BF16).astype(F32)
    low = rest - middle
    lane = lax.broadcasted_iota(jnp.int32, (rows, D), 1)
    return jnp.where(lane == 0, high, jnp.where(lane == 1, middle, jnp.where(lane == 2, low, 0.0)))


def join_stat(block):
    return block[..., 0:1] + block[..., 1:2] + block[..., 2:3]


def dot_t(a, b):
    return lax.dot_general(a, b, (((1,), (1,)), ((), ())), preferred_element_type=F32)


def dot(a, b):
    return lax.dot_general(a, b, (((1,), (0,)), ((), ())), preferred_element_type=F32)


def suffix_kernel(slots, tokens, heads, len_ref, q_ref, sk_ref, sv_ref, k_ref, v_ref, out_ref, q_rows):
    step = pl.program_id(0)
    rows = tokens * heads
    span = k_ref.shape[1]
    row_token = lax.broadcasted_iota(jnp.int32, (rows, tokens), 0) % tokens
    key_token = lax.broadcasted_iota(jnp.int32, (rows, tokens), 1)
    causal = key_token <= row_token
    position = lax.broadcasted_iota(jnp.int32, (rows, span), 1)
    for i in range(slots):
        length = len_ref[step * slots + i]
        wide = q_ref[i].astype(F32)
        for h in range(heads):
            q_rows[i, h * tokens : (h + 1) * tokens, :] = wide[:, h * D : (h + 1) * D]
        q = q_rows[i].astype(BF16)
        scores = dot_t(q, k_ref[i]) * SCALE2
        scores = jnp.where(position < length, scores, HIDDEN)
        step_scores = dot_t(q, sk_ref[i]) * SCALE2
        step_scores = jnp.where(causal, step_scores, HIDDEN)
        top = jnp.maximum(
            jnp.max(scores, axis=1, keepdims=True), jnp.max(step_scores, axis=1, keepdims=True)
        )
        weights = jnp.exp2(scores - top)
        step_weights = jnp.exp2(step_scores - top)
        total = jnp.sum(weights, axis=1, keepdims=True) + jnp.sum(
            step_weights, axis=1, keepdims=True
        )
        numer = dot(weights.astype(BF16), v_ref[i]) + dot(step_weights.astype(BF16), sv_ref[i])
        out_ref[i, 0:rows, :] = q
        out_ref[i, rows : 2 * rows, :] = (numer / total).astype(BF16)
        out_ref[i, 2 * rows : 3 * rows, :] = split_stat(top + jnp.log2(total), rows).astype(BF16)


def suffix_attention(q_step, step_k, step_values, suffix_k, suffix_values, lengths):
    count, tokens, width = q_step.shape
    heads = width // D
    span = suffix_k.shape[1]
    rows = tokens * heads
    per = 2
    return pl.pallas_call(
        lambda *refs: suffix_kernel(per, tokens, heads, *refs),
        grid_spec=pltpu.PrefetchScalarGridSpec(
            num_scalar_prefetch=1,
            grid=(count // per,),
            in_specs=[
                pl.BlockSpec((per, tokens, width), lambda i, n: (i, 0, 0)),
                pl.BlockSpec((per, tokens, D), lambda i, n: (i, 0, 0)),
                pl.BlockSpec((per, tokens, D), lambda i, n: (i, 0, 0)),
                pl.BlockSpec((per, span, D), lambda i, n: (i, 0, 0)),
                pl.BlockSpec((per, span, D), lambda i, n: (i, 0, 0)),
            ],
            out_specs=pl.BlockSpec((per, 3 * rows, D), lambda i, n: (i, 0, 0)),
            scratch_shapes=[pltpu.VMEM((per, rows, D), F32)],
        ),
        out_shape=jax.ShapeDtypeStruct((count, 3 * rows, D), BF16),
        compiler_params=pltpu.CompilerParams(vmem_limit_bytes=VMEM_LIMIT),
        name="suffix_attention",
    )(lengths, q_step, step_k, step_values, suffix_k, suffix_values)


def reorder_kernel(rows, place_ref, in_ref, out_ref):
    for s in range(in_ref.shape[0]):
        out_ref[place_ref[s]] = in_ref[s, 0:rows, :]


def reorder(placement, gathered, rows):
    slots = gathered.shape[0]
    return pl.pallas_call(
        lambda *refs: reorder_kernel(rows, *refs),
        in_specs=[
            pl.BlockSpec(memory_space=pltpu.SMEM),
            pl.BlockSpec(memory_space=pltpu.VMEM),
        ],
        out_specs=pl.BlockSpec(memory_space=pltpu.VMEM),
        out_shape=jax.ShapeDtypeStruct((slots, rows, D), BF16),
        compiler_params=pltpu.CompilerParams(vmem_limit_bytes=VMEM_LIMIT),
        name="reorder_queries",
    )(placement, gathered)


def prefix_kernel(indices, rows, q_ref, k_ref, v_ref, out_ref):
    total_rows = indices * rows
    chunk = 128
    lower = lax.broadcasted_iota(jnp.int32, (chunk // 8, 8, D), 1) < 4
    per_index = chunk // rows
    for start in range(0, total_rows, chunk):
        first = start // rows
        pair = []
        for u in range(2):
            q = q_ref[first : first + per_index, u].reshape(chunk, D)
            scores = dot_t(q, k_ref[u]) * SCALE2
            top = jnp.max(scores, axis=1, keepdims=True)
            weights = jnp.exp2(scores - top)
            total = jnp.sum(weights, axis=1, keepdims=True)
            numer = dot(weights.astype(BF16), v_ref[u]) / total
            stat = split_stat(top + jnp.log2(total), chunk)
            pair.append((numer.reshape(chunk // 8, 8, D), stat.reshape(chunk // 8, 8, D)))
        for part in range(2):
            one, two = pair[0][part], pair[1][part]
            even = jnp.where(lower, one, pltpu.roll(two, 4, 1))
            odd = jnp.where(lower, pltpu.roll(one, 4, 1), two)
            groups = rows // 8
            for parity, value in ((0, even), (1, odd)):
                value = value.reshape(per_index, groups, 8, D).astype(BF16)
                for g in range(groups):
                    out_ref[
                        first : first + per_index, 2 * g + parity, part * 8 : part * 8 + 8, :
                    ] = value[:, g]


def prefix_attention(q_rows, prefix_k, prefix_v, cand):
    indices, _, rows, _ = q_rows.shape
    return pl.pallas_call(
        lambda *refs: prefix_kernel(indices, rows, *refs),
        in_specs=[pl.BlockSpec(memory_space=pltpu.VMEM)] * 3,
        out_specs=pl.BlockSpec(memory_space=pltpu.VMEM),
        out_shape=jax.ShapeDtypeStruct((indices, cand, 16, D), BF16),
        compiler_params=pltpu.CompilerParams(vmem_limit_bytes=VMEM_LIMIT),
        name="prefix_attention",
    )(q_rows, prefix_k, prefix_v)


def project_kernel(
    rows, tokens, place_ref, cand_ref, col_ref, parts_ref, gathered_ref, w_ref, out_ref, attention, own, own_stat
):
    step = pl.program_id(0)
    owners, cand = parts_ref.shape[0], parts_ref.shape[1]
    slots = gathered_ref.shape[0]

    @pl.when(step == 0)
    def _():
        share = rows // cand
        shift = rows - share * cand_ref[0]
        for s in range(slots):
            u = place_ref[s]
            value = gathered_ref[s, rows : 2 * rows, :].astype(F32)
            stat = gathered_ref[s, 2 * rows : 3 * rows, :].astype(F32)
            own[u] = pltpu.roll(value, shift, 0)[0:8]
            own_stat[u] = pltpu.roll(stat, shift, 0)[0:8]
        lower = lax.broadcasted_iota(jnp.int32, (owners, 8, D), 1) < 4

        def paired(ref):
            both = ref[...].reshape(owners, 2, 8, D)
            return jnp.where(lower, both[:, 0], pltpu.roll(both[:, 1], 4, 1))

        values = [paired(own)]
        levels = [join_stat(paired(own_stat))]
        for c in range(cand):
            block = parts_ref[:, c].astype(F32)
            values.append(block[:, 0:8])
            levels.append(join_stat(block[:, 8:16]))
        top = levels[0]
        for level in levels[1:]:
            top = jnp.maximum(top, level)
        total = jnp.zeros_like(top)
        numer = jnp.zeros_like(values[0])
        for value, level in zip(values, levels):
            weight = jnp.exp2(level - top)
            total = total + weight
            numer = numer + value * weight
        merged = (numer / total).astype(BF16).reshape(owners * 8, D)
        lane = lax.broadcasted_iota(jnp.int32, (slots * tokens, owners * 8), 1)
        for h in range(2):
            pick = jnp.where(lane == col_ref[...] + h * tokens, 1.0, 0.0).astype(BF16)
            attention[:, h * D : (h + 1) * D] = dot(pick, merged).astype(BF16)

    blocks = out_ref.shape[0]
    width = out_ref.shape[2]
    for j in range(blocks):
        out_ref[j] = dot(attention[...], w_ref[:, j * width : (j + 1) * width]).astype(BF16)


def merge_project(placement, cand_index, columns, parts, gathered, weight, rows, tokens, shares):
    owners, cand, _, _ = parts.shape
    slots = gathered.shape[0]
    depth, width = weight.shape
    out_rows = slots * tokens
    steps = 4
    return pl.pallas_call(
        lambda *refs: project_kernel(rows, tokens, *refs),
        grid=(steps,),
        in_specs=[
            pl.BlockSpec(memory_space=pltpu.SMEM),
            pl.BlockSpec(memory_space=pltpu.SMEM),
            pl.BlockSpec((out_rows, 1), lambda i: (0, 0)),
            pl.BlockSpec(parts.shape, lambda i: (0, 0, 0, 0)),
            pl.BlockSpec(gathered.shape, lambda i: (0, 0, 0)),
            pl.BlockSpec((depth, width // steps), lambda i: (0, i)),
        ],
        out_specs=pl.BlockSpec((shares // steps, out_rows, width // shares), lambda i: (i, 0, 0)),
        scratch_shapes=[
            pltpu.VMEM((out_rows, depth), BF16),
            pltpu.VMEM((slots, 8, D), F32),
            pltpu.VMEM((slots, 8, D), F32),
        ],
        out_shape=jax.ShapeDtypeStruct((shares, out_rows, width // shares), BF16),
        compiler_params=pltpu.CompilerParams(vmem_limit_bytes=VMEM_LIMIT),
        name="merge_project",
    )(placement, cand_index, columns, parts, gathered, weight)


def sum_kernel(in_ref, out_ref):
    total = in_ref[0].astype(F32)
    for j in range(1, in_ref.shape[0]):
        total = total + in_ref[j].astype(F32)
    out_ref[...] = total.astype(BF16)


def sum_shares(shares):
    return pl.pallas_call(
        sum_kernel,
        in_specs=[pl.BlockSpec(memory_space=pltpu.VMEM)],
        out_specs=pl.BlockSpec(memory_space=pltpu.VMEM),
        out_shape=jax.ShapeDtypeStruct(shares.shape[1:], BF16),
        compiler_params=pltpu.CompilerParams(vmem_limit_bytes=VMEM_LIMIT),
        name="sum_shares",
    )(shares)


def body(
    q_step,
    step_k,
    step_values,
    prefix_k,
    prefix_v,
    suffix_k,
    suffix_values,
    lengths,
    placement,
    output_weight,
):
    slot_count, tokens, width = q_step.shape
    rows = tokens * width // D
    indices = lax.axis_size("prompt")
    cand = lax.axis_size("cand")
    shares = lax.axis_size("tensor") * cand
    slots = placement.shape[1]
    place = placement[0]
    local = suffix_attention(q_step, step_k, step_values, suffix_k, suffix_values, lengths)
    gathered = lax.all_gather(local, "cand", axis=0, tiled=True)
    ordered = reorder(place, gathered, rows)
    arrived = lax.all_to_all(
        ordered.reshape(slots * rows, D), "prompt", split_axis=0, concat_axis=0, tiled=True
    )
    parts = prefix_attention(
        arrived.reshape(indices, slots // indices, rows, D), prefix_k, prefix_v, cand
    )
    returned = lax.all_to_all(
        parts.reshape(indices * cand * 16, D), ("prompt", "cand"), split_axis=0, concat_axis=0, tiled=True
    )
    columns = (place[:, None] * (rows // cand) + jnp.arange(tokens, dtype=jnp.int32)[None, :]).reshape(
        slots * tokens, 1
    )
    cand_index = lax.axis_index("cand").astype(jnp.int32).reshape(1)
    projected = merge_project(
        place,
        cand_index,
        columns,
        returned.reshape(indices, cand, 16, D),
        gathered,
        output_weight,
        rows,
        tokens,
        shares,
    )
    spread = lax.all_to_all(
        projected, ("tensor", "cand"), split_axis=0, concat_axis=0, tiled=True
    )
    return sum_shares(spread).reshape(slots, tokens, -1)


def solution(mesh):
    return jax.shard_map(
        body,
        mesh=mesh,
        in_specs=(
            P(("prompt", "cand"), None, "tensor"),
            P(("prompt", "cand"), None, "tensor"),
            P(("prompt", "cand"), None, "tensor"),
            P("prompt", "cand", "tensor"),
            P("prompt", "cand", "tensor"),
            P(("prompt", "cand"), None, "tensor"),
            P(("prompt", "cand"), None, "tensor"),
            P(("prompt", "cand")),
            P("prompt", None),
            P(("tensor", "cand"), None),
        ),
        out_specs=P("prompt", None, ("tensor", "cand")),
        check_vma=False,
    )
```

time: 353 us -> 89.2 us (0.25)
  waiting for transfers between devices: 257 us -> 12.5 us
  matrix products: 30.5 us -> 0 us
  blocking collectives: 33.2 us -> 48.8 us
  between operations: 13.3 us -> 0.06 us
  Pallas kernels: 0 us -> 11.5 us
  starting transfers between devices: 0.12 us -> 7.88 us
  local copies, waits for them, and re-layouts: 13.8 us -> 7.91 us
    all_gather x3 -> x0, waiting for transfers between devices: 187 us -> none  [the longest x1 94.7 us: body(): value_piece = lax.all_gather(prefix_v, 'prompt', axis=0, tiled=True)]
    reduce_scatter x1 -> x0, waiting for transfers between devices: 68.6 us -> none  [body(): lax.psum_scatter(projected.astype(jnp.bfloat16), ('tensor', 'cand'), scat...]
    dot_general x17 -> x0, matrix products: 30.5 us -> none  [the longest x5 7.74 us: slot_partial(): jnp.einsum('stkgd,slkd->stkgl', shaped, key_view, preferred_element_type=...]
    all_to_all x1 -> x2, blocking collectives: 8.59 us -> 38.1 us  [the longest x1 23.3 us: body(): lax.all_to_all(projected, ('tensor', 'cand'), split_axis=0, concat_axis=0...]
    all_gather x3 -> x1, blocking collectives: 24.6 us -> 10.7 us  [body(): gathered = lax.all_gather(local, 'cand', axis=0, tiled=True)]
    all_to_all x0 -> x1, waiting for transfers between devices: none -> 12.5 us  [body(): lax.all_to_all(parts.reshape(indices * cand * 16, D), ('prompt', 'cand'),...]
    pallas_call x0 -> x5, Pallas kernels: none -> 11.5 us  [the longest x1 5.9 us: suffix_attention(): pl.pallas_call(lambda *refs: suffix_kernel(per, tokens, heads, *refs), gr...]
    all_to_all x0 -> x1, starting transfers between devices: none -> 7.88 us  [body(): lax.all_to_all(parts.reshape(indices * cand * 16, D), ('prompt', 'cand'),...]
  transfers between devices with their start and end apart: 4 -> 1, of which waited for: 3 -> 1; matrix products, arithmetic and copies ran while one was open for 7% -> 0% of each run, Pallas kernels for 0% -> 0%
where the time goes in v1:
time: 89.2 us; the launch traced here: 88.7 us
  blocking collectives  48.8 us (55%)
  waiting for transfers between devices  12.5 us (14%)
  Pallas kernels  11.5 us (13%)
  local copies, waits for them, and re-layouts  7.91 us (9%)
  starting transfers between devices  7.88 us (9%)
    all_to_all x1, blocking collectives, body(): lax.all_to_all(projected, ('tensor', 'cand'), split_axis=0, concat_axis=0...  23.3 us
    all_to_all x1, blocking collectives, body(): lax.all_to_all(ordered.reshape(slots * rows, D), 'prompt', split_axis=0,...  14.7 us
    all_to_all x1, waiting for transfers between devices, body(): lax.all_to_all(parts.reshape(indices * cand * 16, D), ('prompt', 'cand'),...  12.5 us
    all_gather x1, blocking collectives, body(): gathered = lax.all_gather(local, 'cand', axis=0, tiled=True)  10.7 us
    all_to_all x1, starting transfers between devices, body(): lax.all_to_all(parts.reshape(indices * cand * 16, D), ('prompt', 'cand'),...  7.88 us
    unnamed x18, local copies, waits for them, and re-layouts  7.17 us
    pallas_call x1, Pallas kernels, suffix_attention(): pl.pallas_call(lambda *refs: suffix_kernel(per, tokens, heads, *refs), gr...  5.9 us
    pallas_call x1, Pallas kernels, merge_project(): pl.pallas_call(lambda *refs: project_kernel(rows, tokens, *refs), grid=(s...  2.6 us
  transfers between devices with their start and end apart: 1, of which 1 were waited for; matrix products, arithmetic and copies ran while one was open for 0% of the time, Pallas kernels for 0%

profile of v1, /device:TPU:1, one launch (start us, length us, event | category | flops | bytes accessed | tf_op | source)
XLA Modules:
  0.0 88.7 jit_solution(9070244021572655085)
XLA Ops:
  0.0 0.0 copy-start
  0.0 2.2 %copy-done = bf16[8,2048,128]{2,1,0:T(8,128)(2,1)S(1)} copy-done((bf16[8,2048,128]{2,1,0:T(8,128)(2,1)S(1)}, bf16[8,2048,128]{2,1,0:T(8,128)(2,1)}, u32[]{:S(2)}) %copy-start) | copy-done | bytes 4194328
  2.2 0.0 copy-start.4
  2.2 0.8 copy-done.4
  2.9 0.0 copy-start.5
  2.9 0.7 copy-done.5
  3.6 0.0 copy-start.6
  3.6 0.7 copy-done.6
  4.3 0.0 copy-start.8
  4.3 0.7 copy-done.8
  5.0 0.0 copy-start.7
  5.0 0.0 copy-start.2
  5.0 0.0 copy-start.3
  5.0 5.9 %suffix_attention.1 = bf16[8,48,128]{2,1,0:T(8,128)(2,1)S(1)} custom-call(s32[8]{0:T(128)S(1)} %copy-done.8, bf16[8,2,1024]{2,1,0:T(2,128)(2,1)S(1)} %copy-done.4, bf16[8,2,128]{2,1,0:T(2,128)(2,1)S(1)} %copy-done.5, bf16[8,2,128]{2,1,0:T(2,128)(2,1)S(1)} %copy-done.6, bf16[8,2048,128]{2,1,0:T(8,128)(2,1)S(1)} %copy-done, bf16[8,2048,128]{2,1,0:T(8,128)(2,1)} %refs_5_.2), custom_call_target="tpu_custom_call" | custom-call | tf_op jit(solution)/shard_map/suffix_attention/pallas_call | solution.py:78
  10.9 10.7 %all_gather.3.refs_1_.refs_4_ = bf16[32,48,128]{2,1,0:T(8,128)(2,1)S(1)} all-gather(bf16[8,48,128]{2,1,0:T(8,128)(2,1)S(1)} %suffix_attention.1), channel_id=1, replica_groups=mesh['tensor'=4,'prompt'=16,'cand'=4] {'cand'}, dimensions={0}, use_global_device_ids=true | all-gather | bytes 491520 | tf_op jit(solution)/shard_map/all_gather | solution.py:278
  21.6 0.0 copy-done.7
  21.6 0.6 reorder_queries.1
  22.2 14.7 %all_to_all.23 = bf16[16,32,128]{2,1,0:T(8,128)(2,1)S(1)} all-to-all(bf16[16,32,128]{2,1,0:T(8,128)(2,1)S(1)} %bitcast.8), channel_id=1, replica_groups=mesh['tensor'=4,'prompt'=16,'cand'=4] {'prompt'}, dimensions={0} | all-to-all | bytes 262144 | tf_op jit(solution)/shard_map/all_to_all | solution.py:280
  36.9 0.0 copy-done.2
  36.9 0.0 copy-done.3
  36.9 2.3 %prefix_attention.1 = bf16[16,4,16,128]{3,2,1,0:T(8,128)(2,1)} custom-call(bf16[16,2,16,128]{3,2,1,0:T(8,128)(2,1)S(1)} %bitcast.9, bf16[2,1024,128]{2,1,0:T(8,128)(2,1)S(1)} %copy-done.2, bf16[2,1024,128]{2,1,0:T(8,128)(2,1)S(1)} %copy-done.3), custom_call_target="tpu_custom_call" | custom-call | tf_op jit(solution)/shard_map/prefix_attention/pallas_call | solution.py:151
  39.2 7.9 %all-to-all-start.1 = ((bf16[64,16,128]{2,1,0:T(8,128)(2,1)}), bf16[64,16,128]{2,1,0:T(8,128)(2,1)S(1)}, u32[]{:S(2)}, u32[]{:S(2)}) async-start(bf16[64,16,128]{2,1,0:T(8,128)(2,1)} %bitcast.4), calls=%async_computation.1 | async-start | bytes 524288 | tf_op jit(solution)/shard_map/all_to_all | solution.py:286
  47.1 0.1 iota_add_fusion
  47.2 0.1 add.27.refs_2_
  47.3 12.5 %all-to-all-done.1 = bf16[64,16,128]{2,1,0:T(8,128)(2,1)S(1)} async-done(((bf16[64,16,128]{2,1,0:T(8,128)(2,1)}), bf16[64,16,128]{2,1,0:T(8,128)(2,1)S(1)}, u32[]{:S(2)}, u32[]{:S(2)}) %all-to-all-start.1) | async-done | bytes 262176 | tf_op jit(solution)/shard_map/all_to_all | solution.py:286
  59.7 0.0 copy-start.1
  59.7 2.2 %copy-done.1 = bf16[256,8192]{1,0:T(8,128)(2,1)S(1)} copy-done((bf16[256,8192]{1,0:T(8,128)(2,1)S(1)}, bf16[256,8192]{1,0:T(8,128)(2,1)}, u32[]{:S(2)}) %copy-start.1) | copy-done | bytes 4194328
  61.9 2.6 %merge_project.1 = bf16[16,64,512]{2,1,0:T(8,128)(2,1)S(1)} custom-call(s32[32]{0:T(128)S(1)} %bitcast.11, s32[1]{0:T(128)} %bitcast.1.refs_1_, s32[64,1]{1,0:T(8,128)S(1)} %add.27.refs_2_, bf16[16,4,16,128]{3,2,1,0:T(8,128)(2,1)S(1)} %bitcast.7, bf16[32,48,128]{2,1,0:T(8,128)(2,1)S(1)} %all_gather.3.refs_1_.refs_4_, bf16[256,8192]{1,0:T(8,128)(2,1)S(1)} %copy-done.1), custom_call_target="tpu_custom_call" | custom-call | tf_op jit(solution)/shard_map/merge_project/pallas_call | solution.py:217
  64.5 23.3 %all_to_all.24.in_ref = bf16[16,64,512]{2,1,0:T(8,128)(2,1)S(1)} all-to-all(bf16[16,64,512]{2,1,0:T(8,128)(2,1)S(1)} %merge_project.1), channel_id=1, replica_groups=mesh['tensor'=4,'prompt'=16,'cand'=4] {'tensor','cand'}, dimensions={0} | all-to-all | bytes 2097152 | tf_op jit(solution)/shard_map/all_to_all | solution.py:304
  87.9 0.1 sum_shares.1
  88.0 0.7 reshape.55
  (1 shorter events, 0.0 us)
Async XLA Ops:
  0.0 2.2 %copy-start = (bf16[8,2048,128]{2,1,0:T(8,128)(2,1)S(1)}, bf16[8,2048,128]{2,1,0:T(8,128)(2,1)}, u32[]{:S(2)}) copy-start(bf16[8,2048,128]{2,1,0:T(8,128)(2,1)} %refs_4_.1) | copy-start | bytes 12582916
  2.2 0.8 copy-start.4
  2.9 0.7 copy-start.5
  3.6 0.7 copy-start.6
  4.3 0.7 copy-start.8
  5.0 16.6 %copy-start.7 = (s32[1,32]{1,0:T(1,128)S(1)}, s32[1,32]{1,0:T(1,128)}, u32[]{:S(2)}) copy-start(s32[1,32]{1,0:T(1,128)} %param.18) | copy-start | bytes 388
  5.0 31.9 %copy-start.2 = (bf16[2,1024,128]{2,1,0:T(8,128)(2,1)S(1)}, bf16[2,1024,128]{2,1,0:T(8,128)(2,1)}, u32[]{:S(2)}) copy-start(bf16[2,1024,128]{2,1,0:T(8,128)(2,1)} %refs_1_.3) | copy-start | bytes 1572868
  5.0 31.9 %copy-start.3 = (bf16[2,1024,128]{2,1,0:T(8,128)(2,1)S(1)}, bf16[2,1024,128]{2,1,0:T(8,128)(2,1)}, u32[]{:S(2)}) copy-start(bf16[2,1024,128]{2,1,0:T(8,128)(2,1)} %refs_2_.3) | copy-start | bytes 1572868
  39.2 20.5 %all-to-all-start.1 = ((bf16[64,16,128]{2,1,0:T(8,128)(2,1)}), bf16[64,16,128]{2,1,0:T(8,128)(2,1)S(1)}, u32[]{:S(2)}, u32[]{:S(2)}) async-start(bf16[64,16,128]{2,1,0:T(8,128)(2,1)} %bitcast.4), calls=%async_computation.1 | async-start | bytes 524288 | tf_op jit(solution)/shard_map/all_to_all | solution.py:286
  59.7 2.2 %copy-start.1 = (bf16[256,8192]{1,0:T(8,128)(2,1)S(1)}, bf16[256,8192]{1,0:T(8,128)(2,1)}, u32[]{:S(2)}) copy-start(bf16[256,8192]{1,0:T(8,128)(2,1)} %refs_5_.3) | copy-start | bytes 12582916

commit v2 on v0

v2 whole, which is shorter than its diff:
```python
import math

import jax
import jax.numpy as jnp
from jax import lax
from jax.experimental import pallas as pl
from jax.experimental.pallas import tpu as pltpu
from jax.sharding import Mesh, PartitionSpec as P

D = 128
SCALE2 = 1.4426950408889634 / math.sqrt(D)
HIDDEN = -1e30
GROUP = 2
F32 = jnp.float32
BF16 = jnp.bfloat16
VMEM_LIMIT = 32 * 1024 * 1024
VMEM_MOST = 57 * 1024 * 1024
VMEM_SPEC = pl.BlockSpec(memory_space=pltpu.VMEM)
SMEM_SPEC = pl.BlockSpec(memory_space=pltpu.SMEM)
HBM_SPEC = pl.BlockSpec(memory_space=pltpu.HBM)
PARAMS = pltpu.CompilerParams(vmem_limit_bytes=VMEM_LIMIT)


def split_stat(level):
    high = level.astype(BF16).astype(F32)
    rest = level - high
    middle = rest.astype(BF16).astype(F32)
    low = rest - middle
    lane = lax.broadcasted_iota(jnp.int32, (level.shape[0], D), 1)
    return jnp.where(lane == 0, high, jnp.where(lane == 1, middle, jnp.where(lane == 2, low, 0.0)))


def join_stat(block):
    return block[..., 0:1] + block[..., 1:2] + block[..., 2:3]


def dot_t(a, b):
    return lax.dot_general(a, b, (((1,), (1,)), ((), ())), preferred_element_type=F32)


def dot(a, b):
    return lax.dot_general(a, b, (((1,), (0,)), ((), ())), preferred_element_type=F32)


def lower_rows(shape):
    return lax.broadcasted_iota(jnp.int32, shape, len(shape) - 2) < 4


def queries_kernel(me_ref, q_ref, all_ref, mine_ref, other_ref, rows):
    slots, tokens, width = q_ref.shape
    core = me_ref[1]
    for i in range(slots):
        wide = q_ref[i].astype(F32)
        for h in range(width // D):
            place = (h // 4) * 4 + (h % 2) * tokens
            rows[(h // 2) % 2, i, place : place + tokens, :] = wide[:, h * D : (h + 1) * D]
    all_ref[...] = jnp.concatenate([rows[0], rows[1]], axis=1).astype(BF16)
    mine_ref[...] = rows[core].reshape(slots * 8, D).astype(BF16)
    other_ref[...] = rows[1 - core].reshape(slots * 8, D).astype(BF16)


def split_queries(me, q_step):
    slots = q_step.shape[0]
    half = jax.ShapeDtypeStruct((slots * 8, D), BF16)
    return pl.pallas_call(
        queries_kernel,
        in_specs=[SMEM_SPEC, VMEM_SPEC],
        out_specs=[VMEM_SPEC] * 3,
        out_shape=[jax.ShapeDtypeStruct((slots, 16, D), BF16), half, half],
        scratch_shapes=[pltpu.VMEM((2, slots, 8, D), F32)],
        compiler_params=PARAMS,
        name="split_queries",
    )(me, q_step)


def route_kernel(me_ref, place_ref, mine_ref, other_ref, out_ref, rows):
    xh, core = me_ref[0], me_ref[1]
    count = mine_ref.shape[0] // 8
    rows[...] = jnp.zeros_like(rows)
    for ref, column in ((mine_ref, core), (other_ref, 1 - core)):
        value = ref[...].astype(F32)
        for i in range(count):
            slot = (2 * xh + column) * count + i
            rows[place_ref[slot]] = value[i * 8 : (i + 1) * 8]
    packed = rows[...].reshape(out_ref.shape[0], 16, D).astype(BF16)
    for j in range(out_ref.shape[1]):
        out_ref[:, j] = packed


def route(me, placement, mine, other, indices):
    slots = placement.shape[0]
    return pl.pallas_call(
        route_kernel,
        in_specs=[SMEM_SPEC, SMEM_SPEC, VMEM_SPEC, VMEM_SPEC],
        out_specs=VMEM_SPEC,
        out_shape=jax.ShapeDtypeStruct((indices, 2, 16, D), BF16),
        scratch_shapes=[pltpu.VMEM((slots, 8, D), F32)],
        compiler_params=PARAMS,
        name="route_queries",
    )(me, placement, mine, other)


def suffix_kernel(me_ref, len_ref, q_ref, sk_ref, sv_ref, k_hbm, v_hbm, *rest):
    outs, (keys, values, tiles, key_sem, value_sem) = rest[:4], rest[4:]
    slots, span, _ = k_hbm.shape
    tokens = sk_ref.shape[1]
    xh, core = me_ref[0], me_ref[1]
    lower = lower_rows((8, D))

    def copies(i):
        return (
            pltpu.make_async_copy(k_hbm.at[i], keys.at[i], key_sem.at[i]),
            pltpu.make_async_copy(v_hbm.at[i], values.at[i], value_sem.at[i]),
        )

    for i in range(slots):
        for copy in copies(i):
            copy.start()
    rows = q_ref.shape[1]
    row_token = lax.broadcasted_iota(jnp.int32, (rows, tokens), 0) % tokens
    key_token = lax.broadcasted_iota(jnp.int32, (rows, tokens), 1)
    causal = key_token <= row_token
    position = lax.broadcasted_iota(jnp.int32, (rows, span), 1)
    for first in range(0, slots, GROUP):
        group = range(first, first + GROUP)
        for i in group:
            for copy in copies(i):
                copy.wait()
        q = [q_ref[i] for i in group]
        scores = [dot_t(q[n], keys[i]) for n, i in enumerate(group)]
        step_scores = [dot_t(q[n], sk_ref[i]) for n, i in enumerate(group)]
        scores = [
            jnp.where(position < len_ref[i], scores[n] * SCALE2, HIDDEN) for n, i in enumerate(group)
        ]
        step_scores = [jnp.where(causal, x * SCALE2, HIDDEN) for x in step_scores]
        top = [
            jnp.maximum(jnp.max(x, axis=1, keepdims=True), jnp.max(y, axis=1, keepdims=True))
            for x, y in zip(scores, step_scores)
        ]
        weights = [jnp.exp2(x - m) for x, m in zip(scores, top)]
        step_weights = [jnp.exp2(x - m) for x, m in zip(step_scores, top)]
        total = [
            jnp.sum(x, axis=1, keepdims=True) + jnp.sum(y, axis=1, keepdims=True)
            for x, y in zip(weights, step_weights)
        ]
        for n, i in enumerate(group):
            numer = dot(weights[n].astype(BF16), values[i])
            numer = numer + dot(step_weights[n].astype(BF16), sv_ref[i])
            value = numer / total[n]
            stat = split_stat(top[n] + jnp.log2(total[n]))
            for c in range(2):
                one, two = value[c * 8 : c * 8 + 8], stat[c * 8 : c * 8 + 8]
                tiles[c, i] = jnp.where(lower, one, pltpu.roll(two, 4, 0))
                tiles[2 + c, i] = jnp.where(lower, pltpu.roll(one, 4, 0), two)
    for j, out in enumerate(outs):
        to_xh = xh if j // 2 == 0 else 1 - xh
        to_core = core if j % 2 == 0 else 1 - core
        out[...] = tiles[2 * to_xh + to_core].reshape(slots * 8, D).astype(BF16)


def suffix_attention(me, lengths, q_rows, step_k, step_values, suffix_k, suffix_values):
    slots, span, _ = suffix_k.shape
    rows = q_rows.shape[1]
    piece = jax.ShapeDtypeStruct((slots * 8, D), BF16)
    return pl.pallas_call(
        suffix_kernel,
        in_specs=[SMEM_SPEC, SMEM_SPEC, VMEM_SPEC, VMEM_SPEC, VMEM_SPEC, HBM_SPEC, HBM_SPEC],
        out_specs=[VMEM_SPEC] * 4,
        out_shape=[piece] * 4,
        scratch_shapes=[
            pltpu.VMEM((slots, span, D), BF16),
            pltpu.VMEM((slots, span, D), BF16),
            pltpu.VMEM((4, slots, 8, D), F32),
            pltpu.SemaphoreType.DMA((slots,)),
            pltpu.SemaphoreType.DMA((slots,)),
        ],
        cost_estimate=pl.CostEstimate(
            flops=4 * slots * rows * span * D * 8,
            bytes_accessed=4 * slots * span * D,
            transcendentals=slots * rows * span,
        ),
        compiler_params=pltpu.CompilerParams(vmem_limit_bytes=VMEM_MOST),
        name="suffix_attention",
    )(me, lengths, q_rows, step_k, step_values, suffix_k, suffix_values)


def prefix_kernel(q_ref, k_own, k_other, v_own, v_other, out_ref):
    indices = q_ref.shape[0]
    q_both = q_ref[:, 0].astype(F32) + q_ref[:, 1].astype(F32)
    pair = []
    for u in range(2):
        q = q_both[:, u * 8 : u * 8 + 8].reshape(indices * 8, D).astype(BF16)
        scores = [dot_t(q, k[u]) * SCALE2 for k in (k_own, k_other)]
        top = jnp.maximum(
            jnp.max(scores[0], axis=1, keepdims=True), jnp.max(scores[1], axis=1, keepdims=True)
        )
        weights = [jnp.exp2(part - top) for part in scores]
        total = sum(jnp.sum(part, axis=1, keepdims=True) for part in weights)
        numer = sum(
            dot(part.astype(BF16), v[u]) for part, v in zip(weights, (v_own, v_other))
        )
        pair.append(
            (
                (numer / total).reshape(indices, 8, D),
                split_stat(top + jnp.log2(total)).reshape(indices, 8, D),
            )
        )
    lower = lower_rows((indices, 8, D))
    for j in range(2):
        halves = []
        for part in range(2):
            one, two = pair[0][part], pair[1][part]
            if j == 0:
                halves.append(jnp.where(lower, one, pltpu.roll(two, 4, 1)))
            else:
                halves.append(jnp.where(lower, pltpu.roll(one, 4, 1), two))
        out_ref[:, j] = jnp.concatenate(halves, axis=1).astype(BF16)


def prefix_attention(q_rows, k_own, k_other, v_own, v_other):
    return pl.pallas_call(
        prefix_kernel,
        in_specs=[VMEM_SPEC] * 5,
        out_specs=VMEM_SPEC,
        out_shape=jax.ShapeDtypeStruct(q_rows.shape, BF16),
        compiler_params=PARAMS,
        name="prefix_attention",
    )(q_rows, k_own, k_other, v_own, v_other)


def stage_kernel(me_ref, w_hbm, after_ref, away_ref, mine_ref, sem):
    core = me_ref[1]
    blocks, _, width = mine_ref.shape
    copies = []
    for half, (out_ref, which) in enumerate(((away_ref, 1 - core), (mine_ref, core))):
        for b in range(blocks):
            columns = pl.ds(pl.multiple_of((2 * b + which) * width, width), width)
            copies.append(
                pltpu.make_async_copy(w_hbm.at[:, columns], out_ref.at[b], sem.at[half, b])
            )
    for copy in copies:
        copy.start()
    for copy in copies:
        copy.wait()


def stage_weight(me, weight, after, blocks):
    depth, width = weight.shape
    half = jax.ShapeDtypeStruct((blocks, depth, width // (2 * blocks)), BF16)
    return pl.pallas_call(
        stage_kernel,
        in_specs=[SMEM_SPEC, HBM_SPEC, HBM_SPEC],
        out_specs=[VMEM_SPEC] * 2,
        out_shape=[half] * 2,
        scratch_shapes=[pltpu.SemaphoreType.DMA((2, blocks))],
        cost_estimate=pl.CostEstimate(
            flops=0, bytes_accessed=4 * depth * width, transcendentals=0
        ),
        compiler_params=pltpu.CompilerParams(vmem_limit_bytes=54 * 1024 * 1024),
        name="stage_weight",
    )(me, weight, after)


def merge_kernel(
    me_ref, place_ref, col_ref, parts_ref, suf0, suf1, suf2, suf3, w_ref, out_ref, att_ref, own
):
    xh, core = me_ref[0], me_ref[1]
    blocks, out_rows, _ = out_ref.shape
    owners = parts_ref.shape[0]
    count = suf0.shape[0] // 8
    for j, ref in enumerate((suf0, suf1, suf2, suf3)):
        from_xh = xh if j // 2 == 0 else 1 - xh
        from_core = core if j % 2 == 0 else 1 - core
        value = ref[...].astype(F32)
        for i in range(count):
            slot = (2 * from_xh + from_core) * count + i
            own[place_ref[slot]] = value[i * 8 : (i + 1) * 8]
    lower = lower_rows((owners, 8, D))
    both = own[...].reshape(owners, 2, 8, D)
    one, two = both[:, 0], both[:, 1]
    values = [jnp.where(lower, one, pltpu.roll(two, 4, 1))]
    levels = [join_stat(jnp.where(lower, pltpu.roll(one, 4, 1), two))]
    for c in range(parts_ref.shape[1]):
        block = parts_ref[:, c].astype(F32)
        values.append(block[:, 0:8])
        levels.append(join_stat(block[:, 8:16]))
    top = levels[0]
    for level in levels[1:]:
        top = jnp.maximum(top, level)
    total = jnp.zeros_like(top)
    numer = jnp.zeros_like(values[0])
    for value, level in zip(values, levels):
        weight = jnp.exp2(level - top)
        total = total + weight
        numer = numer + value * weight
    merged = (numer / total).astype(BF16).reshape(owners * 8, D)
    lane = lax.broadcasted_iota(jnp.int32, (out_rows, owners * 8), 1)
    for h in range(2):
        pick = jnp.where(lane == col_ref[...] + 2 * h, 1.0, 0.0).astype(BF16)
        att_ref[:, h * D : (h + 1) * D] = dot(pick, merged).astype(BF16)
    for b in range(blocks):
        out_ref[b] = dot(att_ref[...], w_ref[b]).astype(BF16)


def merge_and_project(me, placement, columns, parts, pieces, weight):
    slots = placement.shape[0]
    blocks, depth, width = weight.shape
    out_rows = columns.shape[0]
    return pl.pallas_call(
        merge_kernel,
        in_specs=[SMEM_SPEC, SMEM_SPEC] + [VMEM_SPEC] * 7,
        out_specs=[VMEM_SPEC, VMEM_SPEC],
        out_shape=[
            jax.ShapeDtypeStruct((blocks, out_rows, width), BF16),
            jax.ShapeDtypeStruct((out_rows, depth), BF16),
        ],
        scratch_shapes=[pltpu.VMEM((slots, 8, D), F32)],
        compiler_params=PARAMS,
        name="merge_and_project",
    )(me, placement, columns, parts, *pieces, weight)


def project_kernel(att_ref, w_ref, out_ref):
    for b in range(out_ref.shape[0]):
        out_ref[b] = dot(att_ref[...], w_ref[b])


def project(attention, weight):
    out_rows = attention.shape[0]
    blocks, depth, width = weight.shape
    return pl.pallas_call(
        project_kernel,
        in_specs=[VMEM_SPEC] * 2,
        out_specs=VMEM_SPEC,
        out_shape=jax.ShapeDtypeStruct((blocks, out_rows, width), F32),
        cost_estimate=pl.CostEstimate(
            flops=2 * out_rows * depth * width * blocks * 8,
            bytes_accessed=2 * depth * width * blocks,
            transcendentals=0,
        ),
        compiler_params=PARAMS,
        name="project",
    )(attention, weight)


def add_kernel(one_ref, two_ref, out_ref):
    out_ref[...] = (one_ref[...] + two_ref[...].astype(F32)).astype(BF16)


def add_halves(one, two):
    return pl.pallas_call(
        add_kernel,
        in_specs=[VMEM_SPEC] * 2,
        out_specs=VMEM_SPEC,
        out_shape=jax.ShapeDtypeStruct(two.shape, BF16),
        compiler_params=PARAMS,
        name="add_halves",
    )(one, two)


def sum_kernel(in_ref, out_ref):
    total = in_ref[0].astype(F32)
    for j in range(1, in_ref.shape[0]):
        total = total + in_ref[j].astype(F32)
    out_ref[...] = total.astype(BF16).reshape(out_ref.shape)


def sum_shares(shares, tokens):
    _, rows, width = shares.shape
    return pl.pallas_call(
        sum_kernel,
        in_specs=[VMEM_SPEC],
        out_specs=VMEM_SPEC,
        out_shape=jax.ShapeDtypeStruct((rows // tokens, tokens, width), BF16),
        compiler_params=PARAMS,
        name="sum_shares",
    )(shares)


def swap(value, axes):
    size = 2 ** len(axes)
    return lax.ppermute(value, axes, [(i, size - 1 - i) for i in range(size)])


def body(
    q_step,
    step_k,
    step_values,
    prefix_k,
    prefix_v,
    suffix_k,
    suffix_values,
    lengths,
    placement,
    output_weight,
):
    tokens = q_step.shape[1]
    indices = lax.axis_size("prompt")
    blocks = lax.axis_size("tensor") * 2
    place = placement[0]
    slots = place.shape[0]
    me = jnp.stack([lax.axis_index("xh"), lax.axis_index("core")]).astype(jnp.int32)

    all_rows, mine, other = split_queries(me, q_step)
    other = swap(other, ("core",))
    k_other = swap(prefix_k, ("core",))
    v_other = swap(prefix_v, ("core",))
    routed = route(me, place, mine, other, indices)
    arrived = lax.all_to_all(
        routed.reshape(indices * 2, 16, D), ("prompt", "xh"), split_axis=0, concat_axis=0, tiled=True
    )
    pieces = suffix_attention(
        me, lengths, all_rows, step_k, step_values, suffix_k, suffix_values
    )
    parts = prefix_attention(
        arrived.reshape(indices, 2, 16, D), prefix_k, k_other, prefix_v, v_other
    )
    pieces, parts = lax.optimization_barrier((pieces, parts))
    returned = lax.all_to_all(
        parts.reshape(indices * 2, 16, D), ("prompt", "xh"), split_axis=0, concat_axis=0, tiled=True
    )
    pieces = [
        pieces[0],
        swap(pieces[1], ("core",)),
        swap(pieces[2], ("xh",)),
        swap(pieces[3], ("xh", "core")),
    ]
    weight_away, weight_mine = stage_weight(me, output_weight, parts, blocks)
    columns = (place[:, None] * 4 + jnp.arange(tokens, dtype=jnp.int32)[None, :]).reshape(
        slots * tokens, 1
    )
    away, attention = merge_and_project(
        me, place, columns, returned.reshape(indices, 2, 16, D), pieces, weight_away
    )
    away = swap(away, ("core",))
    stay = project(attention, weight_mine)
    spread = lax.all_to_all(
        add_halves(stay, away), ("tensor", "xh"), split_axis=0, concat_axis=0, tiled=True
    )
    return sum_shares(spread, tokens)


def solution(mesh):
    sizes = mesh.shape
    fine = Mesh(
        mesh.devices.reshape(sizes["tensor"], sizes["prompt"], 2, sizes["cand"] // 2),
        ("tensor", "prompt", "xh", "core"),
    )
    slot = ("prompt", "xh", "core")
    cand = ("xh", "core")
    return jax.shard_map(
        body,
        mesh=fine,
        in_specs=(
            P(slot, None, "tensor"),
            P(slot, None, "tensor"),
            P(slot, None, "tensor"),
            P("prompt", cand, "tensor"),
            P("prompt", cand, "tensor"),
            P(slot, None, "tensor"),
            P(slot, None, "tensor"),
            P(slot),
            P("prompt", None),
            P(("tensor",) + cand, None),
        ),
        out_specs=P("prompt", None, ("tensor",) + cand),
        check_vma=False,
    )
```

time: 353 us -> 69.2 us (0.20)
  waiting for transfers between devices: 257 us -> 4.09 us
  matrix products: 30.5 us -> 0 us
  starting transfers between devices: 0.12 us -> 25.8 us
  blocking collectives: 33.2 us -> 15.8 us
  Pallas kernels: 0 us -> 17.4 us
  between operations: 13.3 us -> 0.21 us
  local copies, waits for them, and re-layouts: 13.8 us -> 5.3 us
    all_gather x3 -> x0, waiting for transfers between devices: 187 us -> none  [the longest x1 94.7 us: body(): value_piece = lax.all_gather(prefix_v, 'prompt', axis=0, tiled=True)]
    reduce_scatter x1 -> x0, waiting for transfers between devices: 68.6 us -> none  [body(): lax.psum_scatter(projected.astype(jnp.bfloat16), ('tensor', 'cand'), scat...]
    dot_general x17 -> x0, matrix products: 30.5 us -> none  [the longest x5 7.74 us: slot_partial(): jnp.einsum('stkgd,slkd->stkgl', shaped, key_view, preferred_element_type=...]
    all_gather x3 -> x0, blocking collectives: 24.6 us -> none  [the longest x2 14.4 us: joined(): everything = jax.tree.map(lambda part: lax.all_gather(part, axis), array)]
    pallas_call x0 -> x9, Pallas kernels: none -> 17.4 us  [the longest x1 6.12 us: suffix_attention(): pl.pallas_call(suffix_kernel, in_specs=[SMEM_SPEC, SMEM_SPEC, VMEM_SPEC,...]
    all_to_all x0 -> x2, starting transfers between devices: none -> 15.3 us  [the longest x1 9.3 us: body(): lax.all_to_all(routed.reshape(indices * 2, 16, D), ('prompt', 'xh'), spli...]
    ppermute x0 -> x7, starting transfers between devices: none -> 10.5 us  [swap(): return lax.ppermute(value, axes, [(i, size - 1 - i) for i in range(size)])]
    all_to_all x1, blocking collectives: 8.59 us -> 15.8 us  [body(): lax.all_to_all(add_halves(stay, away), ('tensor', 'xh'), split_axis=0, co...]
  transfers between devices with their start and end apart: 4 -> 9, of which waited for: 3 -> 2; matrix products, arithmetic and copies ran while one was open for 7% -> 0% of each run, Pallas kernels for 0% -> 19%
where the time goes in v2:
time: 69.2 us; the launch traced here: 68.8 us
  starting transfers between devices  25.8 us (37%)
  Pallas kernels  17.4 us (25%)
  blocking collectives  15.8 us (23%)
  local copies, waits for them, and re-layouts  5.3 us (8%)
  waiting for transfers between devices  4.09 us (6%)
    all_to_all x1, blocking collectives, body(): lax.all_to_all(add_halves(stay, away), ('tensor', 'xh'), split_axis=0, co...  15.8 us
    ppermute x7, starting transfers between devices, swap(): return lax.ppermute(value, axes, [(i, size - 1 - i) for i in range(size)])  10.5 us
    all_to_all x1, starting transfers between devices, body(): lax.all_to_all(routed.reshape(indices * 2, 16, D), ('prompt', 'xh'), spli...  9.3 us
    pallas_call x1, Pallas kernels, suffix_attention(): pl.pallas_call(suffix_kernel, in_specs=[SMEM_SPEC, SMEM_SPEC, VMEM_SPEC,...  6.12 us
    all_to_all x1, starting transfers between devices, body(): lax.all_to_all(parts.reshape(indices * 2, 16, D), ('prompt', 'xh'), split...  6.01 us
    unnamed x22, local copies, waits for them, and re-layouts  5.23 us
    pallas_call x1, Pallas kernels, stage_weight(): pl.pallas_call(stage_kernel, in_specs=[SMEM_SPEC, HBM_SPEC, HBM_SPEC], ou...  4.92 us
    all_to_all x1, waiting for transfers between devices, body(): lax.all_to_all(routed.reshape(indices * 2, 16, D), ('prompt', 'xh'), spli...  3.23 us
  transfers between devices with their start and end apart: 9, of which 2 were waited for; matrix products, arithmetic and copies ran while one was open for 0% of the time, Pallas kernels for 19%

profile of v2, /device:TPU:1, one launch (start us, length us, event | category | flops | bytes accessed | tf_op | source)
XLA Modules:
  0.0 68.8 jit_solution(14452107987469658469)
XLA Ops:
  0.0 3.2 %collective-permute-start.1 = (bf16[2,1024,128]{2,1,0:T(8,128)(2,1)}, bf16[2,1024,128]{2,1,0:T(8,128)(2,1)S(1)}, u32[]{:S(2)}, u32[]{:S(2)}) collective-permute-start(bf16[2,1024,128]{2,1,0:T(8,128)(2,1)} %k_own.1), channel_id=1, source_target_pairs={{0,1},{1,0},{2,3},{3,2},{4,5},{5,4},{6,7},{7,6},{8,9},{9,8},{10,11... | collective-permute-start | bytes 1572872 | tf_op jit(solution)/shard_map/ppermute | solution.py:382
  3.2 0.0 collective-permute-start.2
  3.2 0.1 pad_add_fusion.me_ref
  3.3 0.8 %copy-done.4 = bf16[8,2,1024]{2,1,0:T(2,128)(2,1)S(1)} copy-done((bf16[8,2,1024]{2,1,0:T(2,128)(2,1)S(1)}, bf16[8,2,1024]{2,1,0:T(2,128)(2,1)}, u32[]{:S(2)}) %copy-start.4) | copy-done | bytes 32792
  4.1 0.6 split_queries.1
  4.7 0.0 copy-start.3
  4.7 0.6 copy-done.3
  5.3 0.5 collective-permute-start
  5.8 0.8 %collective-permute-done.other_ref = bf16[64,128]{1,0:T(8,128)(2,1)S(1)} collective-permute-done((bf16[64,128]{1,0:T(8,128)(2,1)S(1)}, bf16[64,128]{1,0:T(8,128)(2,1)S(1)}, u32[]{:S(2)}, u32[]{:S(2)}) %collective-permute-start) | collective-permute-done | bytes 16416 | tf_op jit(solution)/shard_map/ppermute | solution.py:382
  6.6 0.7 copy-done.8
  7.3 1.2 %route_queries.1 = bf16[16,2,16,128]{3,2,1,0:T(8,128)(2,1)} custom-call(s32[2]{0:T(128)S(1)} %pad_add_fusion.me_ref, s32[32]{0:T(128)S(1)} %bitcast.10, bf16[64,128]{1,0:T(8,128)(2,1)S(1)} %get-tuple-element.26.mine_ref, bf16[64,128]{1,0:T(8,128)(2,1)S(1)} %collective-permute-done.other_ref), custom_call_target="tpu_custom_call" | custom-call | tf_op jit(solution)/shard_map/route_queries/pallas_call | solution.py:92
  8.5 9.3 %all-to-all-start = ((bf16[32,16,128]{2,1,0:T(8,128)(2,1)}), bf16[32,16,128]{2,1,0:T(8,128)(2,1)S(1)}, u32[]{:S(2)}, u32[]{:S(2)}) async-start(bf16[32,16,128]{2,1,0:T(8,128)(2,1)} %bitcast.3), calls=%async_computation | async-start | bytes 262144 | tf_op jit(solution)/shard_map/all_to_all | solution.py:409
  17.8 0.0 copy-done.6
  17.8 0.0 copy-start.1
  17.8 0.0 copy-start.2
  17.8 0.0 copy-start.9
  17.8 6.1 %suffix_attention.1 = (bf16[64,128]{1,0:T(8,128)(2,1)}, bf16[64,128]{1,0:T(8,128)(2,1)}, bf16[64,128]{1,0:T(8,128)(2,1)}, bf16[64,128]{1,0:T(8,128)(2,1)}) custom-call(s32[2]{0:T(128)} %copy-done.6, s32[8]{0:T(128)} %len_ref.1, bf16[8,16,128]{2,1,0:T(8,128)(2,1)} %copy-done.3, bf16[8,2,128]{2,1,0:T(2,128)(2,1)} %sk_ref.1, bf16[8,2,128]{2,1,0:T(2,128)(2,1)} %sv_ref.1, ...), custom_call_target="tpu_custom_call" | custom-call | flops 1073741824 | bytes 8388608 | tf_op jit(solution)/shard_map/suffix_attention/pallas_call | solution.py:165
  24.0 0.0 copy-start.5
  24.0 0.0 copy-start.7
  24.0 3.2 %all-to-all-done = bf16[32,16,128]{2,1,0:T(8,128)(2,1)S(1)} async-done(((bf16[32,16,128]{2,1,0:T(8,128)(2,1)}), bf16[32,16,128]{2,1,0:T(8,128)(2,1)S(1)}, u32[]{:S(2)}, u32[]{:S(2)}) %all-to-all-start) | async-done | bytes 131104 | tf_op jit(solution)/shard_map/all_to_all | solution.py:409
  27.2 0.0 collective-permute-done.1.k_other
  27.2 0.0 collective-permute-done.2.v_other
  27.2 0.0 copy-done.1
  27.2 0.0 copy-done.2
  27.2 1.9 %prefix_attention.1.after_ref = bf16[16,2,16,128]{3,2,1,0:T(8,128)(2,1)} custom-call(bf16[16,2,16,128]{3,2,1,0:T(8,128)(2,1)S(1)} %bitcast.9, bf16[2,1024,128]{2,1,0:T(8,128)(2,1)S(1)} %copy-done.1, bf16[2,1024,128]{2,1,0:T(8,128)(2,1)S(1)} %collective-permute-done.1.k_other, bf16[2,1024,128]{2,1,0:T(8,128)(2,1)S(1)} %copy-done.2, ...), custom_call_target="tpu_custom_call" | custom-call | tf_op jit(solution)/shard_map/prefix_attention/pallas_call | solution.py:221
  29.1 6.0 %all-to-all-start.1 = ((bf16[32,16,128]{2,1,0:T(8,128)(2,1)}), bf16[32,16,128]{2,1,0:T(8,128)(2,1)S(1)}, u32[]{:S(2)}, u32[]{:S(2)}) async-start(bf16[32,16,128]{2,1,0:T(8,128)(2,1)} %bitcast.5), calls=%async_computation.1 | async-start | bytes 262144 | tf_op jit(solution)/shard_map/all_to_all | solution.py:419
  35.2 0.0 copy-done.9
  35.2 1.3 %collective-permute-start.3 = (bf16[64,128]{1,0:T(8,128)(2,1)}, bf16[64,128]{1,0:T(8,128)(2,1)S(1)}, u32[]{:S(2)}, u32[]{:S(2)}) collective-permute-start(bf16[64,128]{1,0:T(8,128)(2,1)} %get-tuple-element.30), channel_id=1, source_target_pairs={{0,1},{1,0},{2,3},{3,2},{4,5},{5,4},{6,7},{7,6},{8,9},{9,8},{10,11... | collective-permute-start | bytes 49160 | tf_op jit(solution)/shard_map/ppermute | solution.py:382
  36.4 3.0 %collective-permute-start.4 = (bf16[64,128]{1,0:T(8,128)(2,1)}, bf16[64,128]{1,0:T(8,128)(2,1)S(1)}, u32[]{:S(2)}, u32[]{:S(2)}) collective-permute-start(bf16[64,128]{1,0:T(8,128)(2,1)} %get-tuple-element.31), channel_id=1, source_target_pairs={{0,2},{2,0},{1,3},{3,1},{4,6},{6,4},{5,7},{7,5},{8,10},{10,8},{9,1... | collective-permute-start | bytes 49160 | tf_op jit(solution)/shard_map/ppermute | solution.py:382
  39.5 0.2 collective-permute-start.5
  39.7 0.1 iota_add_fusion
  39.8 0.1 add.27.col_ref
  39.8 4.9 %stage_weight.1 = (bf16[8,256,512]{2,1,0:T(8,128)(2,1)}, bf16[8,256,512]{2,1,0:T(8,128)(2,1)}) custom-call(s32[2]{0:T(128)} %copy-done.6, bf16[256,8192]{1,0:T(8,128)(2,1)} %w_hbm.1, bf16[16,2,16,128]{3,2,1,0:T(8,128)(2,1)} %prefix_attention.1.after_ref), custom_call_target="tpu_custom_call" | custom-call | bytes 8388608 | tf_op jit(solution)/shard_map/stage_weight/pallas_call | solution.py:250
  44.8 0.0 collective-permute-done.3.suf1
  44.8 0.0 collective-permute-done.4.suf2
  44.8 0.0 collective-permute-done.5.suf3
  44.8 0.0 all-to-all-done.1
  44.8 0.0 copy-done.5
  44.8 0.0 copy-done.7
  44.8 1.6 %copy-done = bf16[8,256,512]{2,1,0:T(8,128)(2,1)S(1)} copy-done((bf16[8,256,512]{2,1,0:T(8,128)(2,1)S(1)}, bf16[8,256,512]{2,1,0:T(8,128)(2,1)}, u32[]{:S(2)}) %copy-start) | copy-done | bytes 2097176
  46.4 1.4 %merge_and_project.1 = (bf16[8,64,512]{2,1,0:T(8,128)(2,1)S(1)}, bf16[64,256]{1,0:T(8,128)(2,1)S(1)}) custom-call(s32[2]{0:T(128)S(1)} %copy-done.7, s32[32]{0:T(128)S(1)} %bitcast.11, s32[64,1]{1,0:T(8,128)S(1)} %add.27.col_ref, bf16[16,2,16,128]{3,2,1,0:T(8,128)(2,1)S(1)} %bitcast.8, bf16[64,128]{1,0:T(8,128)(2,1)S(1)} %copy-done.5, ...), custom_call_target="tpu_custom_call" | custom-call | tf_op jit(solution)/shard_map/merge_and_project/pallas_call | solution.py:309
  47.8 2.2 %collective-permute-start.6 = (bf16[8,64,512]{2,1,0:T(8,128)(2,1)S(1)}, bf16[8,64,512]{2,1,0:T(8,128)(2,1)S(1)}, u32[]{:S(2)}, u32[]{:S(2)}) collective-permute-start(bf16[8,64,512]{2,1,0:T(8,128)(2,1)S(1)} %get-tuple-element.36), channel_id=1, source_target_pairs={{0,1},{1,0},{2,3},{3,2},{4,5},{5,4},{6,7},{7,6},{8,9},{9,8},{10,11... | collective-permute-start | bytes 1572872 | tf_op jit(solution)/shard_map/ppermute | solution.py:382
  50.0 1.6 %copy-done.10 = bf16[8,256,512]{2,1,0:T(8,128)(2,1)S(1)} copy-done((bf16[8,256,512]{2,1,0:T(8,128)(2,1)S(1)}, bf16[8,256,512]{2,1,0:T(8,128)(2,1)}, u32[]{:S(2)}) %copy-start.10) | copy-done | bytes 2097176
  51.6 0.5 project.1.one_ref
  52.1 0.0 collective-permute-done.6.two_ref
  52.1 0.1 add_halves.1
  52.2 15.8 %all_to_all.15.in_ref = bf16[8,64,512]{2,1,0:T(8,128)(2,1)S(1)} all-to-all(bf16[8,64,512]{2,1,0:T(8,128)(2,1)S(1)} %add_halves.1), channel_id=1, replica_groups=mesh['tensor'=4,'prompt'=16,'xh'=2,'core'=2] {'tensor','xh'}, dimensions={0} | all-to-all | bytes 1048576 | tf_op jit(solution)/shard_map/all_to_all | solution.py:437
  68.1 0.7 %sum_shares.1 = bf16[32,2,512]{2,1,0:T(2,128)(2,1)} custom-call(bf16[8,64,512]{2,1,0:T(8,128)(2,1)S(1)} %all_to_all.15.in_ref), custom_call_target="tpu_custom_call" | custom-call | tf_op jit(solution)/shard_map/sum_shares/pallas_call | solution.py:370
  (6 shorter events, 0.0 us)
Async XLA Ops:
  0.0 27.2 %collective-permute-start.1 = (bf16[2,1024,128]{2,1,0:T(8,128)(2,1)}, bf16[2,1024,128]{2,1,0:T(8,128)(2,1)S(1)}, u32[]{:S(2)}, u32[]{:S(2)}) collective-permute-start(bf16[2,1024,128]{2,1,0:T(8,128)(2,1)} %k_own.1), channel_id=1, source_target_pairs={{0,1},{1,0},{2,3},{3,2},{4,5},{5,4},{6,7},{7,6},{8,9},{9,8},{10,11... | collective-permute-start | bytes 1572872 | tf_op jit(solution)/shard_map/ppermute | solution.py:382
  3.2 24.0 %collective-permute-start.2 = (bf16[2,1024,128]{2,1,0:T(8,128)(2,1)}, bf16[2,1024,128]{2,1,0:T(8,128)(2,1)S(1)}, u32[]{:S(2)}, u32[]{:S(2)}) collective-permute-start(bf16[2,1024,128]{2,1,0:T(8,128)(2,1)} %v_own.1), channel_id=1, source_target_pairs={{0,1},{1,0},{2,3},{3,2},{4,5},{5,4},{6,7},{7,6},{8,9},{9,8},{10,11... | collective-permute-start | bytes 1572872 | tf_op jit(solution)/shard_map/ppermute | solution.py:382
  3.3 0.8 %copy-start.4 = (bf16[8,2,1024]{2,1,0:T(2,128)(2,1)S(1)}, bf16[8,2,1024]{2,1,0:T(2,128)(2,1)}, u32[]{:S(2)}) copy-start(bf16[8,2,1024]{2,1,0:T(2,128)(2,1)} %q_ref.1) | copy-start | bytes 98308
  4.1 13.7 %copy-start.6 = (s32[2]{0:T(128)}, s32[2]{0:T(128)S(1)}, u32[]{:S(2)}) copy-start(s32[2]{0:T(128)S(1)} %pad_add_fusion.me_ref) | copy-start | bytes 28
  4.7 0.6 copy-start.3
  5.3 1.3 %collective-permute-start = (bf16[64,128]{1,0:T(8,128)(2,1)S(1)}, bf16[64,128]{1,0:T(8,128)(2,1)S(1)}, u32[]{:S(2)}, u32[]{:S(2)}) collective-permute-start(bf16[64,128]{1,0:T(8,128)(2,1)S(1)} %get-tuple-element.27), channel_id=1, source_target_pairs={{0,1},{1,0},{2,3},{3,2},{4,5},{5,4},{6,7},{7,6},{8,9},{9,8},{10,11... | collective-permute-start | bytes 49160 | tf_op jit(solution)/shard_map/ppermute | solution.py:382
  6.6 0.7 copy-start.8
  8.5 18.7 %all-to-all-start = ((bf16[32,16,128]{2,1,0:T(8,128)(2,1)}), bf16[32,16,128]{2,1,0:T(8,128)(2,1)S(1)}, u32[]{:S(2)}, u32[]{:S(2)}) async-start(bf16[32,16,128]{2,1,0:T(8,128)(2,1)} %bitcast.3), calls=%async_computation | async-start | bytes 262144 | tf_op jit(solution)/shard_map/all_to_all | solution.py:409
  17.8 9.4 %copy-start.1 = (bf16[2,1024,128]{2,1,0:T(8,128)(2,1)S(1)}, bf16[2,1024,128]{2,1,0:T(8,128)(2,1)}, u32[]{:S(2)}) copy-start(bf16[2,1024,128]{2,1,0:T(8,128)(2,1)} %k_own.1) | copy-start | bytes 1572868
  17.8 9.4 %copy-start.2 = (bf16[2,1024,128]{2,1,0:T(8,128)(2,1)S(1)}, bf16[2,1024,128]{2,1,0:T(8,128)(2,1)}, u32[]{:S(2)}) copy-start(bf16[2,1024,128]{2,1,0:T(8,128)(2,1)} %v_own.1) | copy-start | bytes 1572868
  17.8 17.3 %copy-start.9 = (s32[1,32]{1,0:T(1,128)S(1)}, s32[1,32]{1,0:T(1,128)}, u32[]{:S(2)}) copy-start(s32[1,32]{1,0:T(1,128)} %param.18) | copy-start | bytes 388
  24.0 20.8 %copy-start.5 = (bf16[64,128]{1,0:T(8,128)(2,1)S(1)}, bf16[64,128]{1,0:T(8,128)(2,1)}, u32[]{:S(2)}) copy-start(bf16[64,128]{1,0:T(8,128)(2,1)} %get-tuple-element.29.suf0) | copy-start | bytes 49156
  24.0 20.8 %copy-start.7 = (s32[2]{0:T(128)S(1)}, s32[2]{0:T(128)}, u32[]{:S(2)}) copy-start(s32[2]{0:T(128)} %copy-done.6) | copy-start | bytes 28
  29.1 15.6 %all-to-all-start.1 = ((bf16[32,16,128]{2,1,0:T(8,128)(2,1)}), bf16[32,16,128]{2,1,0:T(8,128)(2,1)S(1)}, u32[]{:S(2)}, u32[]{:S(2)}) async-start(bf16[32,16,128]{2,1,0:T(8,128)(2,1)} %bitcast.5), calls=%async_computation.1 | async-start | bytes 262144 | tf_op jit(solution)/shard_map/all_to_all | solution.py:419
  35.2 9.6 %collective-permute-start.3 = (bf16[64,128]{1,0:T(8,128)(2,1)}, bf16[64,128]{1,0:T(8,128)(2,1)S(1)}, u32[]{:S(2)}, u32[]{:S(2)}) collective-permute-start(bf16[64,128]{1,0:T(8,128)(2,1)} %get-tuple-element.30), channel_id=1, source_target_pairs={{0,1},{1,0},{2,3},{3,2},{4,5},{5,4},{6,7},{7,6},{8,9},{9,8},{10,11... | collective-permute-start | bytes 49160 | tf_op jit(solution)/shard_map/ppermute | solution.py:382
  36.4 8.3 %collective-permute-start.4 = (bf16[64,128]{1,0:T(8,128)(2,1)}, bf16[64,128]{1,0:T(8,128)(2,1)S(1)}, u32[]{:S(2)}, u32[]{:S(2)}) collective-permute-start(bf16[64,128]{1,0:T(8,128)(2,1)} %get-tuple-element.31), channel_id=1, source_target_pairs={{0,2},{2,0},{1,3},{3,1},{4,6},{6,4},{5,7},{7,5},{8,10},{10,8},{9,1... | collective-permute-start | bytes 49160 | tf_op jit(solution)/shard_map/ppermute | solution.py:382
  39.5 5.3 %collective-permute-start.5 = (bf16[64,128]{1,0:T(8,128)(2,1)}, bf16[64,128]{1,0:T(8,128)(2,1)S(1)}, u32[]{:S(2)}, u32[]{:S(2)}) collective-permute-start(bf16[64,128]{1,0:T(8,128)(2,1)} %get-tuple-element.32), channel_id=1, source_target_pairs={{0,3},{1,2},{2,1},{3,0},{4,7},{5,6},{6,5},{7,4},{8,11},{9,10},{10,... | collective-permute-start | bytes 49160 | tf_op jit(solution)/shard_map/ppermute | solution.py:382
  44.8 1.6 %copy-start = (bf16[8,256,512]{2,1,0:T(8,128)(2,1)S(1)}, bf16[8,256,512]{2,1,0:T(8,128)(2,1)}, u32[]{:S(2)}) copy-start(bf16[8,256,512]{2,1,0:T(8,128)(2,1)} %get-tuple-element.33.w_ref) | copy-start | bytes 6291460
  47.8 4.3 %collective-permute-start.6 = (bf16[8,64,512]{2,1,0:T(8,128)(2,1)S(1)}, bf16[8,64,512]{2,1,0:T(8,128)(2,1)S(1)}, u32[]{:S(2)}, u32[]{:S(2)}) collective-permute-start(bf16[8,64,512]{2,1,0:T(8,128)(2,1)S(1)} %get-tuple-element.36), channel_id=1, source_target_pairs={{0,1},{1,0},{2,3},{3,2},{4,5},{5,4},{6,7},{7,6},{8,9},{9,8},{10,11... | collective-permute-start | bytes 1572872 | tf_op jit(solution)/shard_map/ppermute | solution.py:382
  50.0 1.6 %copy-start.10 = (bf16[8,256,512]{2,1,0:T(8,128)(2,1)S(1)}, bf16[8,256,512]{2,1,0:T(8,128)(2,1)}, u32[]{:S(2)}) copy-start(bf16[8,256,512]{2,1,0:T(8,128)(2,1)} %get-tuple-element.35.w_ref) | copy-start | bytes 6291460

commit v3 on v2

--- a/solution.py
+++ b/solution.py
@@ -11,10 +11,12 @@
 SCALE2 = 1.4426950408889634 / math.sqrt(D)
 HIDDEN = -1e30
 GROUP = 2
+CHUNKS = 4
+BLOCK = 2048
 F32 = jnp.float32
 BF16 = jnp.bfloat16
 VMEM_LIMIT = 32 * 1024 * 1024
-VMEM_MOST = 57 * 1024 * 1024
+
 VMEM_SPEC = pl.BlockSpec(memory_space=pltpu.VMEM)
 SMEM_SPEC = pl.BlockSpec(memory_space=pltpu.SMEM)
 HBM_SPEC = pl.BlockSpec(memory_space=pltpu.HBM)
@@ -46,77 +48,116 @@
     return lax.broadcasted_iota(jnp.int32, shape, len(shape) - 2) < 4
 
 
-def queries_kernel(me_ref, q_ref, all_ref, mine_ref, other_ref, rows):
+def in_hbm(value):
+    return pltpu.with_memory_space_constraint(value, pltpu.HBM)
+
+
+def split_rows(q_ref, rows):
     slots, tokens, width = q_ref.shape
-    core = me_ref[1]
     for i in range(slots):
         wide = q_ref[i].astype(F32)
         for h in range(width // D):
             place = (h // 4) * 4 + (h % 2) * tokens
             rows[(h // 2) % 2, i, place : place + tokens, :] = wide[:, h * D : (h + 1) * D]
-    all_ref[...] = jnp.concatenate([rows[0], rows[1]], axis=1).astype(BF16)
-    mine_ref[...] = rows[core].reshape(slots * 8, D).astype(BF16)
-    other_ref[...] = rows[1 - core].reshape(slots * 8, D).astype(BF16)
-
-
-def split_queries(me, q_step):
-    slots = q_step.shape[0]
-    half = jax.ShapeDtypeStruct((slots * 8, D), BF16)
-    return pl.pallas_call(
-        queries_kernel,
-        in_specs=[SMEM_SPEC, VMEM_SPEC],
-        out_specs=[VMEM_SPEC] * 3,
-        out_shape=[jax.ShapeDtypeStruct((slots, 16, D), BF16), half, half],
-        scratch_shapes=[pltpu.VMEM((2, slots, 8, D), F32)],
-        compiler_params=PARAMS,
-        name="split_queries",
-    )(me, q_step)
-
-
-def route_kernel(me_ref, place_ref, mine_ref, other_ref, out_ref, rows):
-    xh, core = me_ref[0], me_ref[1]
-    count = mine_ref.shape[0] // 8
+
+
+def scatter_rows(q_ref, here_ref, rows, first, core):
+    count, tokens, _ = q_ref.shape
+    for i in range(count):
+        u = here_ref[2 + first + i]
+        wide = q_ref[i].astype(F32)
+        for j in range(4):
+            h = 4 * (j // 2) + j % 2
+            one = wide[:, h * D : (h + 1) * D]
+            two = wide[:, (h + 2) * D : (h + 3) * D]
+            rows[u, j * tokens : (j + 1) * tokens, :] = jnp.where(core == 0, one, two)
+
+
+def own_kernel(here_ref, q_hbm, rows, mine_ref, sem):
+    xh, core = here_ref[0], here_ref[1]
+    copy = pltpu.make_async_copy(q_hbm, mine_ref, sem)
+    copy.start()
     rows[...] = jnp.zeros_like(rows)
-    for ref, column in ((mine_ref, core), (other_ref, 1 - core)):
-        value = ref[...].astype(F32)
-        for i in range(count):
-            slot = (2 * xh + column) * count + i
-            rows[place_ref[slot]] = value[i * 8 : (i + 1) * 8]
+    copy.wait()
+    scatter_rows(mine_ref, here_ref, rows, (2 * xh + core) * q_hbm.shape[0], core)
+
+
+def own_rows(here, mine, slots):
+    return pl.pallas_call(
+        own_kernel,
+        in_specs=[SMEM_SPEC, HBM_SPEC],
+        out_specs=VMEM_SPEC,
+        out_shape=jax.ShapeDtypeStruct((slots, 8, D), F32),
+        scratch_shapes=[pltpu.VMEM(mine.shape, BF16), pltpu.SemaphoreType.DMA],
+        cost_estimate=pl.CostEstimate(
+            flops=0, bytes_accessed=2 * 1024 * 1024, transcendentals=0
+        ),
+        compiler_params=PARAMS,
+        name="own_rows",
+    )(here, in_hbm(mine))
+
+
+def route_kernel(here_ref, own_ref, other_ref, out_ref, rows):
+    xh, core = here_ref[0], here_ref[1]
+    rows[...] = own_ref[...]
+    first = (2 * xh + 1 - core) * other_ref.shape[0]
+    scatter_rows(other_ref, here_ref, rows, first, core)
     packed = rows[...].reshape(out_ref.shape[0], 16, D).astype(BF16)
     for j in range(out_ref.shape[1]):
         out_ref[:, j] = packed
 
 
-def route(me, placement, mine, other, indices):
-    slots = placement.shape[0]
+def route(here, own, other, indices):
     return pl.pallas_call(
         route_kernel,
-        in_specs=[SMEM_SPEC, SMEM_SPEC, VMEM_SPEC, VMEM_SPEC],
+        in_specs=[SMEM_SPEC, VMEM_SPEC, VMEM_SPEC],
         out_specs=VMEM_SPEC,
         out_shape=jax.ShapeDtypeStruct((indices, 2, 16, D), BF16),
-        scratch_shapes=[pltpu.VMEM((slots, 8, D), F32)],
+        scratch_shapes=[pltpu.VMEM(own.shape, F32)],
         compiler_params=PARAMS,
         name="route_queries",
-    )(me, placement, mine, other)
-
-
-def suffix_kernel(me_ref, len_ref, q_ref, sk_ref, sv_ref, k_hbm, v_hbm, *rest):
-    outs, (keys, values, tiles, key_sem, value_sem) = rest[:4], rest[4:]
+    )(here, own, other)
+
+
+def suffix_kernel(me_ref, len_hbm, q_hbm, sk_hbm, sv_hbm, k_hbm, v_hbm, *rest):
+    keep_ref, core_ref, xh_ref = rest[:3]
+    len_ref, q_ref, sk_ref, sv_ref, rows_ref, keys, values, tiles, small_sem, sem = rest[3:]
     slots, span, _ = k_hbm.shape
-    tokens = sk_ref.shape[1]
+    tokens = sk_hbm.shape[1]
     xh, core = me_ref[0], me_ref[1]
     lower = lower_rows((8, D))
-
-    def copies(i):
+    lengths_copy = pltpu.make_async_copy(len_hbm, len_ref, small_sem.at[0])
+    lengths_copy.start()
+    small = (
+        pltpu.make_async_copy(q_hbm, q_ref, small_sem.at[1]),
+        pltpu.make_async_copy(sk_hbm, sk_ref, small_sem.at[2]),
+        pltpu.make_async_copy(sv_hbm, sv_ref, small_sem.at[3]),
+    )
+
+    def copies(i, b):
+        part = pl.ds(b * BLOCK, BLOCK)
         return (
-            pltpu.make_async_copy(k_hbm.at[i], keys.at[i], key_sem.at[i]),
-            pltpu.make_async_copy(v_hbm.at[i], values.at[i], value_sem.at[i]),
+            pltpu.make_async_copy(k_hbm.at[i, part], keys.at[i, part], sem.at[0, i, b]),
+            pltpu.make_async_copy(v_hbm.at[i, part], values.at[i, part], sem.at[1, i, b]),
         )
 
+    for copy in copies(0, 0) + small:
+        copy.start()
+    lengths_copy.wait()
+    blocks = span // BLOCK
     for i in range(slots):
-        for copy in copies(i):
-            copy.start()
-    rows = q_ref.shape[1]
+        for b in range(blocks):
+            if i + b > 0:
+
+                @pl.when(b * BLOCK < len_ref[i])
+                def _():
+                    for copy in copies(i, b):
+                        copy.start()
+
+    for copy in small:
+        copy.wait()
+    split_rows(q_ref, rows_ref)
+    rows = 16
     row_token = lax.broadcasted_iota(jnp.int32, (rows, tokens), 0) % tokens
     key_token = lax.broadcasted_iota(jnp.int32, (rows, tokens), 1)
     causal = key_token <= row_token
@@ -124,9 +165,25 @@
     for first in range(0, slots, GROUP):
         group = range(first, first + GROUP)
         for i in group:
-            for copy in copies(i):
-                copy.wait()
-        q = [q_ref[i] for i in group]
+            for b in range(blocks):
+                if b == 0:
+                    for copy in copies(i, b):
+                        copy.wait()
+                    continue
+                live = b * BLOCK < len_ref[i]
+
+                @pl.when(live)
+                def _():
+                    for copy in copies(i, b):
+                        copy.wait()
+
+                @pl.when(jnp.logical_not(live))
+                def _():
+                    values[i, b * BLOCK : (b + 1) * BLOCK, :] = jnp.zeros((BLOCK, D), BF16)
+
+        q = [
+            jnp.concatenate([rows_ref[0, i], rows_ref[1, i]], axis=0).astype(BF16) for i in group
+        ]
         scores = [dot_t(q[n], keys[i]) for n, i in enumerate(group)]
         step_scores = [dot_t(q[n], sk_ref[i]) for n, i in enumerate(group)]
         scores = [
@@ -152,36 +209,53 @@
                 one, two = value[c * 8 : c * 8 + 8], stat[c * 8 : c * 8 + 8]
                 tiles[c, i] = jnp.where(lower, one, pltpu.roll(two, 4, 0))
                 tiles[2 + c, i] = jnp.where(lower, pltpu.roll(one, 4, 0), two)
-    for j, out in enumerate(outs):
-        to_xh = xh if j // 2 == 0 else 1 - xh
-        to_core = core if j % 2 == 0 else 1 - core
-        out[...] = tiles[2 * to_xh + to_core].reshape(slots * 8, D).astype(BF16)
-
-
-def suffix_attention(me, lengths, q_rows, step_k, step_values, suffix_k, suffix_values):
+
+    def piece(to_xh, to_core):
+        return tiles[2 * to_xh + to_core].reshape(slots * 8, D).astype(BF16)
+
+    keep_ref[...] = piece(xh, core)
+    core_ref[...] = jnp.concatenate([piece(xh, 1 - core), piece(1 - xh, 1 - core)], axis=0)
+    xh_ref[...] = piece(1 - xh, core)
+
+
+def suffix_attention(me, lengths, q_step, step_k, step_values, suffix_k, suffix_values):
     slots, span, _ = suffix_k.shape
-    rows = q_rows.shape[1]
+    rows = 16
     piece = jax.ShapeDtypeStruct((slots * 8, D), BF16)
+    blocks = span // BLOCK
     return pl.pallas_call(
         suffix_kernel,
-        in_specs=[SMEM_SPEC, SMEM_SPEC, VMEM_SPEC, VMEM_SPEC, VMEM_SPEC, HBM_SPEC, HBM_SPEC],
-        out_specs=[VMEM_SPEC] * 4,
-        out_shape=[piece] * 4,
+        in_specs=[SMEM_SPEC] + [HBM_SPEC] * 6,
+        out_specs=[VMEM_SPEC] * 3,
+        out_shape=[piece, jax.ShapeDtypeStruct((slots * 16, D), BF16), piece],
         scratch_shapes=[
+            pltpu.SMEM(lengths.shape, jnp.int32),
+            pltpu.VMEM(q_step.shape, BF16),
+            pltpu.VMEM(step_k.shape, BF16),
+            pltpu.VMEM(step_values.shape, BF16),
+            pltpu.VMEM((2, slots, 8, D), F32),
             pltpu.VMEM((slots, span, D), BF16),
             pltpu.VMEM((slots, span, D), BF16),
             pltpu.VMEM((4, slots, 8, D), F32),
-            pltpu.SemaphoreType.DMA((slots,)),
-            pltpu.SemaphoreType.DMA((slots,)),
+            pltpu.SemaphoreType.DMA((4,)),
+            pltpu.SemaphoreType.DMA((2, slots, blocks)),
         ],
         cost_estimate=pl.CostEstimate(
             flops=4 * slots * rows * span * D * 8,
             bytes_accessed=4 * slots * span * D,
             transcendentals=slots * rows * span,
         ),
-        compiler_params=pltpu.CompilerParams(vmem_limit_bytes=VMEM_MOST),
+        compiler_params=PARAMS,
         name="suffix_attention",
-    )(me, lengths, q_rows, step_k, step_values, suffix_k, suffix_values)
+    )(
+        me,
+        in_hbm(lengths),
+        in_hbm(q_step),
+        in_hbm(step_k),
+        in_hbm(step_values),
+        in_hbm(suffix_k),
+        in_hbm(suffix_values),
+    )
 
 
 def prefix_kernel(q_ref, k_own, k_other, v_own, v_other, out_ref):
@@ -228,53 +302,86 @@
     )(q_rows, k_own, k_other, v_own, v_other)
 
 
-def stage_kernel(me_ref, w_hbm, after_ref, away_ref, mine_ref, sem):
-    core = me_ref[1]
-    blocks, _, width = mine_ref.shape
-    copies = []
-    for half, (out_ref, which) in enumerate(((away_ref, 1 - core), (mine_ref, core))):
-        for b in range(blocks):
-            columns = pl.ds(pl.multiple_of((2 * b + which) * width, width), width)
-            copies.append(
-                pltpu.make_async_copy(w_hbm.at[:, columns], out_ref.at[b], sem.at[half, b])
-            )
-    for copy in copies:
+def low_copies(w_hbm, low_ref, sem, which):
+    blocks, depth, width = low_ref.shape
+    return [
+        pltpu.make_async_copy(
+            w_hbm.at[pl.ds(depth, depth), block_columns(2 * b + which, width)],
+            low_ref.at[b],
+            sem.at[b],
+        )
+        for b in range(blocks)
+    ]
+
+
+def stage_kernel(here_ref, w_hbm, after_ref, upper_ref, low_ref, mine_hbm, mine_ref, *sems):
+    upper_sem, low_sem, mine_sem, out_sem = sems
+    core = here_ref[1]
+    chunk = upper_ref.shape[0] // CHUNKS
+    mine = low_copies(w_hbm, mine_ref, mine_sem, core)
+    copies = low_copies(w_hbm, low_ref, low_sem, 1 - core)
+    for j in range(CHUNKS):
+        part = pl.ds(j * chunk, chunk)
+        copies.append(pltpu.make_async_copy(w_hbm.at[part], upper_ref.at[part], upper_sem.at[j]))
+    for copy in mine + copies:
         copy.start()
-    for copy in copies:
+    out = [
+        pltpu.make_async_copy(mine_ref.at[b], mine_hbm.at[b], out_sem.at[b])
+        for b in range(len(mine))
+    ]
+    for arrived, copy in zip(mine, out):
+        arrived.wait()
+        copy.start()
+    for copy in copies + out:
         copy.wait()
 
 
-def stage_weight(me, weight, after, blocks):
+def stage_weight(here, weight, after, blocks):
     depth, width = weight.shape
-    half = jax.ShapeDtypeStruct((blocks, depth, width // (2 * blocks)), BF16)
+    low = (blocks, depth // 2, width // (2 * blocks))
     return pl.pallas_call(
         stage_kernel,
-        in_specs=[SMEM_SPEC, HBM_SPEC, HBM_SPEC],
-        out_specs=[VMEM_SPEC] * 2,
-        out_shape=[half] * 2,
-        scratch_shapes=[pltpu.SemaphoreType.DMA((2, blocks))],
+        in_specs=[SMEM_SPEC, HBM_SPEC, pl.BlockSpec(memory_space=pl.ANY)],
+        out_specs=[VMEM_SPEC, VMEM_SPEC, HBM_SPEC],
+        out_shape=[
+            jax.ShapeDtypeStruct((depth // 2, width), BF16),
+            jax.ShapeDtypeStruct(low, BF16),
+            jax.ShapeDtypeStruct(low, BF16),
+        ],
+        scratch_shapes=[
+            pltpu.VMEM(low, BF16),
+            pltpu.SemaphoreType.DMA((CHUNKS,)),
+            pltpu.SemaphoreType.DMA((blocks,)),
+            pltpu.SemaphoreType.DMA((blocks,)),
+            pltpu.SemaphoreType.DMA((blocks,)),
+        ],
         cost_estimate=pl.CostEstimate(
-            flops=0, bytes_accessed=4 * depth * width, transcendentals=0
+            flops=0, bytes_accessed=5 * depth * width, transcendentals=0
         ),
-        compiler_params=pltpu.CompilerParams(vmem_limit_bytes=54 * 1024 * 1024),
+        compiler_params=PARAMS,
         name="stage_weight",
-    )(me, weight, after)
+    )(here, in_hbm(weight), after)
+
+
+def block_columns(block, width):
+    return pl.ds(pl.multiple_of(block * width, width), width)
 
 
 def merge_kernel(
-    me_ref, place_ref, col_ref, parts_ref, suf0, suf1, suf2, suf3, w_ref, out_ref, att_ref, own
+    here_ref, col_ref, parts_ref, keep_ref, near_ref, far_ref, upper_ref, low_ref, *rest
 ):
-    xh, core = me_ref[0], me_ref[1]
-    blocks, out_rows, _ = out_ref.shape
+    out_ref, att_ref, own = rest
+    xh, core = here_ref[0], here_ref[1]
+    blocks, out_rows, width = out_ref.shape
     owners = parts_ref.shape[0]
-    count = suf0.shape[0] // 8
-    for j, ref in enumerate((suf0, suf1, suf2, suf3)):
-        from_xh = xh if j // 2 == 0 else 1 - xh
-        from_core = core if j % 2 == 0 else 1 - core
-        value = ref[...].astype(F32)
+    count = keep_ref.shape[0] // 8
+    pieces = ((keep_ref, 0, xh, core), (near_ref, 0, xh, 1 - core))
+    pieces += ((far_ref, 0, 1 - xh, core), (far_ref, count, 1 - xh, 1 - core))
+    for ref, start, from_xh, from_core in pieces:
+        value = ref[start * 8 : (start + count) * 8, :].astype(F32)
         for i in range(count):
             slot = (2 * from_xh + from_core) * count + i
-            own[place_ref[slot]] = value[i * 8 : (i + 1) * 8]
+            own[here_ref[2 + slot]] = value[i * 8 : (i + 1) * 8]
     lower = lower_rows((owners, 8, D))
     both = own[...].reshape(owners, 2, 8, D)
     one, two = both[:, 0], both[:, 1]
@@ -298,49 +405,63 @@
     for h in range(2):
         pick = jnp.where(lane == col_ref[...] + 2 * h, 1.0, 0.0).astype(BF16)
         att_ref[:, h * D : (h + 1) * D] = dot(pick, merged).astype(BF16)
+    half = low_ref.shape[1]
     for b in range(blocks):
-        out_ref[b] = dot(att_ref[...], w_ref[b]).astype(BF16)
-
-
-def merge_and_project(me, placement, columns, parts, pieces, weight):
-    slots = placement.shape[0]
-    blocks, depth, width = weight.shape
+        columns = block_columns(2 * b + 1 - core, width)
+        value = dot(att_ref[:, 0:half], upper_ref[:, columns])
+        out_ref[b] = (value + dot(att_ref[:, half:], low_ref[b])).astype(BF16)
+
+
+def merge_and_project(here, slots, columns, parts, pieces, upper, low):
+    blocks, half, width = low.shape
     out_rows = columns.shape[0]
     return pl.pallas_call(
         merge_kernel,
-        in_specs=[SMEM_SPEC, SMEM_SPEC] + [VMEM_SPEC] * 7,
+        in_specs=[SMEM_SPEC] + [VMEM_SPEC] * 7,
         out_specs=[VMEM_SPEC, VMEM_SPEC],
         out_shape=[
             jax.ShapeDtypeStruct((blocks, out_rows, width), BF16),
-            jax.ShapeDtypeStruct((out_rows, depth), BF16),
+            jax.ShapeDtypeStruct((out_rows, 2 * half), BF16),
         ],
         scratch_shapes=[pltpu.VMEM((slots, 8, D), F32)],
         compiler_params=PARAMS,
         name="merge_and_project",
-    )(me, placement, columns, parts, *pieces, weight)
-
-
-def project_kernel(att_ref, w_ref, out_ref):
-    for b in range(out_ref.shape[0]):
-        out_ref[b] = dot(att_ref[...], w_ref[b])
-
-
-def project(attention, weight):
+    )(here, columns, parts, *pieces, upper, low)
+
+
+def project_kernel(here_ref, att_ref, upper_ref, low_hbm, out_ref, low_ref, sem):
+    blocks, half, width = low_ref.shape
+    copies = [
+        pltpu.make_async_copy(low_hbm.at[b], low_ref.at[b], sem.at[b]) for b in range(blocks)
+    ]
+    for copy in copies:
+        copy.start()
+    for b in range(blocks):
+        columns = block_columns(2 * b + here_ref[1], width)
+        out_ref[b] = dot(att_ref[:, 0:half], upper_ref[:, columns])
+    for copy in copies:
+        copy.wait()
+    for b in range(blocks):
+        out_ref[b] += dot(att_ref[:, half:], low_ref[b])
+
+
+def project(here, attention, upper, low):
+    blocks, half, width = low.shape
     out_rows = attention.shape[0]
-    blocks, depth, width = weight.shape
     return pl.pallas_call(
         project_kernel,
-        in_specs=[VMEM_SPEC] * 2,
+        in_specs=[SMEM_SPEC, VMEM_SPEC, VMEM_SPEC, HBM_SPEC],
         out_specs=VMEM_SPEC,
         out_shape=jax.ShapeDtypeStruct((blocks, out_rows, width), F32),
+        scratch_shapes=[pltpu.VMEM(low.shape, BF16), pltpu.SemaphoreType.DMA((blocks,))],
         cost_estimate=pl.CostEstimate(
-            flops=2 * out_rows * depth * width * blocks * 8,
-            bytes_accessed=2 * depth * width * blocks,
+            flops=4 * out_rows * half * width * blocks * 8,
+            bytes_accessed=4 * half * width * blocks,
             transcendentals=0,
         ),
         compiler_params=PARAMS,
         name="project",
-    )(attention, weight)
+    )(here, attention, upper, in_hbm(low))
 
 
 def add_kernel(one_ref, two_ref, out_ref):
@@ -400,40 +521,43 @@
     place = placement[0]
     slots = place.shape[0]
     me = jnp.stack([lax.axis_index("xh"), lax.axis_index("core")]).astype(jnp.int32)
-
-    all_rows, mine, other = split_queries(me, q_step)
-    other = swap(other, ("core",))
+    here = jnp.concatenate([me, place])
+
+    other = swap(q_step, ("core",))
+    own = own_rows(here, q_step, slots)
+    routed = route(here, own, other, indices)
+    routed, prefix_k, prefix_v = lax.optimization_barrier((routed, prefix_k, prefix_v))
     k_other = swap(prefix_k, ("core",))
     v_other = swap(prefix_v, ("core",))
-    routed = route(me, place, mine, other, indices)
     arrived = lax.all_to_all(
         routed.reshape(indices * 2, 16, D), ("prompt", "xh"), split_axis=0, concat_axis=0, tiled=True
     )
-    pieces = suffix_attention(
-        me, lengths, all_rows, step_k, step_values, suffix_k, suffix_values
-    )
+    keep, to_core, to_xh = suffix_attention(
+        here, lengths, q_step, step_k, step_values, suffix_k, suffix_values
+    )
+    near = swap(to_core, ("core",))
+    far = swap(jnp.concatenate([to_xh, near[near.shape[0] // 2 :]], axis=0), ("xh",))
     parts = prefix_attention(
         arrived.reshape(indices, 2, 16, D), prefix_k, k_other, prefix_v, v_other
     )
-    pieces, parts = lax.optimization_barrier((pieces, parts))
     returned = lax.all_to_all(
         parts.reshape(indices * 2, 16, D), ("prompt", "xh"), split_axis=0, concat_axis=0, tiled=True
     )
-    pieces = [
-        pieces[0],
-        swap(pieces[1], ("core",)),
-        swap(pieces[2], ("xh",)),
-        swap(pieces[3], ("xh", "core")),
-    ]
-    weight_away, weight_mine = stage_weight(me, output_weight, parts, blocks)
+    upper, low_away, low_mine = stage_weight(here, output_weight, parts, blocks)
     columns = (place[:, None] * 4 + jnp.arange(tokens, dtype=jnp.int32)[None, :]).reshape(
         slots * tokens, 1
     )
     away, attention = merge_and_project(
-        me, place, columns, returned.reshape(indices, 2, 16, D), pieces, weight_away
+        here,
+        slots,
+        columns,
+        returned.reshape(indices, 2, 16, D),
+        (keep, near, far),
+        upper,
+        low_away,
     )
     away = swap(away, ("core",))
-    stay = project(attention, weight_mine)
+    stay = project(here, attention, upper, low_mine)
     spread = lax.all_to_all(
         add_halves(stay, away), ("tensor", "xh"), split_axis=0, concat_axis=0, tiled=True
     )

time: 69.2 us -> 67.4 us (0.974)
  local copies, waits for them, and re-layouts: 5.3 us -> 1.06 us
  waiting for transfers between devices: 4.09 us -> 6 us
  starting transfers between devices: 25.8 us -> 25 us
    unnamed x22 -> x8, local copies, waits for them, and re-layouts: 5.23 us -> 0.99 us
    all_to_all x1, waiting for transfers between devices: 0.01 us -> 2.38 us  [body(): lax.all_to_all(parts.reshape(indices * 2, 16, D), ('prompt', 'xh'), split...]
    ppermute x7 -> x6, starting transfers between devices: 10.5 us -> 8.99 us  [swap(): return lax.ppermute(value, axes, [(i, size - 1 - i) for i in range(size)])]
    all_to_all x1, starting transfers between devices: 6.01 us -> 6.75 us  [body(): lax.all_to_all(parts.reshape(indices * 2, 16, D), ('prompt', 'xh'), split...]
    concatenate x0 -> x2, other arithmetic: none -> 0.73 us  [the longest x1 0.73 us: body(): here = jnp.concatenate([me, place])]
  transfers between devices with their start and end apart: 9 -> 8, of which waited for: 2 -> 3; matrix products, arithmetic and copies ran while one was open for 0% -> 1% of each run, Pallas kernels for 19% -> 18%
where the time goes in v3:
time: 67.4 us; the launch traced here: 67 us
  starting transfers between devices  25 us (37%)
  Pallas kernels  17.5 us (26%)
  blocking collectives  16.4 us (24%)
  waiting for transfers between devices  6 us (9%)
  local copies, waits for them, and re-layouts  1.06 us (2%)
  other arithmetic  0.81 us (1%)
    all_to_all x1, blocking collectives, body(): lax.all_to_all(add_halves(stay, away), ('tensor', 'xh'), split_axis=0, co...  16.4 us
    all_to_all x1, starting transfers between devices, body(): lax.all_to_all(routed.reshape(indices * 2, 16, D), ('prompt', 'xh'), spli...  9.3 us
    ppermute x6, starting transfers between devices, swap(): return lax.ppermute(value, axes, [(i, size - 1 - i) for i in range(size)])  8.99 us
    all_to_all x1, starting transfers between devices, body(): lax.all_to_all(parts.reshape(indices * 2, 16, D), ('prompt', 'xh'), split...  6.75 us
    pallas_call x1, Pallas kernels, suffix_attention(): pl.pallas_call(suffix_kernel, in_specs=[SMEM_SPEC] + [HBM_SPEC] * 6, out_...  5.64 us
    pallas_call x1, Pallas kernels, stage_weight(): pl.pallas_call(stage_kernel, in_specs=[SMEM_SPEC, HBM_SPEC, pl.BlockSpec(...  3.08 us
    all_to_all x1, waiting for transfers between devices, body(): lax.all_to_all(routed.reshape(indices * 2, 16, D), ('prompt', 'xh'), spli...  2.69 us
    all_to_all x1, waiting for transfers between devices, body(): lax.all_to_all(parts.reshape(indices * 2, 16, D), ('prompt', 'xh'), split...  2.38 us
  transfers between devices with their start and end apart: 8, of which 3 were waited for; matrix products, arithmetic and copies ran while one was open for 1% of the time, Pallas kernels for 18%

profile of v3, /device:TPU:1, one launch (start us, length us, event | category | flops | bytes accessed | tf_op | source)
XLA Modules:
  0.0 67.0 jit_solution(6269281122917564222)
XLA Ops:
  0.0 3.2 %collective-permute-start = (bf16[8,2,1024]{2,1,0:T(2,128)(2,1)}, bf16[8,2,1024]{2,1,0:T(2,128)(2,1)S(1)}, u32[]{:S(2)}, u32[]{:S(2)}) collective-permute-start(bf16[8,2,1024]{2,1,0:T(2,128)(2,1)} %q_hbm.3), channel_id=1, source_target_pairs={{0,1},{1,0},{2,3},{3,2},{4,5},{5,4},{6,7},{7,6},{8,9},{9,8},{10,11... | collective-permute-start | bytes 98312 | tf_op jit(solution)/shard_map/ppermute | solution.py:503
  3.2 0.7 %pad_add_fusion.here_ref.me_ref = s32[34]{0:T(128)S(1)} fusion(s32[32]{0:T(128)} %bitcast.10, s32[1]{0:T(128)} %bitcast.1, s32[1]{0:T(128)} %bitcast), kind=kLoop, calls=%fused_computation.2 | loop fusion | flops 68 | bytes 272 | tf_op jit(solution)/shard_map/concatenate | solution.py:524
  4.0 1.3 %own_rows.1.own_ref = f32[32,8,128]{2,1,0:T(8,128)S(1)} custom-call(s32[34]{0:T(128)S(1)} %pad_add_fusion.here_ref.me_ref, bf16[8,2,1024]{2,1,0:T(2,128)(2,1)} %q_hbm.3), custom_call_target="tpu_custom_call" | custom-call | bytes 2097152 | tf_op jit(solution)/shard_map/own_rows/pallas_call | solution.py:86
  5.3 0.0 collective-permute-done.other_ref
  5.3 1.2 %route_queries.1 = bf16[16,2,16,128]{3,2,1,0:T(8,128)(2,1)} custom-call(s32[34]{0:T(128)S(1)} %pad_add_fusion.here_ref.me_ref, f32[32,8,128]{2,1,0:T(8,128)S(1)} %own_rows.1.own_ref, bf16[8,2,1024]{2,1,0:T(2,128)(2,1)S(1)} %collective-permute-done.other_ref), custom_call_target="tpu_custom_call" | custom-call | tf_op jit(solution)/shard_map/route_queries/pallas_call | solution.py:111
  6.5 0.0 collective-permute-start.1
  6.6 0.5 collective-permute-start.2
  7.1 9.3 %all-to-all-start = ((bf16[32,16,128]{2,1,0:T(8,128)(2,1)}), bf16[32,16,128]{2,1,0:T(8,128)(2,1)S(1)}, u32[]{:S(2)}, u32[]{:S(2)}) async-start(bf16[32,16,128]{2,1,0:T(8,128)(2,1)} %bitcast.3), calls=%async_computation | async-start | bytes 262144 | tf_op jit(solution)/shard_map/all_to_all | solution.py:532
  16.4 0.0 copy-start.3
  16.4 0.0 copy-start.1
  16.4 0.0 copy-start.2
  16.4 5.6 %suffix_attention.1 = (bf16[64,128]{1,0:T(8,128)(2,1)S(1)}, bf16[128,128]{1,0:T(8,128)(2,1)S(1)}, bf16[64,128]{1,0:T(8,128)(2,1)S(1)}) custom-call(s32[34]{0:T(128)S(1)} %pad_add_fusion.here_ref.me_ref, s32[8]{0:T(128)} %len_hbm.1, bf16[8,2,1024]{2,1,0:T(2,128)(2,1)} %q_hbm.3, bf16[8,2,128]{2,1,0:T(2,128)(2,1)} %sk_hbm.1, bf16[8,2,128]{2,1,0:T(2,128)(2,1)} %sv_hbm.1, ...), custom_call_target="tpu_custom_call" | custom-call | flops 1073741824 | bytes 8388608 | tf_op jit(solution)/shard_map/suffix_attention/pallas_call | solution.py:226
  22.1 0.4 collective-permute-start.3
  22.4 0.0 copy-done.3
  22.4 0.9 %collective-permute-done.3.near_ref = bf16[128,128]{1,0:T(8,128)(2,1)S(1)} collective-permute-done((bf16[128,128]{1,0:T(8,128)(2,1)S(1)}, bf16[128,128]{1,0:T(8,128)(2,1)S(1)}, u32[]{:S(2)}, u32[]{:S(2)}) %collective-permute-start.3) | collective-permute-done | bytes 32800 | tf_op jit(solution)/shard_map/ppermute | solution.py:503
  23.4 2.7 %all-to-all-done = bf16[32,16,128]{2,1,0:T(8,128)(2,1)S(1)} async-done(((bf16[32,16,128]{2,1,0:T(8,128)(2,1)}), bf16[32,16,128]{2,1,0:T(8,128)(2,1)S(1)}, u32[]{:S(2)}, u32[]{:S(2)}) %all-to-all-start) | async-done | bytes 131104 | tf_op jit(solution)/shard_map/all_to_all | solution.py:532
  26.0 0.0 collective-permute-done.1.k_other
  26.0 0.0 collective-permute-done.2.v_other
  26.1 0.0 copy-done.1
  26.1 0.0 copy-done.2
  26.1 1.9 %prefix_attention.1.after_ref = bf16[16,2,16,128]{3,2,1,0:T(8,128)(2,1)} custom-call(bf16[16,2,16,128]{3,2,1,0:T(8,128)(2,1)S(1)} %bitcast.9, bf16[2,1024,128]{2,1,0:T(8,128)(2,1)S(1)} %copy-done.1, bf16[2,1024,128]{2,1,0:T(8,128)(2,1)S(1)} %collective-permute-done.1.k_other, bf16[2,1024,128]{2,1,0:T(8,128)(2,1)S(1)} %copy-done.2, ...), custom_call_target="tpu_custom_call" | custom-call | tf_op jit(solution)/shard_map/prefix_attention/pallas_call | solution.py:295
  28.0 6.8 %all-to-all-start.1 = ((bf16[32,16,128]{2,1,0:T(8,128)(2,1)}), bf16[32,16,128]{2,1,0:T(8,128)(2,1)S(1)}, u32[]{:S(2)}, u32[]{:S(2)}) async-start(bf16[32,16,128]{2,1,0:T(8,128)(2,1)} %bitcast.5), calls=%async_computation.1 | async-start | bytes 262144 | tf_op jit(solution)/shard_map/all_to_all | solution.py:543
  34.7 2.8 %collective-permute-start.4 = (bf16[128,128]{1,0:T(8,128)(2,1)S(1)}, bf16[128,128]{1,0:T(8,128)(2,1)S(1)}, u32[]{:S(2)}, u32[]{:S(2)}) collective-permute-start(bf16[128,128]{1,0:T(8,128)(2,1)S(1)} %pad_maximum_fusion), channel_id=1, source_target_pairs={{0,2},{2,0},{1,3},{3,1},{4,6},{6,4},{5,7},{7,5},{8,10},{10,8},{9,1... | collective-permute-start | bytes 98312 | tf_op jit(solution)/shard_map/ppermute | solution.py:503
  37.6 0.1 iota_add_fusion
  37.6 0.1 add.27.col_ref
  37.7 3.1 %stage_weight.1 = (bf16[128,8192]{1,0:T(8,128)(2,1)S(1)}, bf16[8,128,512]{2,1,0:T(8,128)(2,1)S(1)}, bf16[8,128,512]{2,1,0:T(8,128)(2,1)S(1)}) custom-call(s32[34]{0:T(128)S(1)} %pad_add_fusion.here_ref.me_ref, bf16[256,8192]{1,0:T(8,128)(2,1)} %w_hbm.1, bf16[16,2,16,128]{3,2,1,0:T(8,128)(2,1)} %prefix_attention.1.after_ref), custom_call_target="tpu_custom_call" | custom-call | bytes 10485760 | tf_op jit(solution)/shard_map/stage_weight/pallas_call | solution.py:342
  40.8 0.0 copy-start
  40.8 1.0 %copy-done = bf16[8,128,512]{2,1,0:T(8,128)(2,1)} copy-done((bf16[8,128,512]{2,1,0:T(8,128)(2,1)}, bf16[8,128,512]{2,1,0:T(8,128)(2,1)S(1)}, u32[]{:S(2)}) %copy-start) | copy-done | bytes 1048600
  41.8 0.0 collective-permute-done.4.far_ref
  41.8 2.4 %all-to-all-done.1 = bf16[32,16,128]{2,1,0:T(8,128)(2,1)S(1)} async-done(((bf16[32,16,128]{2,1,0:T(8,128)(2,1)}), bf16[32,16,128]{2,1,0:T(8,128)(2,1)S(1)}, u32[]{:S(2)}, u32[]{:S(2)}) %all-to-all-start.1) | async-done | bytes 131104 | tf_op jit(solution)/shard_map/all_to_all | solution.py:543
  44.1 1.3 %merge_and_project.1 = (bf16[8,64,512]{2,1,0:T(8,128)(2,1)S(1)}, bf16[64,256]{1,0:T(8,128)(2,1)S(1)}) custom-call(s32[34]{0:T(128)S(1)} %pad_add_fusion.here_ref.me_ref, s32[64,1]{1,0:T(8,128)S(1)} %add.27.col_ref, bf16[16,2,16,128]{3,2,1,0:T(8,128)(2,1)S(1)} %bitcast.8, bf16[64,128]{1,0:T(8,128)(2,1)S(1)} %get-tuple-element.19.keep_ref, ...), custom_call_target="tpu_custom_call" | custom-call | tf_op jit(solution)/shard_map/merge_and_project/pallas_call | solution.py:418
  45.5 2.0 %collective-permute-start.5 = (bf16[8,64,512]{2,1,0:T(8,128)(2,1)S(1)}, bf16[8,64,512]{2,1,0:T(8,128)(2,1)S(1)}, u32[]{:S(2)}, u32[]{:S(2)}) collective-permute-start(bf16[8,64,512]{2,1,0:T(8,128)(2,1)S(1)} %get-tuple-element.26), channel_id=1, source_target_pairs={{0,1},{1,0},{2,3},{3,2},{4,5},{5,4},{6,7},{7,6},{8,9},{9,8},{10,11... | collective-permute-start | bytes 1572872 | tf_op jit(solution)/shard_map/ppermute | solution.py:503
  47.5 2.2 %project.1.one_ref = f32[8,64,512]{2,1,0:T(8,128)S(1)} custom-call(s32[34]{0:T(128)S(1)} %pad_add_fusion.here_ref.me_ref, bf16[64,256]{1,0:T(8,128)(2,1)S(1)} %get-tuple-element.24.att_ref, bf16[128,8192]{1,0:T(8,128)(2,1)S(1)} %get-tuple-element.22.upper_ref, bf16[8,128,512]{2,1,0:T(8,128)(2,1)} %copy-done), custom_call_target="tpu_custom_call" | custom-call | flops 1073741824 | bytes 2097152 | tf_op jit(solution)/shard_map/project/pallas_call | solution.py:451
  49.8 0.0 collective-permute-done.5.two_ref
  49.8 0.1 add_halves.1
  49.9 16.4 %all_to_all.15.in_ref = bf16[8,64,512]{2,1,0:T(8,128)(2,1)S(1)} all-to-all(bf16[8,64,512]{2,1,0:T(8,128)(2,1)S(1)} %add_halves.1), channel_id=1, replica_groups=mesh['tensor'=4,'prompt'=16,'xh'=2,'core'=2] {'tensor','xh'}, dimensions={0} | all-to-all | bytes 1048576 | tf_op jit(solution)/shard_map/all_to_all | solution.py:561
  66.3 0.7 %sum_shares.1 = bf16[32,2,512]{2,1,0:T(2,128)(2,1)} custom-call(bf16[8,64,512]{2,1,0:T(8,128)(2,1)S(1)} %all_to_all.15.in_ref), custom_call_target="tpu_custom_call" | custom-call | tf_op jit(solution)/shard_map/sum_shares/pallas_call | solution.py:491
  (3 shorter events, 0.0 us)
Async XLA Ops:
  0.0 5.3 %collective-permute-start = (bf16[8,2,1024]{2,1,0:T(2,128)(2,1)}, bf16[8,2,1024]{2,1,0:T(2,128)(2,1)S(1)}, u32[]{:S(2)}, u32[]{:S(2)}) collective-permute-start(bf16[8,2,1024]{2,1,0:T(2,128)(2,1)} %q_hbm.3), channel_id=1, source_target_pairs={{0,1},{1,0},{2,3},{3,2},{4,5},{5,4},{6,7},{7,6},{8,9},{9,8},{10,11... | collective-permute-start | bytes 98312 | tf_op jit(solution)/shard_map/ppermute | solution.py:503
  6.5 19.5 %collective-permute-start.1 = (bf16[2,1024,128]{2,1,0:T(8,128)(2,1)}, bf16[2,1024,128]{2,1,0:T(8,128)(2,1)S(1)}, u32[]{:S(2)}, u32[]{:S(2)}) collective-permute-start(bf16[2,1024,128]{2,1,0:T(8,128)(2,1)} %k_own), channel_id=1, source_target_pairs={{0,1},{1,0},{2,3},{3,2},{4,5},{5,4},{6,7},{7,6},{8,9},{9,8},{10,11... | collective-permute-start | bytes 1572872 | tf_op jit(solution)/shard_map/ppermute | solution.py:503
  6.6 19.5 %collective-permute-start.2 = (bf16[2,1024,128]{2,1,0:T(8,128)(2,1)}, bf16[2,1024,128]{2,1,0:T(8,128)(2,1)S(1)}, u32[]{:S(2)}, u32[]{:S(2)}) collective-permute-start(bf16[2,1024,128]{2,1,0:T(8,128)(2,1)} %v_own), channel_id=1, source_target_pairs={{0,1},{1,0},{2,3},{3,2},{4,5},{5,4},{6,7},{7,6},{8,9},{9,8},{10,11... | collective-permute-start | bytes 1572872 | tf_op jit(solution)/shard_map/ppermute | solution.py:503
  7.1 19.0 %all-to-all-start = ((bf16[32,16,128]{2,1,0:T(8,128)(2,1)}), bf16[32,16,128]{2,1,0:T(8,128)(2,1)S(1)}, u32[]{:S(2)}, u32[]{:S(2)}) async-start(bf16[32,16,128]{2,1,0:T(8,128)(2,1)} %bitcast.3), calls=%async_computation | async-start | bytes 262144 | tf_op jit(solution)/shard_map/all_to_all | solution.py:532
  16.4 6.1 %copy-start.3 = (s32[1,32]{1,0:T(1,128)S(1)}, s32[1,32]{1,0:T(1,128)}, u32[]{:S(2)}) copy-start(s32[1,32]{1,0:T(1,128)} %param.18) | copy-start | bytes 388
  16.4 9.7 %copy-start.1 = (bf16[2,1024,128]{2,1,0:T(8,128)(2,1)S(1)}, bf16[2,1024,128]{2,1,0:T(8,128)(2,1)}, u32[]{:S(2)}) copy-start(bf16[2,1024,128]{2,1,0:T(8,128)(2,1)} %k_own) | copy-start | bytes 1572868
  16.4 9.7 %copy-start.2 = (bf16[2,1024,128]{2,1,0:T(8,128)(2,1)S(1)}, bf16[2,1024,128]{2,1,0:T(8,128)(2,1)}, u32[]{:S(2)}) copy-start(bf16[2,1024,128]{2,1,0:T(8,128)(2,1)} %v_own) | copy-start | bytes 1572868
  22.1 1.3 %collective-permute-start.3 = (bf16[128,128]{1,0:T(8,128)(2,1)S(1)}, bf16[128,128]{1,0:T(8,128)(2,1)S(1)}, u32[]{:S(2)}, u32[]{:S(2)}) collective-permute-start(bf16[128,128]{1,0:T(8,128)(2,1)S(1)} %get-tuple-element.20), channel_id=1, source_target_pairs={{0,1},{1,0},{2,3},{3,2},{4,5},{5,4},{6,7},{7,6},{8,9},{9,8},{10,11... | collective-permute-start | bytes 98312 | tf_op jit(solution)/shard_map/ppermute | solution.py:503
  28.0 16.2 %all-to-all-start.1 = ((bf16[32,16,128]{2,1,0:T(8,128)(2,1)}), bf16[32,16,128]{2,1,0:T(8,128)(2,1)S(1)}, u32[]{:S(2)}, u32[]{:S(2)}) async-start(bf16[32,16,128]{2,1,0:T(8,128)(2,1)} %bitcast.5), calls=%async_computation.1 | async-start | bytes 262144 | tf_op jit(solution)/shard_map/all_to_all | solution.py:543
  34.7 7.0 %collective-permute-start.4 = (bf16[128,128]{1,0:T(8,128)(2,1)S(1)}, bf16[128,128]{1,0:T(8,128)(2,1)S(1)}, u32[]{:S(2)}, u32[]{:S(2)}) collective-permute-start(bf16[128,128]{1,0:T(8,128)(2,1)S(1)} %pad_maximum_fusion), channel_id=1, source_target_pairs={{0,2},{2,0},{1,3},{3,1},{4,6},{6,4},{5,7},{7,5},{8,10},{10,8},{9,1... | collective-permute-start | bytes 98312 | tf_op jit(solution)/shard_map/ppermute | solution.py:503
  40.8 1.0 %copy-start = (bf16[8,128,512]{2,1,0:T(8,128)(2,1)}, bf16[8,128,512]{2,1,0:T(8,128)(2,1)S(1)}, u32[]{:S(2)}) copy-start(bf16[8,128,512]{2,1,0:T(8,128)(2,1)S(1)} %get-tuple-element.25.low_hbm) | copy-start | bytes 3145732
  45.5 4.3 %collective-permute-start.5 = (bf16[8,64,512]{2,1,0:T(8,128)(2,1)S(1)}, bf16[8,64,512]{2,1,0:T(8,128)(2,1)S(1)}, u32[]{:S(2)}, u32[]{:S(2)}) collective-permute-start(bf16[8,64,512]{2,1,0:T(8,128)(2,1)S(1)} %get-tuple-element.26), channel_id=1, source_target_pairs={{0,1},{1,0},{2,3},{3,2},{4,5},{5,4},{6,7},{7,6},{8,9},{9,8},{10,11... | collective-permute-start | bytes 1572872 | tf_op jit(solution)/shard_map/ppermute | solution.py:503

commit v4 on v3

--- a/solution.py
+++ b/solution.py
@@ -61,10 +61,10 @@
             rows[(h // 2) % 2, i, place : place + tokens, :] = wide[:, h * D : (h + 1) * D]
 
 
-def scatter_rows(q_ref, here_ref, rows, first, core):
+def scatter_rows(q_ref, place_ref, rows, first, core):
     count, tokens, _ = q_ref.shape
     for i in range(count):
-        u = here_ref[2 + first + i]
+        u = place_ref[0, first + i]
         wide = q_ref[i].astype(F32)
         for j in range(4):
             h = 4 * (j // 2) + j % 2
@@ -73,50 +73,63 @@
             rows[u, j * tokens : (j + 1) * tokens, :] = jnp.where(core == 0, one, two)
 
 
-def own_kernel(here_ref, q_hbm, rows, mine_ref, sem):
-    xh, core = here_ref[0], here_ref[1]
-    copy = pltpu.make_async_copy(q_hbm, mine_ref, sem)
-    copy.start()
+def own_kernel(me_ref, place_hbm, q_hbm, rows, place_out, place_ref, mine_ref, sem):
+    xh, core = me_ref[0], me_ref[1]
+    copies = (
+        pltpu.make_async_copy(place_hbm, place_ref, sem.at[0]),
+        pltpu.make_async_copy(q_hbm, mine_ref, sem.at[1]),
+        pltpu.make_async_copy(place_hbm, place_out, sem.at[2]),
+    )
+    for copy in copies:
+        copy.start()
     rows[...] = jnp.zeros_like(rows)
-    copy.wait()
-    scatter_rows(mine_ref, here_ref, rows, (2 * xh + core) * q_hbm.shape[0], core)
-
-
-def own_rows(here, mine, slots):
+    for copy in copies:
+        copy.wait()
+    scatter_rows(mine_ref, place_ref, rows, (2 * xh + core) * q_hbm.shape[0], core)
+
+
+def own_rows(me, placement, mine):
     return pl.pallas_call(
         own_kernel,
-        in_specs=[SMEM_SPEC, HBM_SPEC],
-        out_specs=VMEM_SPEC,
-        out_shape=jax.ShapeDtypeStruct((slots, 8, D), F32),
-        scratch_shapes=[pltpu.VMEM(mine.shape, BF16), pltpu.SemaphoreType.DMA],
+        in_specs=[SMEM_SPEC, HBM_SPEC, HBM_SPEC],
+        out_specs=[VMEM_SPEC, VMEM_SPEC],
+        out_shape=[
+            jax.ShapeDtypeStruct((placement.shape[1], 8, D), F32),
+            jax.ShapeDtypeStruct(placement.shape, jnp.int32),
+        ],
+        scratch_shapes=[
+            pltpu.SMEM(placement.shape, jnp.int32),
+            pltpu.VMEM(mine.shape, BF16),
+            pltpu.SemaphoreType.DMA((3,)),
+        ],
         cost_estimate=pl.CostEstimate(
             flops=0, bytes_accessed=2 * 1024 * 1024, transcendentals=0
         ),
         compiler_params=PARAMS,
         name="own_rows",
-    )(here, in_hbm(mine))
-
-
-def route_kernel(here_ref, own_ref, other_ref, out_ref, rows):
-    xh, core = here_ref[0], here_ref[1]
+    )(me, in_hbm(placement), in_hbm(mine))
+
+
+def route_kernel(me_ref, place_ref, own_ref, other_ref, out_ref, rows):
+    xh, core = me_ref[0], me_ref[1]
     rows[...] = own_ref[...]
     first = (2 * xh + 1 - core) * other_ref.shape[0]
-    scatter_rows(other_ref, here_ref, rows, first, core)
+    scatter_rows(other_ref, place_ref, rows, first, core)
     packed = rows[...].reshape(out_ref.shape[0], 16, D).astype(BF16)
     for j in range(out_ref.shape[1]):
         out_ref[:, j] = packed
 
 
-def route(here, own, other, indices):
+def route(me, placement, own, other, indices):
     return pl.pallas_call(
         route_kernel,
-        in_specs=[SMEM_SPEC, VMEM_SPEC, VMEM_SPEC],
+        in_specs=[SMEM_SPEC, SMEM_SPEC, VMEM_SPEC, VMEM_SPEC],
         out_specs=VMEM_SPEC,
         out_shape=jax.ShapeDtypeStruct((indices, 2, 16, D), BF16),
         scratch_shapes=[pltpu.VMEM(own.shape, F32)],
         compiler_params=PARAMS,
         name="route_queries",
-    )(here, own, other)
+    )(me, placement, own, other)
 
 
 def suffix_kernel(me_ref, len_hbm, q_hbm, sk_hbm, sv_hbm, k_hbm, v_hbm, *rest):
@@ -261,24 +274,25 @@
 def prefix_kernel(q_ref, k_own, k_other, v_own, v_other, out_ref):
     indices = q_ref.shape[0]
     q_both = q_ref[:, 0].astype(F32) + q_ref[:, 1].astype(F32)
-    pair = []
-    for u in range(2):
-        q = q_both[:, u * 8 : u * 8 + 8].reshape(indices * 8, D).astype(BF16)
-        scores = [dot_t(q, k[u]) * SCALE2 for k in (k_own, k_other)]
-        top = jnp.maximum(
-            jnp.max(scores[0], axis=1, keepdims=True), jnp.max(scores[1], axis=1, keepdims=True)
+    q = [q_both[:, u * 8 : u * 8 + 8].reshape(indices * 8, D).astype(BF16) for u in range(2)]
+    scores = [[dot_t(q[u], k[u]) * SCALE2 for k in (k_own, k_other)] for u in range(2)]
+    top = [
+        jnp.maximum(jnp.max(one, axis=1, keepdims=True), jnp.max(two, axis=1, keepdims=True))
+        for one, two in scores
+    ]
+    weights = [[jnp.exp2(part - top[u]) for part in scores[u]] for u in range(2)]
+    total = [sum(jnp.sum(part, axis=1, keepdims=True) for part in weights[u]) for u in range(2)]
+    numer = [
+        sum(dot(part.astype(BF16), v[u]) for part, v in zip(weights[u], (v_own, v_other)))
+        for u in range(2)
+    ]
+    pair = [
+        (
+            (numer[u] / total[u]).reshape(indices, 8, D),
+            split_stat(top[u] + jnp.log2(total[u])).reshape(indices, 8, D),
         )
-        weights = [jnp.exp2(part - top) for part in scores]
-        total = sum(jnp.sum(part, axis=1, keepdims=True) for part in weights)
-        numer = sum(
-            dot(part.astype(BF16), v[u]) for part, v in zip(weights, (v_own, v_other))
-        )
-        pair.append(
-            (
-                (numer / total).reshape(indices, 8, D),
-                split_stat(top + jnp.log2(total)).reshape(indices, 8, D),
-            )
-        )
+        for u in range(2)
+    ]
     lower = lower_rows((indices, 8, D))
     for j in range(2):
         halves = []
@@ -314,9 +328,9 @@
     ]
 
 
-def stage_kernel(here_ref, w_hbm, after_ref, upper_ref, low_ref, mine_hbm, mine_ref, *sems):
+def stage_kernel(me_ref, w_hbm, after_ref, upper_ref, low_ref, mine_hbm, mine_ref, *sems):
     upper_sem, low_sem, mine_sem, out_sem = sems
-    core = here_ref[1]
+    core = me_ref[1]
     chunk = upper_ref.shape[0] // CHUNKS
     mine = low_copies(w_hbm, mine_ref, mine_sem, core)
     copies = low_copies(w_hbm, low_ref, low_sem, 1 - core)
@@ -336,7 +350,7 @@
         copy.wait()
 
 
-def stage_weight(here, weight, after, blocks):
+def stage_weight(me, weight, after, blocks):
     depth, width = weight.shape
     low = (blocks, depth // 2, width // (2 * blocks))
     return pl.pallas_call(
@@ -346,7 +360,7 @@
         out_shape=[
             jax.ShapeDtypeStruct((depth // 2, width), BF16),
             jax.ShapeDtypeStruct(low, BF16),
-            jax.ShapeDtypeStruct(low, BF16),
+            pltpu.HBM(low, BF16),
         ],
         scratch_shapes=[
             pltpu.VMEM(low, BF16),
@@ -360,20 +374,16 @@
         ),
         compiler_params=PARAMS,
         name="stage_weight",
-    )(here, in_hbm(weight), after)
+    )(me, in_hbm(weight), after)
 
 
 def block_columns(block, width):
     return pl.ds(pl.multiple_of(block * width, width), width)
 
 
-def merge_kernel(
-    here_ref, col_ref, parts_ref, keep_ref, near_ref, far_ref, upper_ref, low_ref, *rest
-):
-    out_ref, att_ref, own = rest
-    xh, core = here_ref[0], here_ref[1]
-    blocks, out_rows, width = out_ref.shape
-    owners = parts_ref.shape[0]
+def collect_kernel(me_ref, place_ref, keep_ref, near_ref, far_ref, value_ref, level_ref, own):
+    xh, core = me_ref[0], me_ref[1]
+    owners = value_ref.shape[0]
     count = keep_ref.shape[0] // 8
     pieces = ((keep_ref, 0, xh, core), (near_ref, 0, xh, 1 - core))
     pieces += ((far_ref, 0, 1 - xh, core), (far_ref, count, 1 - xh, 1 - core))
@@ -381,16 +391,43 @@
         value = ref[start * 8 : (start + count) * 8, :].astype(F32)
         for i in range(count):
             slot = (2 * from_xh + from_core) * count + i
-            own[here_ref[2 + slot]] = value[i * 8 : (i + 1) * 8]
+            own[place_ref[0, slot]] = value[i * 8 : (i + 1) * 8]
     lower = lower_rows((owners, 8, D))
     both = own[...].reshape(owners, 2, 8, D)
     one, two = both[:, 0], both[:, 1]
-    values = [jnp.where(lower, one, pltpu.roll(two, 4, 1))]
-    levels = [join_stat(jnp.where(lower, pltpu.roll(one, 4, 1), two))]
+    value_ref[...] = jnp.where(lower, one, pltpu.roll(two, 4, 1))
+    level = join_stat(jnp.where(lower, pltpu.roll(one, 4, 1), two))
+    level_ref[...] = jnp.broadcast_to(level, level_ref.shape)
+
+
+def collect_suffix(me, placement, pieces, owners):
+    part = jax.ShapeDtypeStruct((owners, 8, D), F32)
+    return pl.pallas_call(
+        collect_kernel,
+        in_specs=[SMEM_SPEC] * 2 + [VMEM_SPEC] * 3,
+        out_specs=[VMEM_SPEC] * 2,
+        out_shape=[part, part],
+        scratch_shapes=[pltpu.VMEM((placement.shape[1], 8, D), F32)],
+        cost_estimate=pl.CostEstimate(
+            flops=0, bytes_accessed=1024 * 1024, transcendentals=0
+        ),
+        compiler_params=PARAMS,
+        name="collect_suffix",
+    )(me, placement, *pieces)
+
+
+def merge_kernel(
+    me_ref, col_ref, parts_ref, value_ref, level_ref, upper_ref, low_ref, out_ref, att_ref
+):
+    core = me_ref[1]
+    blocks, out_rows, width = out_ref.shape
+    owners = parts_ref.shape[0]
+    values = [value_ref[...]]
+    levels = [level_ref[...]]
     for c in range(parts_ref.shape[1]):
         block = parts_ref[:, c].astype(F32)
         values.append(block[:, 0:8])
-        levels.append(join_stat(block[:, 8:16]))
+        levels.append(jnp.broadcast_to(join_stat(block[:, 8:16]), level_ref.shape))
     top = levels[0]
     for level in levels[1:]:
         top = jnp.maximum(top, level)
@@ -412,24 +449,23 @@
         out_ref[b] = (value + dot(att_ref[:, half:], low_ref[b])).astype(BF16)
 
 
-def merge_and_project(here, slots, columns, parts, pieces, upper, low):
+def merge_and_project(me, columns, parts, suffix, upper, low):
     blocks, half, width = low.shape
     out_rows = columns.shape[0]
     return pl.pallas_call(
         merge_kernel,
-        in_specs=[SMEM_SPEC] + [VMEM_SPEC] * 7,
+        in_specs=[SMEM_SPEC] + [VMEM_SPEC] * 6,
         out_specs=[VMEM_SPEC, VMEM_SPEC],
         out_shape=[
             jax.ShapeDtypeStruct((blocks, out_rows, width), BF16),
             jax.ShapeDtypeStruct((out_rows, 2 * half), BF16),
         ],
-        scratch_shapes=[pltpu.VMEM((slots, 8, D), F32)],
         compiler_params=PARAMS,
         name="merge_and_project",
-    )(here, columns, parts, *pieces, upper, low)
-
-
-def project_kernel(here_ref, att_ref, upper_ref, low_hbm, out_ref, low_ref, sem):
+    )(me, columns, parts, *suffix, upper, low)
+
+
+def project_kernel(me_ref, att_ref, upper_ref, low_hbm, out_ref, low_ref, sem):
     blocks, half, width = low_ref.shape
     copies = [
         pltpu.make_async_copy(low_hbm.at[b], low_ref.at[b], sem.at[b]) for b in range(blocks)
@@ -437,7 +473,7 @@
     for copy in copies:
         copy.start()
     for b in range(blocks):
-        columns = block_columns(2 * b + here_ref[1], width)
+        columns = block_columns(2 * b + me_ref[1], width)
         out_ref[b] = dot(att_ref[:, 0:half], upper_ref[:, columns])
     for copy in copies:
         copy.wait()
@@ -445,7 +481,7 @@
         out_ref[b] += dot(att_ref[:, half:], low_ref[b])
 
 
-def project(here, attention, upper, low):
+def project(me, attention, upper, low):
     blocks, half, width = low.shape
     out_rows = attention.shape[0]
     return pl.pallas_call(
@@ -461,7 +497,7 @@
         ),
         compiler_params=PARAMS,
         name="project",
-    )(here, attention, upper, in_hbm(low))
+    )(me, attention, upper, in_hbm(low))
 
 
 def add_kernel(one_ref, two_ref, out_ref):
@@ -521,11 +557,9 @@
     place = placement[0]
     slots = place.shape[0]
     me = jnp.stack([lax.axis_index("xh"), lax.axis_index("core")]).astype(jnp.int32)
-    here = jnp.concatenate([me, place])
-
     other = swap(q_step, ("core",))
-    own = own_rows(here, q_step, slots)
-    routed = route(here, own, other, indices)
+    own, place_here = own_rows(me, placement, q_step)
+    routed = route(me, place_here, own, other, indices)
     routed, prefix_k, prefix_v = lax.optimization_barrier((routed, prefix_k, prefix_v))
     k_other = swap(prefix_k, ("core",))
     v_other = swap(prefix_v, ("core",))
@@ -533,31 +567,31 @@
         routed.reshape(indices * 2, 16, D), ("prompt", "xh"), split_axis=0, concat_axis=0, tiled=True
     )
     keep, to_core, to_xh = suffix_attention(
-        here, lengths, q_step, step_k, step_values, suffix_k, suffix_values
+        me, lengths, q_step, step_k, step_values, suffix_k, suffix_values
     )
     near = swap(to_core, ("core",))
-    far = swap(jnp.concatenate([to_xh, near[near.shape[0] // 2 :]], axis=0), ("xh",))
     parts = prefix_attention(
         arrived.reshape(indices, 2, 16, D), prefix_k, k_other, prefix_v, v_other
     )
+    near, parts = lax.optimization_barrier((near, parts))
+    far = swap(jnp.concatenate([to_xh, near[near.shape[0] // 2 :]], axis=0), ("xh",))
     returned = lax.all_to_all(
         parts.reshape(indices * 2, 16, D), ("prompt", "xh"), split_axis=0, concat_axis=0, tiled=True
     )
-    upper, low_away, low_mine = stage_weight(here, output_weight, parts, blocks)
+    upper, low_away, low_mine = stage_weight(me, output_weight, parts, blocks)
     columns = (place[:, None] * 4 + jnp.arange(tokens, dtype=jnp.int32)[None, :]).reshape(
         slots * tokens, 1
     )
     away, attention = merge_and_project(
-        here,
-        slots,
+        me,
         columns,
         returned.reshape(indices, 2, 16, D),
-        (keep, near, far),
+        collect_suffix(me, place_here, (keep, near, far), indices),
         upper,
         low_away,
     )
     away = swap(away, ("core",))
-    stay = project(here, attention, upper, low_mine)
+    stay = project(me, attention, upper, low_mine)
     spread = lax.all_to_all(
         add_halves(stay, away), ("tensor", "xh"), split_axis=0, concat_axis=0, tiled=True
     )

time: 67.4 us -> 65.7 us (0.975)
  Pallas kernels: 17.5 us -> 18.7 us
  starting transfers between devices: 25 us -> 23.9 us
  local copies, waits for them, and re-layouts: 1.06 us -> 0.1 us
    unnamed x8 -> x6, local copies, waits for them, and re-layouts: 0.99 us -> 0.02 us
    all_to_all x1, waiting for transfers between devices: 2.69 us -> 3.62 us  [body(): lax.all_to_all(routed.reshape(indices * 2, 16, D), ('prompt', 'xh'), spli...]
    ppermute x6, waiting for transfers between devices: 0.93 us -> 0.02 us  [swap(): return lax.ppermute(value, axes, [(i, size - 1 - i) for i in range(size)])]
    all_to_all x1, starting transfers between devices: 6.75 us -> 5.9 us  [body(): lax.all_to_all(parts.reshape(indices * 2, 16, D), ('prompt', 'xh'), split...]
    concatenate x1 -> x0, other arithmetic: 0.73 us -> none  [body(): here = jnp.concatenate([me, place])]
    pallas_call x3 -> x4, Pallas kernels: 3.9 us -> 4.6 us  [the longest x1 1.34 us: own_rows(): pl.pallas_call(own_kernel, in_specs=[SMEM_SPEC, HBM_SPEC, HBM_SPEC], out_...]
  transfers between devices with their start and end apart: 8 -> 8, of which waited for: 3 -> 2; matrix products, arithmetic and copies ran while one was open for 1% -> 0% of each run, Pallas kernels for 18% -> 24%
where the time goes in v4:
time: 65.7 us; the launch traced here: 65.3 us
  starting transfers between devices  23.9 us (36%)
  Pallas kernels  18.7 us (28%)
  blocking collectives  16.5 us (25%)
  waiting for transfers between devices  5.82 us (9%)
    all_to_all x1, blocking collectives, body(): lax.all_to_all(add_halves(stay, away), ('tensor', 'xh'), split_axis=0, co...  16.5 us
    all_to_all x1, starting transfers between devices, body(): lax.all_to_all(routed.reshape(indices * 2, 16, D), ('prompt', 'xh'), spli...  9.3 us
    ppermute x6, starting transfers between devices, swap(): return lax.ppermute(value, axes, [(i, size - 1 - i) for i in range(size)])  8.73 us
    all_to_all x1, starting transfers between devices, body(): lax.all_to_all(parts.reshape(indices * 2, 16, D), ('prompt', 'xh'), split...  5.9 us
    pallas_call x1, Pallas kernels, suffix_attention(): pl.pallas_call(suffix_kernel, in_specs=[SMEM_SPEC] + [HBM_SPEC] * 6, out_...  5.64 us
    pallas_call x1, Pallas kernels, stage_weight(): pl.pallas_call(stage_kernel, in_specs=[SMEM_SPEC, HBM_SPEC, pl.BlockSpec(...  3.71 us
    all_to_all x1, waiting for transfers between devices, body(): lax.all_to_all(routed.reshape(indices * 2, 16, D), ('prompt', 'xh'), spli...  3.62 us
    pallas_call x1, Pallas kernels, project(): pl.pallas_call(project_kernel, in_specs=[SMEM_SPEC, VMEM_SPEC, VMEM_SPEC,...  2.21 us
  transfers between devices with their start and end apart: 8, of which 2 were waited for; matrix products, arithmetic and copies ran while one was open for 0% of the time, Pallas kernels for 24%

profile of v4, /device:TPU:1, one launch (start us, length us, event | category | flops | bytes accessed | tf_op | source)
XLA Modules:
  0.0 65.3 jit_solution(14738484993613879006)
XLA Ops:
  0.0 3.2 %collective-permute-start.1 = (bf16[8,2,1024]{2,1,0:T(2,128)(2,1)}, bf16[8,2,1024]{2,1,0:T(2,128)(2,1)S(1)}, u32[]{:S(2)}, u32[]{:S(2)}) collective-permute-start(bf16[8,2,1024]{2,1,0:T(2,128)(2,1)} %q_hbm.3), channel_id=1, source_target_pairs={{0,1},{1,0},{2,3},{3,2},{4,5},{5,4},{6,7},{7,6},{8,9},{9,8},{10,11... | collective-permute-start | bytes 98312 | tf_op jit(solution)/shard_map/ppermute | solution.py:539
  3.2 0.1 pad_add_fusion.me_ref
  3.3 1.3 %own_rows.1 = (f32[32,8,128]{2,1,0:T(8,128)S(1)}, s32[1,32]{1,0:T(1,128)S(1)}) custom-call(s32[2]{0:T(128)S(1)} %pad_add_fusion.me_ref, s32[1,32]{1,0:T(1,128)} %place_hbm.1, bf16[8,2,1024]{2,1,0:T(2,128)(2,1)} %q_hbm.3), custom_call_target="tpu_custom_call" | custom-call | bytes 2097152 | tf_op jit(solution)/shard_map/own_rows/pallas_call | solution.py:92
  4.7 0.0 collective-permute-done.1.other_ref
  4.7 1.2 %route_queries.1 = bf16[16,2,16,128]{3,2,1,0:T(8,128)(2,1)} custom-call(s32[2]{0:T(128)S(1)} %pad_add_fusion.me_ref, s32[1,32]{1,0:T(1,128)S(1)} %get-tuple-element.23.place_ref, f32[32,8,128]{2,1,0:T(8,128)S(1)} %get-tuple-element.24.own_ref, bf16[8,2,1024]{2,1,0:T(2,128)(2,1)S(1)} %collective-permute-done.1.other_ref), custom_call_target="tpu_custom_call" | custom-call | tf_op jit(solution)/shard_map/route_queries/pallas_call | solution.py:124
  5.9 0.0 collective-permute-start.2
  5.9 0.5 collective-permute-start.3
  6.4 9.3 %all-to-all-start = ((bf16[32,16,128]{2,1,0:T(8,128)(2,1)}), bf16[32,16,128]{2,1,0:T(8,128)(2,1)S(1)}, u32[]{:S(2)}, u32[]{:S(2)}) async-start(bf16[32,16,128]{2,1,0:T(8,128)(2,1)} %bitcast.3), calls=%async_computation | async-start | bytes 262144 | tf_op jit(solution)/shard_map/all_to_all | solution.py:566
  15.7 0.0 copy-start.2
  15.7 0.0 copy-start
  15.8 0.0 copy-start.1
  15.8 5.6 %suffix_attention.1 = (bf16[64,128]{1,0:T(8,128)(2,1)S(1)}, bf16[128,128]{1,0:T(8,128)(2,1)S(1)}, bf16[64,128]{1,0:T(8,128)(2,1)S(1)}) custom-call(s32[2]{0:T(128)S(1)} %pad_add_fusion.me_ref, s32[8]{0:T(128)} %len_hbm.1, bf16[8,2,1024]{2,1,0:T(2,128)(2,1)} %q_hbm.3, bf16[8,2,128]{2,1,0:T(2,128)(2,1)} %sk_hbm.1, bf16[8,2,128]{2,1,0:T(2,128)(2,1)} %sv_hbm.1, ...), custom_call_target="tpu_custom_call" | custom-call | flops 1073741824 | bytes 8388608 | tf_op jit(solution)/shard_map/suffix_attention/pallas_call | solution.py:239
  21.4 0.4 collective-permute-start
  21.8 0.0 copy-done.2
  21.8 3.6 %all-to-all-done = bf16[32,16,128]{2,1,0:T(8,128)(2,1)S(1)} async-done(((bf16[32,16,128]{2,1,0:T(8,128)(2,1)}), bf16[32,16,128]{2,1,0:T(8,128)(2,1)S(1)}, u32[]{:S(2)}, u32[]{:S(2)}) %all-to-all-start) | async-done | bytes 131104 | tf_op jit(solution)/shard_map/all_to_all | solution.py:566
  25.4 0.0 collective-permute-done.2.k_other
  25.4 0.0 collective-permute-done.3.v_other
  25.4 0.0 copy-done
  25.4 0.0 copy-done.1
  25.4 1.7 %prefix_attention.1.after_ref = bf16[16,2,16,128]{3,2,1,0:T(8,128)(2,1)} custom-call(bf16[16,2,16,128]{3,2,1,0:T(8,128)(2,1)S(1)} %bitcast.9, bf16[2,1024,128]{2,1,0:T(8,128)(2,1)S(1)} %copy-done, bf16[2,1024,128]{2,1,0:T(8,128)(2,1)S(1)} %collective-permute-done.2.k_other, bf16[2,1024,128]{2,1,0:T(8,128)(2,1)S(1)} %copy-done.1, ...), custom_call_target="tpu_custom_call" | custom-call | tf_op jit(solution)/shard_map/prefix_attention/pallas_call | solution.py:309
  27.1 0.0 collective-permute-done.near_ref
  27.1 5.9 %all-to-all-start.1 = ((bf16[32,16,128]{2,1,0:T(8,128)(2,1)}), bf16[32,16,128]{2,1,0:T(8,128)(2,1)S(1)}, u32[]{:S(2)}, u32[]{:S(2)}) async-start(bf16[32,16,128]{2,1,0:T(8,128)(2,1)} %bitcast.5), calls=%async_computation.1 | async-start | bytes 262144 | tf_op jit(solution)/shard_map/all_to_all | solution.py:578
  33.1 2.8 %collective-permute-start.4 = (bf16[128,128]{1,0:T(8,128)(2,1)S(1)}, bf16[128,128]{1,0:T(8,128)(2,1)S(1)}, u32[]{:S(2)}, u32[]{:S(2)}) collective-permute-start(bf16[128,128]{1,0:T(8,128)(2,1)S(1)} %pad_maximum_fusion), channel_id=1, source_target_pairs={{0,2},{2,0},{1,3},{3,1},{4,6},{6,4},{5,7},{7,5},{8,10},{10,8},{9,1... | collective-permute-start | bytes 98312 | tf_op jit(solution)/shard_map/ppermute | solution.py:539
  35.9 0.1 iota_add_fusion
  36.0 0.1 add.27.col_ref
  36.0 3.7 %stage_weight.1 = (bf16[128,8192]{1,0:T(8,128)(2,1)S(1)}, bf16[8,128,512]{2,1,0:T(8,128)(2,1)S(1)}, bf16[8,128,512]{2,1,0:T(8,128)(2,1)}) custom-call(s32[2]{0:T(128)S(1)} %pad_add_fusion.me_ref, bf16[256,8192]{1,0:T(8,128)(2,1)} %w_hbm.1, bf16[16,2,16,128]{3,2,1,0:T(8,128)(2,1)} %prefix_attention.1.after_ref), custom_call_target="tpu_custom_call" | custom-call | bytes 10485760 | tf_op jit(solution)/shard_map/stage_weight/pallas_call | solution.py:356
  39.8 0.0 collective-permute-done.4.far_ref
  39.8 0.8 %collect_suffix.1 = (f32[16,8,128]{2,1,0:T(8,128)S(1)}, f32[16,8,128]{2,1,0:T(8,128)S(1)}) custom-call(s32[2]{0:T(128)S(1)} %pad_add_fusion.me_ref, s32[1,32]{1,0:T(1,128)S(1)} %get-tuple-element.23.place_ref, bf16[64,128]{1,0:T(8,128)(2,1)S(1)} %get-tuple-element.29.keep_ref, bf16[128,128]{1,0:T(8,128)(2,1)S(1)} %collective-permute-done.near_ref, ...), custom_call_target="tpu_custom_call" | custom-call | bytes 1048576 | tf_op jit(solution)/shard_map/collect_suffix/pallas_call | solution.py:405
  40.5 2.2 %all-to-all-done.1 = bf16[32,16,128]{2,1,0:T(8,128)(2,1)S(1)} async-done(((bf16[32,16,128]{2,1,0:T(8,128)(2,1)}), bf16[32,16,128]{2,1,0:T(8,128)(2,1)S(1)}, u32[]{:S(2)}, u32[]{:S(2)}) %all-to-all-start.1) | async-done | bytes 131104 | tf_op jit(solution)/shard_map/all_to_all | solution.py:578
  42.7 1.3 %merge_and_project.1 = (bf16[8,64,512]{2,1,0:T(8,128)(2,1)S(1)}, bf16[64,256]{1,0:T(8,128)(2,1)S(1)}) custom-call(s32[2]{0:T(128)S(1)} %pad_add_fusion.me_ref, s32[64,1]{1,0:T(8,128)S(1)} %add.27.col_ref, bf16[16,2,16,128]{3,2,1,0:T(8,128)(2,1)S(1)} %bitcast.8, f32[16,8,128]{2,1,0:T(8,128)S(1)} %get-tuple-element.32.value_ref, ...), custom_call_target="tpu_custom_call" | custom-call | tf_op jit(solution)/shard_map/merge_and_project/pallas_call | solution.py:455
  44.0 1.8 %collective-permute-start.5 = (bf16[8,64,512]{2,1,0:T(8,128)(2,1)S(1)}, bf16[8,64,512]{2,1,0:T(8,128)(2,1)S(1)}, u32[]{:S(2)}, u32[]{:S(2)}) collective-permute-start(bf16[8,64,512]{2,1,0:T(8,128)(2,1)S(1)} %get-tuple-element.38), channel_id=1, source_target_pairs={{0,1},{1,0},{2,3},{3,2},{4,5},{5,4},{6,7},{7,6},{8,9},{9,8},{10,11... | collective-permute-start | bytes 1572872 | tf_op jit(solution)/shard_map/ppermute | solution.py:539
  45.8 2.2 %project.1.one_ref = f32[8,64,512]{2,1,0:T(8,128)S(1)} custom-call(s32[2]{0:T(128)S(1)} %pad_add_fusion.me_ref, bf16[64,256]{1,0:T(8,128)(2,1)S(1)} %get-tuple-element.36.att_ref, bf16[128,8192]{1,0:T(8,128)(2,1)S(1)} %get-tuple-element.34.upper_ref, bf16[8,128,512]{2,1,0:T(8,128)(2,1)} %get-tuple-element.37.low_hbm), custom_call_target="tpu_custom_call" | custom-call | flops 1073741824 | bytes 2097152 | tf_op jit(solution)/shard_map/project/pallas_call | solution.py:487
  48.0 0.0 collective-permute-done.5.two_ref
  48.0 0.1 add_halves.1
  48.1 16.5 %all_to_all.15.in_ref = bf16[8,64,512]{2,1,0:T(8,128)(2,1)S(1)} all-to-all(bf16[8,64,512]{2,1,0:T(8,128)(2,1)S(1)} %add_halves.1), channel_id=1, replica_groups=mesh['tensor'=4,'prompt'=16,'xh'=2,'core'=2] {'tensor','xh'}, dimensions={0} | all-to-all | bytes 1048576 | tf_op jit(solution)/shard_map/all_to_all | solution.py:595
  64.6 0.7 %sum_shares.1 = bf16[32,2,512]{2,1,0:T(2,128)(2,1)} custom-call(bf16[8,64,512]{2,1,0:T(8,128)(2,1)S(1)} %all_to_all.15.in_ref), custom_call_target="tpu_custom_call" | custom-call | tf_op jit(solution)/shard_map/sum_shares/pallas_call | solution.py:527
  (3 shorter events, 0.0 us)
Async XLA Ops:
  0.0 4.7 %collective-permute-start.1 = (bf16[8,2,1024]{2,1,0:T(2,128)(2,1)}, bf16[8,2,1024]{2,1,0:T(2,128)(2,1)S(1)}, u32[]{:S(2)}, u32[]{:S(2)}) collective-permute-start(bf16[8,2,1024]{2,1,0:T(2,128)(2,1)} %q_hbm.3), channel_id=1, source_target_pairs={{0,1},{1,0},{2,3},{3,2},{4,5},{5,4},{6,7},{7,6},{8,9},{9,8},{10,11... | collective-permute-start | bytes 98312 | tf_op jit(solution)/shard_map/ppermute | solution.py:539
  5.9 19.5 %collective-permute-start.2 = (bf16[2,1024,128]{2,1,0:T(8,128)(2,1)}, bf16[2,1024,128]{2,1,0:T(8,128)(2,1)S(1)}, u32[]{:S(2)}, u32[]{:S(2)}) collective-permute-start(bf16[2,1024,128]{2,1,0:T(8,128)(2,1)} %k_own), channel_id=1, source_target_pairs={{0,1},{1,0},{2,3},{3,2},{4,5},{5,4},{6,7},{7,6},{8,9},{9,8},{10,11... | collective-permute-start | bytes 1572872 | tf_op jit(solution)/shard_map/ppermute | solution.py:539
  5.9 19.5 %collective-permute-start.3 = (bf16[2,1024,128]{2,1,0:T(8,128)(2,1)}, bf16[2,1024,128]{2,1,0:T(8,128)(2,1)S(1)}, u32[]{:S(2)}, u32[]{:S(2)}) collective-permute-start(bf16[2,1024,128]{2,1,0:T(8,128)(2,1)} %v_own), channel_id=1, source_target_pairs={{0,1},{1,0},{2,3},{3,2},{4,5},{5,4},{6,7},{7,6},{8,9},{9,8},{10,11... | collective-permute-start | bytes 1572872 | tf_op jit(solution)/shard_map/ppermute | solution.py:539
  6.4 19.0 %all-to-all-start = ((bf16[32,16,128]{2,1,0:T(8,128)(2,1)}), bf16[32,16,128]{2,1,0:T(8,128)(2,1)S(1)}, u32[]{:S(2)}, u32[]{:S(2)}) async-start(bf16[32,16,128]{2,1,0:T(8,128)(2,1)} %bitcast.3), calls=%async_computation | async-start | bytes 262144 | tf_op jit(solution)/shard_map/all_to_all | solution.py:566
  15.7 6.1 %copy-start.2 = (s32[1,32]{1,0:T(1,128)S(1)}, s32[1,32]{1,0:T(1,128)}, u32[]{:S(2)}) copy-start(s32[1,32]{1,0:T(1,128)} %place_hbm.1) | copy-start | bytes 388
  15.7 9.7 %copy-start = (bf16[2,1024,128]{2,1,0:T(8,128)(2,1)S(1)}, bf16[2,1024,128]{2,1,0:T(8,128)(2,1)}, u32[]{:S(2)}) copy-start(bf16[2,1024,128]{2,1,0:T(8,128)(2,1)} %k_own) | copy-start | bytes 1572868
  15.8 9.7 %copy-start.1 = (bf16[2,1024,128]{2,1,0:T(8,128)(2,1)S(1)}, bf16[2,1024,128]{2,1,0:T(8,128)(2,1)}, u32[]{:S(2)}) copy-start(bf16[2,1024,128]{2,1,0:T(8,128)(2,1)} %v_own) | copy-start | bytes 1572868
  21.4 5.7 %collective-permute-start = (bf16[128,128]{1,0:T(8,128)(2,1)S(1)}, bf16[128,128]{1,0:T(8,128)(2,1)S(1)}, u32[]{:S(2)}, u32[]{:S(2)}) collective-permute-start(bf16[128,128]{1,0:T(8,128)(2,1)S(1)} %get-tuple-element.22), channel_id=1, source_target_pairs={{0,1},{1,0},{2,3},{3,2},{4,5},{5,4},{6,7},{7,6},{8,9},{9,8},{10,11... | collective-permute-start | bytes 98312 | tf_op jit(solution)/shard_map/ppermute | solution.py:539
  27.1 15.6 %all-to-all-start.1 = ((bf16[32,16,128]{2,1,0:T(8,128)(2,1)}), bf16[32,16,128]{2,1,0:T(8,128)(2,1)S(1)}, u32[]{:S(2)}, u32[]{:S(2)}) async-start(bf16[32,16,128]{2,1,0:T(8,128)(2,1)} %bitcast.5), calls=%async_computation.1 | async-start | bytes 262144 | tf_op jit(solution)/shard_map/all_to_all | solution.py:578
  33.1 6.7 %collective-permute-start.4 = (bf16[128,128]{1,0:T(8,128)(2,1)S(1)}, bf16[128,128]{1,0:T(8,128)(2,1)S(1)}, u32[]{:S(2)}, u32[]{:S(2)}) collective-permute-start(bf16[128,128]{1,0:T(8,128)(2,1)S(1)} %pad_maximum_fusion), channel_id=1, source_target_pairs={{0,2},{2,0},{1,3},{3,1},{4,6},{6,4},{5,7},{7,5},{8,10},{10,8},{9,1... | collective-permute-start | bytes 98312 | tf_op jit(solution)/shard_map/ppermute | solution.py:539
  44.0 4.0 %collective-permute-start.5 = (bf16[8,64,512]{2,1,0:T(8,128)(2,1)S(1)}, bf16[8,64,512]{2,1,0:T(8,128)(2,1)S(1)}, u32[]{:S(2)}, u32[]{:S(2)}) collective-permute-start(bf16[8,64,512]{2,1,0:T(8,128)(2,1)S(1)} %get-tuple-element.38), channel_id=1, source_target_pairs={{0,1},{1,0},{2,3},{3,2},{4,5},{5,4},{6,7},{7,6},{8,9},{9,8},{10,11... | collective-permute-start | bytes 1572872 | tf_op jit(solution)/shard_map/ppermute | solution.py:539

commit v5 on v4

--- a/solution.py
+++ b/solution.py
@@ -254,7 +254,7 @@
             pltpu.SemaphoreType.DMA((2, slots, blocks)),
         ],
         cost_estimate=pl.CostEstimate(
-            flops=4 * slots * rows * span * D * 8,
+            flops=4 * slots * rows * span * D * 64,
             bytes_accessed=4 * slots * span * D,
             transcendentals=slots * rows * span,
         ),
@@ -316,11 +316,11 @@
     )(q_rows, k_own, k_other, v_own, v_other)
 
 
-def low_copies(w_hbm, low_ref, sem, which):
+def low_copies(me_ref, w_hbm, low_ref, sem, which):
     blocks, depth, width = low_ref.shape
     return [
         pltpu.make_async_copy(
-            w_hbm.at[pl.ds(depth, depth), block_columns(2 * b + which, width)],
+            w_hbm.at[pl.ds(depth, depth), block_columns(me_ref, b, which, width)],
             low_ref.at[b],
             sem.at[b],
         )
@@ -332,8 +332,8 @@
     upper_sem, low_sem, mine_sem, out_sem = sems
     core = me_ref[1]
     chunk = upper_ref.shape[0] // CHUNKS
-    mine = low_copies(w_hbm, mine_ref, mine_sem, core)
-    copies = low_copies(w_hbm, low_ref, low_sem, 1 - core)
+    mine = low_copies(me_ref, w_hbm, mine_ref, mine_sem, core)
+    copies = low_copies(me_ref, w_hbm, low_ref, low_sem, 1 - core)
     for j in range(CHUNKS):
         part = pl.ds(j * chunk, chunk)
         copies.append(pltpu.make_async_copy(w_hbm.at[part], upper_ref.at[part], upper_sem.at[j]))
@@ -377,7 +377,10 @@
     )(me, in_hbm(weight), after)
 
 
-def block_columns(block, width):
+def block_columns(me_ref, step, which, width):
+    ahead = (me_ref[2] + step // 2) % 4
+    xh = me_ref[0] if step % 2 == 0 else 1 - me_ref[0]
+    block = 4 * ahead + 2 * xh + which
     return pl.ds(pl.multiple_of(block * width, width), width)
 
 
@@ -444,7 +447,7 @@
         att_ref[:, h * D : (h + 1) * D] = dot(pick, merged).astype(BF16)
     half = low_ref.shape[1]
     for b in range(blocks):
-        columns = block_columns(2 * b + 1 - core, width)
+        columns = block_columns(me_ref, b, 1 - core, width)
         value = dot(att_ref[:, 0:half], upper_ref[:, columns])
         out_ref[b] = (value + dot(att_ref[:, half:], low_ref[b])).astype(BF16)
 
@@ -473,7 +476,7 @@
     for copy in copies:
         copy.start()
     for b in range(blocks):
-        columns = block_columns(2 * b + me_ref[1], width)
+        columns = block_columns(me_ref, b, me_ref[1], width)
         out_ref[b] = dot(att_ref[:, 0:half], upper_ref[:, columns])
     for copy in copies:
         copy.wait()
@@ -500,38 +503,63 @@
     )(me, attention, upper, in_hbm(low))
 
 
-def add_kernel(one_ref, two_ref, out_ref):
-    out_ref[...] = (one_ref[...] + two_ref[...].astype(F32)).astype(BF16)
+def add_kernel(one_ref, two_ref, keep_ref, *out_refs):
+    keep_ref[...] = one_ref[0:2] + two_ref[0:2].astype(F32)
+    for b, out_ref in enumerate(out_refs, 1):
+        value = one_ref[2 * b : 2 * b + 2] + two_ref[2 * b : 2 * b + 2].astype(F32)
+        out_ref[...] = value.astype(BF16)
 
 
 def add_halves(one, two):
+    steps = one.shape[0] // 2
+    shape = (2,) + one.shape[1:]
     return pl.pallas_call(
         add_kernel,
         in_specs=[VMEM_SPEC] * 2,
-        out_specs=VMEM_SPEC,
-        out_shape=jax.ShapeDtypeStruct(two.shape, BF16),
+        out_specs=[VMEM_SPEC] * steps,
+        out_shape=[jax.ShapeDtypeStruct(shape, F32)]
+        + [jax.ShapeDtypeStruct(shape, BF16)] * (steps - 1),
         compiler_params=PARAMS,
         name="add_halves",
     )(one, two)
 
 
-def sum_kernel(in_ref, out_ref):
-    total = in_ref[0].astype(F32)
-    for j in range(1, in_ref.shape[0]):
-        total = total + in_ref[j].astype(F32)
+def tensor_kernel(keep_ref, *rest):
+    in_refs, stay_ref, away_ref = rest[:-2], rest[-2], rest[-1]
+    for away, out_ref in ((0, stay_ref), (1, away_ref)):
+        total = keep_ref[away]
+        for ref in in_refs:
+            total = total + ref[away].astype(F32)
+        out_ref[...] = total.astype(out_ref.dtype)
+
+
+def sum_tensor(keep, shares):
+    shape = keep.shape[1:]
+    return pl.pallas_call(
+        tensor_kernel,
+        in_specs=[VMEM_SPEC] * (1 + len(shares)),
+        out_specs=[VMEM_SPEC] * 2,
+        out_shape=[jax.ShapeDtypeStruct(shape, F32), jax.ShapeDtypeStruct(shape, BF16)],
+        compiler_params=PARAMS,
+        name="sum_tensor",
+    )(keep, *shares)
+
+
+def sum_kernel(one_ref, two_ref, out_ref):
+    total = one_ref[...] + two_ref[...].astype(F32)
     out_ref[...] = total.astype(BF16).reshape(out_ref.shape)
 
 
-def sum_shares(shares, tokens):
-    _, rows, width = shares.shape
+def sum_shares(one, two, tokens):
+    rows, width = one.shape
     return pl.pallas_call(
         sum_kernel,
-        in_specs=[VMEM_SPEC],
+        in_specs=[VMEM_SPEC] * 2,
         out_specs=VMEM_SPEC,
         out_shape=jax.ShapeDtypeStruct((rows // tokens, tokens, width), BF16),
         compiler_params=PARAMS,
         name="sum_shares",
-    )(shares)
+    )(one, two)
 
 
 def swap(value, axes):
@@ -556,7 +584,7 @@
     blocks = lax.axis_size("tensor") * 2
     place = placement[0]
     slots = place.shape[0]
-    me = jnp.stack([lax.axis_index("xh"), lax.axis_index("core")]).astype(jnp.int32)
+    me = jnp.stack([lax.axis_index("xh"), lax.axis_index("core"), lax.axis_index("tensor")]).astype(jnp.int32)
     other = swap(q_step, ("core",))
     own, place_here = own_rows(me, placement, q_step)
     routed = route(me, place_here, own, other, indices)
@@ -592,10 +620,14 @@
     )
     away = swap(away, ("core",))
     stay = project(me, attention, upper, low_mine)
-    spread = lax.all_to_all(
-        add_halves(stay, away), ("tensor", "xh"), split_axis=0, concat_axis=0, tiled=True
-    )
-    return sum_shares(spread, tokens)
+    keep_t, *shares = add_halves(stay, away)
+    steps = blocks // 2
+    shares = [
+        lax.ppermute(shares[b - 1], "tensor", [(i, (i + b) % steps) for i in range(steps)])
+        for b in (2, 1, 3)
+    ]
+    one, two = sum_tensor(keep_t, shares)
+    return sum_shares(one, swap(two, ("xh",)), tokens)
 
 
 def solution(mesh):

time: 65.7 us -> 64.2 us (0.977)
  blocking collectives: 16.5 us -> 0 us
  starting transfers between devices: 23.9 us -> 31.9 us
  waiting for transfers between devices: 5.82 us -> 12.6 us
    all_to_all x1 -> x0, blocking collectives: 16.5 us -> none  [body(): lax.all_to_all(add_halves(stay, away), ('tensor', 'xh'), split_axis=0, co...]
    ppermute x0 -> x3, starting transfers between devices: none -> 5.7 us  [body(): lax.ppermute(shares[b - 1], 'tensor', [(i, (i + b) % steps) for i in rang...]
    ppermute x0 -> x3, waiting for transfers between devices: none -> 4.18 us  [body(): lax.ppermute(shares[b - 1], 'tensor', [(i, (i + b) % steps) for i in rang...]
    ppermute x6 -> x7, waiting for transfers between devices: 0.02 us -> 3.33 us  [swap(): return lax.ppermute(value, axes, [(i, size - 1 - i) for i in range(size)])]
    ppermute x6 -> x7, starting transfers between devices: 8.73 us -> 10.4 us  [swap(): return lax.ppermute(value, axes, [(i, size - 1 - i) for i in range(size)])]
  transfers between devices with their start and end apart: 8 -> 12, of which waited for: 2 -> 6; matrix products, arithmetic and copies ran while one was open for 0% -> 0% of each run, Pallas kernels for 24% -> 24%
where the time goes in v5:
time: 64.2 us; the launch traced here: 63.6 us
  starting transfers between devices  31.9 us (50%)
  Pallas kernels  18.7 us (29%)
  waiting for transfers between devices  12.6 us (20%)
    ppermute x7, starting transfers between devices, swap(): return lax.ppermute(value, axes, [(i, size - 1 - i) for i in range(size)])  10.4 us
    all_to_all x1, starting transfers between devices, body(): lax.all_to_all(routed.reshape(indices * 2, 16, D), ('prompt', 'xh'), spli...  9.3 us
    all_to_all x1, starting transfers between devices, body(): lax.all_to_all(parts.reshape(indices * 2, 16, D), ('prompt', 'xh'), split...  6.51 us
    ppermute x3, starting transfers between devices, body(): lax.ppermute(shares[b - 1], 'tensor', [(i, (i + b) % steps) for i in rang...  5.7 us
    pallas_call x1, Pallas kernels, suffix_attention(): pl.pallas_call(suffix_kernel, in_specs=[SMEM_SPEC] + [HBM_SPEC] * 6, out_...  5.63 us
    ppermute x3, waiting for transfers between devices, body(): lax.ppermute(shares[b - 1], 'tensor', [(i, (i + b) % steps) for i in rang...  4.18 us
    pallas_call x1, Pallas kernels, stage_weight(): pl.pallas_call(stage_kernel, in_specs=[SMEM_SPEC, HBM_SPEC, pl.BlockSpec(...  3.68 us
    ppermute x7, waiting for transfers between devices, swap(): return lax.ppermute(value, axes, [(i, size - 1 - i) for i in range(size)])  3.33 us
  transfers between devices with their start and end apart: 12, of which 6 were waited for; matrix products, arithmetic and copies ran while one was open for 0% of the time, Pallas kernels for 24%

profile of v5, /device:TPU:1, one launch (start us, length us, event | category | flops | bytes accessed | tf_op | source)
XLA Modules:
  0.0 63.6 jit_solution(12187369268902853661)
XLA Ops:
  0.0 3.2 %collective-permute-start.1 = (bf16[8,2,1024]{2,1,0:T(2,128)(2,1)}, bf16[8,2,1024]{2,1,0:T(2,128)(2,1)S(1)}, u32[]{:S(2)}, u32[]{:S(2)}) collective-permute-start(bf16[8,2,1024]{2,1,0:T(2,128)(2,1)} %q_hbm.3), channel_id=1, source_target_pairs={{0,1},{1,0},{2,3},{3,2},{4,5},{5,4},{6,7},{7,6},{8,9},{9,8},{10,11... | collective-permute-start | bytes 98312 | tf_op jit(solution)/shard_map/ppermute | solution.py:567
  3.2 0.1 pad_add_fusion.me_ref
  3.3 1.3 %own_rows.1 = (f32[32,8,128]{2,1,0:T(8,128)S(1)}, s32[1,32]{1,0:T(1,128)S(1)}) custom-call(s32[3]{0:T(128)S(1)} %pad_add_fusion.me_ref, s32[1,32]{1,0:T(1,128)} %place_hbm.1, bf16[8,2,1024]{2,1,0:T(2,128)(2,1)} %q_hbm.3), custom_call_target="tpu_custom_call" | custom-call | bytes 2097152 | tf_op jit(solution)/shard_map/own_rows/pallas_call | solution.py:92
  4.7 0.0 collective-permute-done.1.other_ref
  4.7 1.2 %route_queries.1 = bf16[16,2,16,128]{3,2,1,0:T(8,128)(2,1)} custom-call(s32[3]{0:T(128)S(1)} %pad_add_fusion.me_ref, s32[1,32]{1,0:T(1,128)S(1)} %get-tuple-element.29.place_ref, f32[32,8,128]{2,1,0:T(8,128)S(1)} %get-tuple-element.30.own_ref, bf16[8,2,1024]{2,1,0:T(2,128)(2,1)S(1)} %collective-permute-done.1.other_ref), custom_call_target="tpu_custom_call" | custom-call | tf_op jit(solution)/shard_map/route_queries/pallas_call | solution.py:124
  5.9 9.3 %all-to-all-start = ((bf16[32,16,128]{2,1,0:T(8,128)(2,1)}), bf16[32,16,128]{2,1,0:T(8,128)(2,1)S(1)}, u32[]{:S(2)}, u32[]{:S(2)}) async-start(bf16[32,16,128]{2,1,0:T(8,128)(2,1)} %bitcast.4), calls=%async_computation | async-start | bytes 262144 | tf_op jit(solution)/shard_map/all_to_all | solution.py:594
  15.2 0.0 copy-start.2
  15.2 0.0 copy-start
  15.2 0.0 copy-start.1
  15.3 0.4 collective-permute-start.2
  15.6 0.2 collective-permute-start.3
  15.9 5.6 %suffix_attention.1 = (bf16[64,128]{1,0:T(8,128)(2,1)S(1)}, bf16[128,128]{1,0:T(8,128)(2,1)S(1)}, bf16[64,128]{1,0:T(8,128)(2,1)S(1)}) custom-call(s32[3]{0:T(128)S(1)} %pad_add_fusion.me_ref, s32[8]{0:T(128)} %len_hbm.1, bf16[8,2,1024]{2,1,0:T(2,128)(2,1)} %q_hbm.3, bf16[8,2,128]{2,1,0:T(2,128)(2,1)} %sk_hbm.1, bf16[8,2,128]{2,1,0:T(2,128)(2,1)} %sv_hbm.1, ...), custom_call_target="tpu_custom_call" | custom-call | flops 8589934592 | bytes 8388608 | tf_op jit(solution)/shard_map/suffix_attention/pallas_call | solution.py:239
  21.5 0.4 collective-permute-start
  21.9 0.0 copy-done.2
  21.9 3.0 %all-to-all-done = bf16[32,16,128]{2,1,0:T(8,128)(2,1)S(1)} async-done(((bf16[32,16,128]{2,1,0:T(8,128)(2,1)}), bf16[32,16,128]{2,1,0:T(8,128)(2,1)S(1)}, u32[]{:S(2)}, u32[]{:S(2)}) %all-to-all-start) | async-done | bytes 131104 | tf_op jit(solution)/shard_map/all_to_all | solution.py:594
  24.9 0.0 collective-permute-done.2.k_other
  24.9 0.0 collective-permute-done.3.v_other
  24.9 0.0 copy-done
  24.9 0.0 copy-done.1
  24.9 1.7 %prefix_attention.1.after_ref = bf16[16,2,16,128]{3,2,1,0:T(8,128)(2,1)} custom-call(bf16[16,2,16,128]{3,2,1,0:T(8,128)(2,1)S(1)} %bitcast.10, bf16[2,1024,128]{2,1,0:T(8,128)(2,1)S(1)} %copy-done, bf16[2,1024,128]{2,1,0:T(8,128)(2,1)S(1)} %collective-permute-done.2.k_other, bf16[2,1024,128]{2,1,0:T(8,128)(2,1)S(1)} %copy-done.1, ...), custom_call_target="tpu_custom_call" | custom-call | tf_op jit(solution)/shard_map/prefix_attention/pallas_call | solution.py:309
  26.6 0.0 collective-permute-done.near_ref
  26.6 6.5 %all-to-all-start.1 = ((bf16[32,16,128]{2,1,0:T(8,128)(2,1)}), bf16[32,16,128]{2,1,0:T(8,128)(2,1)S(1)}, u32[]{:S(2)}, u32[]{:S(2)}) async-start(bf16[32,16,128]{2,1,0:T(8,128)(2,1)} %bitcast.6), calls=%async_computation.1 | async-start | bytes 262144 | tf_op jit(solution)/shard_map/all_to_all | solution.py:606
  33.2 2.8 %collective-permute-start.4 = (bf16[128,128]{1,0:T(8,128)(2,1)S(1)}, bf16[128,128]{1,0:T(8,128)(2,1)S(1)}, u32[]{:S(2)}, u32[]{:S(2)}) collective-permute-start(bf16[128,128]{1,0:T(8,128)(2,1)S(1)} %pad_maximum_fusion), channel_id=1, source_target_pairs={{0,2},{2,0},{1,3},{3,1},{4,6},{6,4},{5,7},{7,5},{8,10},{10,8},{9,1... | collective-permute-start | bytes 98312 | tf_op jit(solution)/shard_map/ppermute | solution.py:567
  36.0 0.1 iota_add_fusion
  36.1 0.1 add.27.col_ref
  36.1 3.7 %stage_weight.1 = (bf16[128,8192]{1,0:T(8,128)(2,1)S(1)}, bf16[8,128,512]{2,1,0:T(8,128)(2,1)S(1)}, bf16[8,128,512]{2,1,0:T(8,128)(2,1)}) custom-call(s32[3]{0:T(128)S(1)} %pad_add_fusion.me_ref, bf16[256,8192]{1,0:T(8,128)(2,1)} %w_hbm.1, bf16[16,2,16,128]{3,2,1,0:T(8,128)(2,1)} %prefix_attention.1.after_ref), custom_call_target="tpu_custom_call" | custom-call | bytes 10485760 | tf_op jit(solution)/shard_map/stage_weight/pallas_call | solution.py:356
  39.8 0.0 collective-permute-done.4.far_ref
  39.8 0.8 %collect_suffix.1 = (f32[16,8,128]{2,1,0:T(8,128)S(1)}, f32[16,8,128]{2,1,0:T(8,128)S(1)}) custom-call(s32[3]{0:T(128)S(1)} %pad_add_fusion.me_ref, s32[1,32]{1,0:T(1,128)S(1)} %get-tuple-element.29.place_ref, bf16[64,128]{1,0:T(8,128)(2,1)S(1)} %get-tuple-element.35.keep_ref, bf16[128,128]{1,0:T(8,128)(2,1)S(1)} %collective-permute-done.near_ref, ...), custom_call_target="tpu_custom_call" | custom-call | bytes 1048576 | tf_op jit(solution)/shard_map/collect_suffix/pallas_call | solution.py:408
  40.6 2.0 %all-to-all-done.1 = bf16[32,16,128]{2,1,0:T(8,128)(2,1)S(1)} async-done(((bf16[32,16,128]{2,1,0:T(8,128)(2,1)}), bf16[32,16,128]{2,1,0:T(8,128)(2,1)S(1)}, u32[]{:S(2)}, u32[]{:S(2)}) %all-to-all-start.1) | async-done | bytes 131104 | tf_op jit(solution)/shard_map/all_to_all | solution.py:606
  42.6 1.3 %merge_and_project.1 = (bf16[8,64,512]{2,1,0:T(8,128)(2,1)S(1)}, bf16[64,256]{1,0:T(8,128)(2,1)S(1)}) custom-call(s32[3]{0:T(128)S(1)} %pad_add_fusion.me_ref, s32[64,1]{1,0:T(8,128)S(1)} %add.27.col_ref, bf16[16,2,16,128]{3,2,1,0:T(8,128)(2,1)S(1)} %bitcast.9, f32[16,8,128]{2,1,0:T(8,128)S(1)} %get-tuple-element.38.value_ref, ...), custom_call_target="tpu_custom_call" | custom-call | tf_op jit(solution)/shard_map/merge_and_project/pallas_call | solution.py:458
  43.9 2.0 %collective-permute-start.5 = (bf16[8,64,512]{2,1,0:T(8,128)(2,1)S(1)}, bf16[8,64,512]{2,1,0:T(8,128)(2,1)S(1)}, u32[]{:S(2)}, u32[]{:S(2)}) collective-permute-start(bf16[8,64,512]{2,1,0:T(8,128)(2,1)S(1)} %get-tuple-element.44), channel_id=1, source_target_pairs={{0,1},{1,0},{2,3},{3,2},{4,5},{5,4},{6,7},{7,6},{8,9},{9,8},{10,11... | collective-permute-start | bytes 1572872 | tf_op jit(solution)/shard_map/ppermute | solution.py:567
  45.9 2.2 %project.1.one_ref = f32[8,64,512]{2,1,0:T(8,128)S(1)} custom-call(s32[3]{0:T(128)S(1)} %pad_add_fusion.me_ref, bf16[64,256]{1,0:T(8,128)(2,1)S(1)} %get-tuple-element.42.att_ref, bf16[128,8192]{1,0:T(8,128)(2,1)S(1)} %get-tuple-element.40.upper_ref, bf16[8,128,512]{2,1,0:T(8,128)(2,1)} %get-tuple-element.43.low_hbm), custom_call_target="tpu_custom_call" | custom-call | flops 1073741824 | bytes 2097152 | tf_op jit(solution)/shard_map/project/pallas_call | solution.py:490
  48.1 0.0 collective-permute-done.5.two_ref
  48.1 0.1 add_halves.1
  48.3 3.0 %collective-permute-start.6 = (bf16[2,64,512]{2,1,0:T(8,128)(2,1)S(1)}, bf16[2,64,512]{2,1,0:T(8,128)(2,1)S(1)}, u32[]{:S(2)}, u32[]{:S(2)}) collective-permute-start(bf16[2,64,512]{2,1,0:T(8,128)(2,1)S(1)} %get-tuple-element.46), channel_id=1, source_target_pairs={{0,128},{64,192},{128,0},{192,64},{1,129},{65,193},{129,1},{193,65... | collective-permute-start | bytes 393224 | tf_op jit(solution)/shard_map/ppermute | solution.py:626
  51.3 0.4 collective-permute-start.7
  51.7 2.3 %collective-permute-start.8 = (bf16[2,64,512]{2,1,0:T(8,128)(2,1)S(1)}, bf16[2,64,512]{2,1,0:T(8,128)(2,1)S(1)}, u32[]{:S(2)}, u32[]{:S(2)}) collective-permute-start(bf16[2,64,512]{2,1,0:T(8,128)(2,1)S(1)} %get-tuple-element.48), channel_id=1, source_target_pairs={{0,192},{64,0},{128,64},{192,128},{1,193},{65,1},{129,65},{193,129... | collective-permute-start | bytes 393224 | tf_op jit(solution)/shard_map/ppermute | solution.py:626
  54.0 1.0 %collective-permute-done.6.rest_0_ = bf16[2,64,512]{2,1,0:T(8,128)(2,1)S(1)} collective-permute-done((bf16[2,64,512]{2,1,0:T(8,128)(2,1)S(1)}, bf16[2,64,512]{2,1,0:T(8,128)(2,1)S(1)}, u32[]{:S(2)}, u32[]{:S(2)}) %collective-permute-start.6) | collective-permute-done | bytes 131104 | tf_op jit(solution)/shard_map/ppermute | solution.py:626
  55.0 2.9 %collective-permute-done.7.rest_1_ = bf16[2,64,512]{2,1,0:T(8,128)(2,1)S(1)} collective-permute-done((bf16[2,64,512]{2,1,0:T(8,128)(2,1)S(1)}, bf16[2,64,512]{2,1,0:T(8,128)(2,1)S(1)}, u32[]{:S(2)}, u32[]{:S(2)}) %collective-permute-start.7) | collective-permute-done | bytes 131104 | tf_op jit(solution)/shard_map/ppermute | solution.py:626
  57.9 0.3 collective-permute-done.8.rest_2_
  58.2 0.1 sum_tensor.1
  58.2 1.4 %collective-permute-start.9 = (bf16[64,512]{1,0:T(8,128)(2,1)S(1)}, bf16[64,512]{1,0:T(8,128)(2,1)S(1)}, u32[]{:S(2)}, u32[]{:S(2)}) collective-permute-start(bf16[64,512]{1,0:T(8,128)(2,1)S(1)} %get-tuple-element.50), channel_id=1, source_target_pairs={{0,2},{2,0},{1,3},{3,1},{4,6},{6,4},{5,7},{7,5},{8,10},{10,8},{9,1... | collective-permute-start | bytes 196616 | tf_op jit(solution)/shard_map/ppermute | solution.py:567
  59.6 3.3 %collective-permute-done.9.two_ref = bf16[64,512]{1,0:T(8,128)(2,1)S(1)} collective-permute-done((bf16[64,512]{1,0:T(8,128)(2,1)S(1)}, bf16[64,512]{1,0:T(8,128)(2,1)S(1)}, u32[]{:S(2)}, u32[]{:S(2)}) %collective-permute-start.9) | collective-permute-done | bytes 65568 | tf_op jit(solution)/shard_map/ppermute | solution.py:567
  62.9 0.7 %sum_shares.1 = bf16[32,2,512]{2,1,0:T(2,128)(2,1)} custom-call(f32[64,512]{1,0:T(8,128)S(1)} %get-tuple-element.49.one_ref, bf16[64,512]{1,0:T(8,128)(2,1)S(1)} %collective-permute-done.9.two_ref), custom_call_target="tpu_custom_call" | custom-call | tf_op jit(solution)/shard_map/sum_shares/pallas_call | solution.py:555
  (3 shorter events, 0.0 us)
Async XLA Ops:
  0.0 4.7 %collective-permute-start.1 = (bf16[8,2,1024]{2,1,0:T(2,128)(2,1)}, bf16[8,2,1024]{2,1,0:T(2,128)(2,1)S(1)}, u32[]{:S(2)}, u32[]{:S(2)}) collective-permute-start(bf16[8,2,1024]{2,1,0:T(2,128)(2,1)} %q_hbm.3), channel_id=1, source_target_pairs={{0,1},{1,0},{2,3},{3,2},{4,5},{5,4},{6,7},{7,6},{8,9},{9,8},{10,11... | collective-permute-start | bytes 98312 | tf_op jit(solution)/shard_map/ppermute | solution.py:567
  5.9 19.0 %all-to-all-start = ((bf16[32,16,128]{2,1,0:T(8,128)(2,1)}), bf16[32,16,128]{2,1,0:T(8,128)(2,1)S(1)}, u32[]{:S(2)}, u32[]{:S(2)}) async-start(bf16[32,16,128]{2,1,0:T(8,128)(2,1)} %bitcast.4), calls=%async_computation | async-start | bytes 262144 | tf_op jit(solution)/shard_map/all_to_all | solution.py:594
  15.2 6.6 %copy-start.2 = (s32[1,32]{1,0:T(1,128)S(1)}, s32[1,32]{1,0:T(1,128)}, u32[]{:S(2)}) copy-start(s32[1,32]{1,0:T(1,128)} %place_hbm.1) | copy-start | bytes 388
  15.2 9.7 %copy-start = (bf16[2,1024,128]{2,1,0:T(8,128)(2,1)S(1)}, bf16[2,1024,128]{2,1,0:T(8,128)(2,1)}, u32[]{:S(2)}) copy-start(bf16[2,1024,128]{2,1,0:T(8,128)(2,1)} %k_own) | copy-start | bytes 1572868
  15.2 9.7 %copy-start.1 = (bf16[2,1024,128]{2,1,0:T(8,128)(2,1)S(1)}, bf16[2,1024,128]{2,1,0:T(8,128)(2,1)}, u32[]{:S(2)}) copy-start(bf16[2,1024,128]{2,1,0:T(8,128)(2,1)} %v_own) | copy-start | bytes 1572868
  15.3 9.6 %collective-permute-start.2 = (bf16[2,1024,128]{2,1,0:T(8,128)(2,1)}, bf16[2,1024,128]{2,1,0:T(8,128)(2,1)S(1)}, u32[]{:S(2)}, u32[]{:S(2)}) collective-permute-start(bf16[2,1024,128]{2,1,0:T(8,128)(2,1)} %k_own), channel_id=1, source_target_pairs={{0,1},{1,0},{2,3},{3,2},{4,5},{5,4},{6,7},{7,6},{8,9},{9,8},{10,11... | collective-permute-start | bytes 1572872 | tf_op jit(solution)/shard_map/ppermute | solution.py:567
  15.6 9.3 %collective-permute-start.3 = (bf16[2,1024,128]{2,1,0:T(8,128)(2,1)}, bf16[2,1024,128]{2,1,0:T(8,128)(2,1)S(1)}, u32[]{:S(2)}, u32[]{:S(2)}) collective-permute-start(bf16[2,1024,128]{2,1,0:T(8,128)(2,1)} %v_own), channel_id=1, source_target_pairs={{0,1},{1,0},{2,3},{3,2},{4,5},{5,4},{6,7},{7,6},{8,9},{9,8},{10,11... | collective-permute-start | bytes 1572872 | tf_op jit(solution)/shard_map/ppermute | solution.py:567
  21.5 5.1 %collective-permute-start = (bf16[128,128]{1,0:T(8,128)(2,1)S(1)}, bf16[128,128]{1,0:T(8,128)(2,1)S(1)}, u32[]{:S(2)}, u32[]{:S(2)}) collective-permute-start(bf16[128,128]{1,0:T(8,128)(2,1)S(1)} %get-tuple-element.28), channel_id=1, source_target_pairs={{0,1},{1,0},{2,3},{3,2},{4,5},{5,4},{6,7},{7,6},{8,9},{9,8},{10,11... | collective-permute-start | bytes 98312 | tf_op jit(solution)/shard_map/ppermute | solution.py:567
  26.6 16.0 %all-to-all-start.1 = ((bf16[32,16,128]{2,1,0:T(8,128)(2,1)}), bf16[32,16,128]{2,1,0:T(8,128)(2,1)S(1)}, u32[]{:S(2)}, u32[]{:S(2)}) async-start(bf16[32,16,128]{2,1,0:T(8,128)(2,1)} %bitcast.6), calls=%async_computation.1 | async-start | bytes 262144 | tf_op jit(solution)/shard_map/all_to_all | solution.py:606
  33.2 6.7 %collective-permute-start.4 = (bf16[128,128]{1,0:T(8,128)(2,1)S(1)}, bf16[128,128]{1,0:T(8,128)(2,1)S(1)}, u32[]{:S(2)}, u32[]{:S(2)}) collective-permute-start(bf16[128,128]{1,0:T(8,128)(2,1)S(1)} %pad_maximum_fusion), channel_id=1, source_target_pairs={{0,2},{2,0},{1,3},{3,1},{4,6},{6,4},{5,7},{7,5},{8,10},{10,8},{9,1... | collective-permute-start | bytes 98312 | tf_op jit(solution)/shard_map/ppermute | solution.py:567
  43.9 4.2 %collective-permute-start.5 = (bf16[8,64,512]{2,1,0:T(8,128)(2,1)S(1)}, bf16[8,64,512]{2,1,0:T(8,128)(2,1)S(1)}, u32[]{:S(2)}, u32[]{:S(2)}) collective-permute-start(bf16[8,64,512]{2,1,0:T(8,128)(2,1)S(1)} %get-tuple-element.44), channel_id=1, source_target_pairs={{0,1},{1,0},{2,3},{3,2},{4,5},{5,4},{6,7},{7,6},{8,9},{9,8},{10,11... | collective-permute-start | bytes 1572872 | tf_op jit(solution)/shard_map/ppermute | solution.py:567
  48.3 6.7 %collective-permute-start.6 = (bf16[2,64,512]{2,1,0:T(8,128)(2,1)S(1)}, bf16[2,64,512]{2,1,0:T(8,128)(2,1)S(1)}, u32[]{:S(2)}, u32[]{:S(2)}) collective-permute-start(bf16[2,64,512]{2,1,0:T(8,128)(2,1)S(1)} %get-tuple-element.46), channel_id=1, source_target_pairs={{0,128},{64,192},{128,0},{192,64},{1,129},{65,193},{129,1},{193,65... | collective-permute-start | bytes 393224 | tf_op jit(solution)/shard_map/ppermute | solution.py:626
  51.3 6.6 %collective-permute-start.7 = (bf16[2,64,512]{2,1,0:T(8,128)(2,1)S(1)}, bf16[2,64,512]{2,1,0:T(8,128)(2,1)S(1)}, u32[]{:S(2)}, u32[]{:S(2)}) collective-permute-start(bf16[2,64,512]{2,1,0:T(8,128)(2,1)S(1)} %get-tuple-element.47), channel_id=1, source_target_pairs={{0,64},{64,128},{128,192},{192,0},{1,65},{65,129},{129,193},{193,1... | collective-permute-start | bytes 393224 | tf_op jit(solution)/shard_map/ppermute | solution.py:626
  51.7 6.5 %collective-permute-start.8 = (bf16[2,64,512]{2,1,0:T(8,128)(2,1)S(1)}, bf16[2,64,512]{2,1,0:T(8,128)(2,1)S(1)}, u32[]{:S(2)}, u32[]{:S(2)}) collective-permute-start(bf16[2,64,512]{2,1,0:T(8,128)(2,1)S(1)} %get-tuple-element.48), channel_id=1, source_target_pairs={{0,192},{64,0},{128,64},{192,128},{1,193},{65,1},{129,65},{193,129... | collective-permute-start | bytes 393224 | tf_op jit(solution)/shard_map/ppermute | solution.py:626
  58.2 4.7 %collective-permute-start.9 = (bf16[64,512]{1,0:T(8,128)(2,1)S(1)}, bf16[64,512]{1,0:T(8,128)(2,1)S(1)}, u32[]{:S(2)}, u32[]{:S(2)}) collective-permute-start(bf16[64,512]{1,0:T(8,128)(2,1)S(1)} %get-tuple-element.50), channel_id=1, source_target_pairs={{0,2},{2,0},{1,3},{3,1},{4,6},{6,4},{5,7},{7,5},{8,10},{10,8},{9,1... | collective-permute-start | bytes 196616 | tf_op jit(solution)/shard_map/ppermute | solution.py:567

commit v6 on v5

--- a/solution.py
+++ b/solution.py
@@ -46,6 +46,10 @@
 
 def lower_rows(shape):
     return lax.broadcasted_iota(jnp.int32, shape, len(shape) - 2) < 4
+
+
+def here():
+    return tuple(lax.axis_index(name) for name in ("xh", "core", "tensor"))
 
 
 def in_hbm(value):
@@ -73,7 +77,8 @@
             rows[u, j * tokens : (j + 1) * tokens, :] = jnp.where(core == 0, one, two)
 
 
-def own_kernel(me_ref, place_hbm, q_hbm, rows, place_out, place_ref, mine_ref, sem):
+def own_kernel(place_hbm, q_hbm, rows, place_out, place_ref, mine_ref, sem):
+    me_ref = here()
     xh, core = me_ref[0], me_ref[1]
     copies = (
         pltpu.make_async_copy(place_hbm, place_ref, sem.at[0]),
@@ -88,10 +93,10 @@
     scatter_rows(mine_ref, place_ref, rows, (2 * xh + core) * q_hbm.shape[0], core)
 
 
-def own_rows(me, placement, mine):
+def own_rows(placement, mine):
     return pl.pallas_call(
         own_kernel,
-        in_specs=[SMEM_SPEC, HBM_SPEC, HBM_SPEC],
+        in_specs=[HBM_SPEC, HBM_SPEC],
         out_specs=[VMEM_SPEC, VMEM_SPEC],
         out_shape=[
             jax.ShapeDtypeStruct((placement.shape[1], 8, D), F32),
@@ -107,10 +112,11 @@
         ),
         compiler_params=PARAMS,
         name="own_rows",
-    )(me, in_hbm(placement), in_hbm(mine))
-
-
-def route_kernel(me_ref, place_ref, own_ref, other_ref, out_ref, rows):
+    )(in_hbm(placement), in_hbm(mine))
+
+
+def route_kernel(place_ref, own_ref, other_ref, out_ref, rows):
+    me_ref = here()
     xh, core = me_ref[0], me_ref[1]
     rows[...] = own_ref[...]
     first = (2 * xh + 1 - core) * other_ref.shape[0]
@@ -120,19 +126,20 @@
         out_ref[:, j] = packed
 
 
-def route(me, placement, own, other, indices):
+def route(placement, own, other, indices):
     return pl.pallas_call(
         route_kernel,
-        in_specs=[SMEM_SPEC, SMEM_SPEC, VMEM_SPEC, VMEM_SPEC],
+        in_specs=[SMEM_SPEC, VMEM_SPEC, VMEM_SPEC],
         out_specs=VMEM_SPEC,
         out_shape=jax.ShapeDtypeStruct((indices, 2, 16, D), BF16),
         scratch_shapes=[pltpu.VMEM(own.shape, F32)],
         compiler_params=PARAMS,
         name="route_queries",
-    )(me, placement, own, other)
-
-
-def suffix_kernel(me_ref, len_hbm, q_hbm, sk_hbm, sv_hbm, k_hbm, v_hbm, *rest):
+    )(placement, own, other)
+
+
+def suffix_kernel(len_hbm, q_hbm, sk_hbm, sv_hbm, k_hbm, v_hbm, *rest):
+    me_ref = here()
     keep_ref, core_ref, xh_ref = rest[:3]
     len_ref, q_ref, sk_ref, sv_ref, rows_ref, keys, values, tiles, small_sem, sem = rest[3:]
     slots, span, _ = k_hbm.shape
@@ -231,14 +238,14 @@
     xh_ref[...] = piece(1 - xh, core)
 
 
-def suffix_attention(me, lengths, q_step, step_k, step_values, suffix_k, suffix_values):
+def suffix_attention(lengths, q_step, step_k, step_values, suffix_k, suffix_values):
     slots, span, _ = suffix_k.shape
     rows = 16
     piece = jax.ShapeDtypeStruct((slots * 8, D), BF16)
     blocks = span // BLOCK
     return pl.pallas_call(
         suffix_kernel,
-        in_specs=[SMEM_SPEC] + [HBM_SPEC] * 6,
+        in_specs=[HBM_SPEC] * 6,
         out_specs=[VMEM_SPEC] * 3,
         out_shape=[piece, jax.ShapeDtypeStruct((slots * 16, D), BF16), piece],
         scratch_shapes=[
@@ -261,7 +268,6 @@
         compiler_params=PARAMS,
         name="suffix_attention",
     )(
-        me,
         in_hbm(lengths),
         in_hbm(q_step),
         in_hbm(step_k),
@@ -328,7 +334,8 @@
     ]
 
 
-def stage_kernel(me_ref, w_hbm, after_ref, upper_ref, low_ref, mine_hbm, mine_ref, *sems):
+def stage_kernel(w_hbm, after_ref, upper_ref, low_ref, mine_hbm, mine_ref, *sems):
+    me_ref = here()
     upper_sem, low_sem, mine_sem, out_sem = sems
     core = me_ref[1]
     chunk = upper_ref.shape[0] // CHUNKS
@@ -350,12 +357,12 @@
         copy.wait()
 
 
-def stage_weight(me, weight, after, blocks):
+def stage_weight(weight, after, blocks):
     depth, width = weight.shape
     low = (blocks, depth // 2, width // (2 * blocks))
     return pl.pallas_call(
         stage_kernel,
-        in_specs=[SMEM_SPEC, HBM_SPEC, pl.BlockSpec(memory_space=pl.ANY)],
+        in_specs=[HBM_SPEC, pl.BlockSpec(memory_space=pl.ANY)],
         out_specs=[VMEM_SPEC, VMEM_SPEC, HBM_SPEC],
         out_shape=[
             jax.ShapeDtypeStruct((depth // 2, width), BF16),
@@ -374,7 +381,7 @@
         ),
         compiler_params=PARAMS,
         name="stage_weight",
-    )(me, in_hbm(weight), after)
+    )(in_hbm(weight), after)
 
 
 def block_columns(me_ref, step, which, width):
@@ -384,8 +391,8 @@
     return pl.ds(pl.multiple_of(block * width, width), width)
 
 
-def collect_kernel(me_ref, place_ref, keep_ref, near_ref, far_ref, value_ref, level_ref, own):
-    xh, core = me_ref[0], me_ref[1]
+def collect_kernel(place_ref, keep_ref, near_ref, far_ref, value_ref, level_ref, own):
+    xh, core, _ = here()
     owners = value_ref.shape[0]
     count = keep_ref.shape[0] // 8
     pieces = ((keep_ref, 0, xh, core), (near_ref, 0, xh, 1 - core))
@@ -403,11 +410,11 @@
     level_ref[...] = jnp.broadcast_to(level, level_ref.shape)
 
 
-def collect_suffix(me, placement, pieces, owners):
+def collect_suffix(placement, pieces, owners):
     part = jax.ShapeDtypeStruct((owners, 8, D), F32)
     return pl.pallas_call(
         collect_kernel,
-        in_specs=[SMEM_SPEC] * 2 + [VMEM_SPEC] * 3,
+        in_specs=[SMEM_SPEC] + [VMEM_SPEC] * 3,
         out_specs=[VMEM_SPEC] * 2,
         out_shape=[part, part],
         scratch_shapes=[pltpu.VMEM((placement.shape[1], 8, D), F32)],
@@ -416,12 +423,13 @@
         ),
         compiler_params=PARAMS,
         name="collect_suffix",
-    )(me, placement, *pieces)
+    )(placement, *pieces)
 
 
 def merge_kernel(
-    me_ref, col_ref, parts_ref, value_ref, level_ref, upper_ref, low_ref, out_ref, att_ref
+    col_ref, parts_ref, value_ref, level_ref, upper_ref, low_ref, out_ref, att_ref
 ):
+    me_ref = here()
     core = me_ref[1]
     blocks, out_rows, width = out_ref.shape
     owners = parts_ref.shape[0]
@@ -452,12 +460,12 @@
         out_ref[b] = (value + dot(att_ref[:, half:], low_ref[b])).astype(BF16)
 
 
-def merge_and_project(me, columns, parts, suffix, upper, low):
+def merge_and_project(columns, parts, suffix, upper, low):
     blocks, half, width = low.shape
     out_rows = columns.shape[0]
     return pl.pallas_call(
         merge_kernel,
-        in_specs=[SMEM_SPEC] + [VMEM_SPEC] * 6,
+        in_specs=[VMEM_SPEC] * 6,
         out_specs=[VMEM_SPEC, VMEM_SPEC],
         out_shape=[
             jax.ShapeDtypeStruct((blocks, out_rows, width), BF16),
@@ -465,10 +473,11 @@
         ],
         compiler_params=PARAMS,
         name="merge_and_project",
-    )(me, columns, parts, *suffix, upper, low)
-
-
-def project_kernel(me_ref, att_ref, upper_ref, low_hbm, out_ref, low_ref, sem):
+    )(columns, parts, *suffix, upper, low)
+
+
+def project_kernel(att_ref, upper_ref, low_hbm, out_ref, low_ref, sem):
+    me_ref = here()
     blocks, half, width = low_ref.shape
     copies = [
         pltpu.make_async_copy(low_hbm.at[b], low_ref.at[b], sem.at[b]) for b in range(blocks)
@@ -484,12 +493,12 @@
         out_ref[b] += dot(att_ref[:, half:], low_ref[b])
 
 
-def project(me, attention, upper, low):
+def project(attention, upper, low):
     blocks, half, width = low.shape
     out_rows = attention.shape[0]
     return pl.pallas_call(
         project_kernel,
-        in_specs=[SMEM_SPEC, VMEM_SPEC, VMEM_SPEC, HBM_SPEC],
+        in_specs=[VMEM_SPEC, VMEM_SPEC, HBM_SPEC],
         out_specs=VMEM_SPEC,
         out_shape=jax.ShapeDtypeStruct((blocks, out_rows, width), F32),
         scratch_shapes=[pltpu.VMEM(low.shape, BF16), pltpu.SemaphoreType.DMA((blocks,))],
@@ -500,7 +509,7 @@
         ),
         compiler_params=PARAMS,
         name="project",
-    )(me, attention, upper, in_hbm(low))
+    )(attention, upper, in_hbm(low))
 
 
 def add_kernel(one_ref, two_ref, keep_ref, *out_refs):
@@ -584,10 +593,9 @@
     blocks = lax.axis_size("tensor") * 2
     place = placement[0]
     slots = place.shape[0]
-    me = jnp.stack([lax.axis_index("xh"), lax.axis_index("core"), lax.axis_index("tensor")]).astype(jnp.int32)
     other = swap(q_step, ("core",))
-    own, place_here = own_rows(me, placement, q_step)
-    routed = route(me, place_here, own, other, indices)
+    own, place_here = own_rows(placement, q_step)
+    routed = route(place_here, own, other, indices)
     routed, prefix_k, prefix_v = lax.optimization_barrier((routed, prefix_k, prefix_v))
     k_other = swap(prefix_k, ("core",))
     v_other = swap(prefix_v, ("core",))
@@ -595,7 +603,7 @@
         routed.reshape(indices * 2, 16, D), ("prompt", "xh"), split_axis=0, concat_axis=0, tiled=True
     )
     keep, to_core, to_xh = suffix_attention(
-        me, lengths, q_step, step_k, step_values, suffix_k, suffix_values
+        lengths, q_step, step_k, step_values, suffix_k, suffix_values
     )
     near = swap(to_core, ("core",))
     parts = prefix_attention(
@@ -606,20 +614,19 @@
     returned = lax.all_to_all(
         parts.reshape(indices * 2, 16, D), ("prompt", "xh"), split_axis=0, concat_axis=0, tiled=True
     )
-    upper, low_away, low_mine = stage_weight(me, output_weight, parts, blocks)
+    upper, low_away, low_mine = stage_weight(output_weight, parts, blocks)
     columns = (place[:, None] * 4 + jnp.arange(tokens, dtype=jnp.int32)[None, :]).reshape(
         slots * tokens, 1
     )
     away, attention = merge_and_project(
-        me,
         columns,
         returned.reshape(indices, 2, 16, D),
-        collect_suffix(me, place_here, (keep, near, far), indices),
+        collect_suffix(place_here, (keep, near, far), indices),
         upper,
         low_away,
     )
     away = swap(away, ("core",))
-    stay = project(me, attention, upper, low_mine)
+    stay = project(attention, upper, low_mine)
     keep_t, *shares = add_halves(stay, away)
     steps = blocks // 2
     shares = [

time: 64.2 us -> 62.5 us (0.974)
  Pallas kernels: 18.7 us -> 15.9 us
    pallas_call x7, Pallas kernels: 16.1 us -> 13.4 us  [the longest x1 5.09 us: suffix_attention(): pl.pallas_call(suffix_kernel, in_specs=[HBM_SPEC] * 6, out_specs=[VMEM_SP...]
  transfers between devices with their start and end apart: 12 -> 12, of which waited for: 6 -> 6; matrix products, arithmetic and copies ran while one was open for 0% -> 0% of each run, Pallas kernels for 24% -> 21%
where the time goes in v6:
time: 62.5 us; the launch traced here: 61.6 us
  starting transfers between devices  32.3 us (52%)
  Pallas kernels  15.9 us (25%)
  waiting for transfers between devices  13.1 us (21%)
    ppermute x7, starting transfers between devices, swap(): return lax.ppermute(value, axes, [(i, size - 1 - i) for i in range(size)])  10.8 us
    all_to_all x1, starting transfers between devices, body(): lax.all_to_all(routed.reshape(indices * 2, 16, D), ('prompt', 'xh'), spli...  9.3 us
    all_to_all x1, starting transfers between devices, body(): lax.all_to_all(parts.reshape(indices * 2, 16, D), ('prompt', 'xh'), split...  6.56 us
    ppermute x3, starting transfers between devices, body(): lax.ppermute(shares[b - 1], 'tensor', [(i, (i + b) % steps) for i in rang...  5.67 us
    pallas_call x1, Pallas kernels, suffix_attention(): pl.pallas_call(suffix_kernel, in_specs=[HBM_SPEC] * 6, out_specs=[VMEM_SP...  5.09 us
    ppermute x3, waiting for transfers between devices, body(): lax.ppermute(shares[b - 1], 'tensor', [(i, (i + b) % steps) for i in rang...  3.95 us
    ppermute x7, waiting for transfers between devices, swap(): return lax.ppermute(value, axes, [(i, size - 1 - i) for i in range(size)])  3.55 us
    pallas_call x1, Pallas kernels, stage_weight(): pl.pallas_call(stage_kernel, in_specs=[HBM_SPEC, pl.BlockSpec(memory_spac...  3.12 us
  transfers between devices with their start and end apart: 12, of which 6 were waited for; matrix products, arithmetic and copies ran while one was open for 0% of the time, Pallas kernels for 21%

profile of v6, /device:TPU:1, one launch (start us, length us, event | category | flops | bytes accessed | tf_op | source)
XLA Modules:
  0.0 61.6 jit_solution(8789835780976831100)
XLA Ops:
  0.0 3.2 %collective-permute-start.1 = (bf16[8,2,1024]{2,1,0:T(2,128)(2,1)}, bf16[8,2,1024]{2,1,0:T(2,128)(2,1)S(1)}, u32[]{:S(2)}, u32[]{:S(2)}) collective-permute-start(bf16[8,2,1024]{2,1,0:T(2,128)(2,1)} %q_hbm.3), channel_id=1, source_target_pairs={{0,1},{1,0},{2,3},{3,2},{4,5},{5,4},{6,7},{7,6},{8,9},{9,8},{10,11... | collective-permute-start | bytes 98312 | tf_op jit(solution)/shard_map/ppermute | solution.py:576
  3.2 0.8 %own_rows.1 = (f32[32,8,128]{2,1,0:T(8,128)S(1)}, s32[1,32]{1,0:T(1,128)S(1)}) custom-call(s32[1,32]{1,0:T(1,128)} %place_hbm.1, bf16[8,2,1024]{2,1,0:T(2,128)(2,1)} %q_hbm.3), custom_call_target="tpu_custom_call" | custom-call | bytes 2097152 | tf_op jit(solution)/shard_map/own_rows/pallas_call | solution.py:97
  4.1 0.3 collective-permute-done.1.other_ref
  4.3 1.2 %route_queries.1 = bf16[16,2,16,128]{3,2,1,0:T(8,128)(2,1)} custom-call(s32[1,32]{1,0:T(1,128)S(1)} %get-tuple-element.29.place_ref, f32[32,8,128]{2,1,0:T(8,128)S(1)} %get-tuple-element.30.own_ref, bf16[8,2,1024]{2,1,0:T(2,128)(2,1)S(1)} %collective-permute-done.1.other_ref), custom_call_target="tpu_custom_call" | custom-call | tf_op jit(solution)/shard_map/route_queries/pallas_call | solution.py:130
  5.5 9.3 %all-to-all-start = ((bf16[32,16,128]{2,1,0:T(8,128)(2,1)}), bf16[32,16,128]{2,1,0:T(8,128)(2,1)S(1)}, u32[]{:S(2)}, u32[]{:S(2)}) async-start(bf16[32,16,128]{2,1,0:T(8,128)(2,1)} %bitcast.1), calls=%async_computation | async-start | bytes 262144 | tf_op jit(solution)/shard_map/all_to_all | solution.py:602
  14.8 0.0 copy-start.2
  14.9 0.0 copy-start
  14.9 0.0 copy-start.1
  14.9 0.7 %collective-permute-start.2 = (bf16[2,1024,128]{2,1,0:T(8,128)(2,1)}, bf16[2,1024,128]{2,1,0:T(8,128)(2,1)S(1)}, u32[]{:S(2)}, u32[]{:S(2)}) collective-permute-start(bf16[2,1024,128]{2,1,0:T(8,128)(2,1)} %k_own), channel_id=1, source_target_pairs={{0,1},{1,0},{2,3},{3,2},{4,5},{5,4},{6,7},{7,6},{8,9},{9,8},{10,11... | collective-permute-start | bytes 1572872 | tf_op jit(solution)/shard_map/ppermute | solution.py:576
  15.6 0.1 collective-permute-start.3
  15.7 5.1 %suffix_attention.1 = (bf16[64,128]{1,0:T(8,128)(2,1)S(1)}, bf16[128,128]{1,0:T(8,128)(2,1)S(1)}, bf16[64,128]{1,0:T(8,128)(2,1)S(1)}) custom-call(s32[8]{0:T(128)} %len_hbm.1, bf16[8,2,1024]{2,1,0:T(2,128)(2,1)} %q_hbm.3, bf16[8,2,128]{2,1,0:T(2,128)(2,1)} %sk_hbm.1, bf16[8,2,128]{2,1,0:T(2,128)(2,1)} %sv_hbm.1, bf16[8,2048,128]{2,1,0:T(8,128)(2,1)} %k_hbm.1, ...), custom_call_target="tpu_custom_call" | custom-call | flops 8589934592 | bytes 8388608 | tf_op jit(solution)/shard_map/suffix_attention/pallas_call | solution.py:246
  20.8 0.5 collective-permute-start
  21.3 0.0 copy-done.2
  21.3 3.0 %all-to-all-done = bf16[32,16,128]{2,1,0:T(8,128)(2,1)S(1)} async-done(((bf16[32,16,128]{2,1,0:T(8,128)(2,1)}), bf16[32,16,128]{2,1,0:T(8,128)(2,1)S(1)}, u32[]{:S(2)}, u32[]{:S(2)}) %all-to-all-start) | async-done | bytes 131104 | tf_op jit(solution)/shard_map/all_to_all | solution.py:602
  24.3 0.0 collective-permute-done.2.k_other
  24.3 0.0 collective-permute-done.3.v_other
  24.3 0.0 copy-done
  24.3 0.0 copy-done.1
  24.3 1.7 %prefix_attention.1.after_ref = bf16[16,2,16,128]{3,2,1,0:T(8,128)(2,1)} custom-call(bf16[16,2,16,128]{3,2,1,0:T(8,128)(2,1)S(1)} %bitcast.6, bf16[2,1024,128]{2,1,0:T(8,128)(2,1)S(1)} %copy-done, bf16[2,1024,128]{2,1,0:T(8,128)(2,1)S(1)} %collective-permute-done.2.k_other, bf16[2,1024,128]{2,1,0:T(8,128)(2,1)S(1)} %copy-done.1, ...), custom_call_target="tpu_custom_call" | custom-call | tf_op jit(solution)/shard_map/prefix_attention/pallas_call | solution.py:315
  26.0 0.0 collective-permute-done.near_ref
  26.0 6.6 %all-to-all-start.1 = ((bf16[32,16,128]{2,1,0:T(8,128)(2,1)}), bf16[32,16,128]{2,1,0:T(8,128)(2,1)S(1)}, u32[]{:S(2)}, u32[]{:S(2)}) async-start(bf16[32,16,128]{2,1,0:T(8,128)(2,1)} %bitcast.3), calls=%async_computation.1 | async-start | bytes 262144 | tf_op jit(solution)/shard_map/all_to_all | solution.py:614
  32.6 2.8 %collective-permute-start.4 = (bf16[128,128]{1,0:T(8,128)(2,1)S(1)}, bf16[128,128]{1,0:T(8,128)(2,1)S(1)}, u32[]{:S(2)}, u32[]{:S(2)}) collective-permute-start(bf16[128,128]{1,0:T(8,128)(2,1)S(1)} %pad_maximum_fusion), channel_id=1, source_target_pairs={{0,2},{2,0},{1,3},{3,1},{4,6},{6,4},{5,7},{7,5},{8,10},{10,8},{9,1... | collective-permute-start | bytes 98312 | tf_op jit(solution)/shard_map/ppermute | solution.py:576
  35.4 0.1 iota_add_fusion
  35.5 0.1 add.27.col_ref
  35.6 3.1 %stage_weight.1 = (bf16[128,8192]{1,0:T(8,128)(2,1)S(1)}, bf16[8,128,512]{2,1,0:T(8,128)(2,1)S(1)}, bf16[8,128,512]{2,1,0:T(8,128)(2,1)}) custom-call(bf16[256,8192]{1,0:T(8,128)(2,1)} %w_hbm.1, bf16[16,2,16,128]{3,2,1,0:T(8,128)(2,1)} %prefix_attention.1.after_ref), custom_call_target="tpu_custom_call" | custom-call | bytes 10485760 | tf_op jit(solution)/shard_map/stage_weight/pallas_call | solution.py:363
  38.7 0.0 collective-permute-done.4.far_ref
  38.7 0.8 %collect_suffix.1 = (f32[16,8,128]{2,1,0:T(8,128)S(1)}, f32[16,8,128]{2,1,0:T(8,128)S(1)}) custom-call(s32[1,32]{1,0:T(1,128)S(1)} %get-tuple-element.29.place_ref, bf16[64,128]{1,0:T(8,128)(2,1)S(1)} %get-tuple-element.35.keep_ref, bf16[128,128]{1,0:T(8,128)(2,1)S(1)} %collective-permute-done.near_ref, bf16[128,128]{1,0:T(8,128)(2,1)S(1)} %collective-permute-done.4.far_ref), custom_call_target="tpu_custom_call" | custom-call | bytes 1048576 | tf_op jit(solution)/shard_map/collect_suffix/pallas_call | solution.py:415
  39.5 2.6 %all-to-all-done.1 = bf16[32,16,128]{2,1,0:T(8,128)(2,1)S(1)} async-done(((bf16[32,16,128]{2,1,0:T(8,128)(2,1)}), bf16[32,16,128]{2,1,0:T(8,128)(2,1)S(1)}, u32[]{:S(2)}, u32[]{:S(2)}) %all-to-all-start.1) | async-done | bytes 131104 | tf_op jit(solution)/shard_map/all_to_all | solution.py:614
  42.1 0.7 %merge_and_project.1 = (bf16[8,64,512]{2,1,0:T(8,128)(2,1)S(1)}, bf16[64,256]{1,0:T(8,128)(2,1)S(1)}) custom-call(s32[64,1]{1,0:T(8,128)S(1)} %add.27.col_ref, bf16[16,2,16,128]{3,2,1,0:T(8,128)(2,1)S(1)} %bitcast.7, f32[16,8,128]{2,1,0:T(8,128)S(1)} %get-tuple-element.38.value_ref, f32[16,8,128]{2,1,0:T(8,128)S(1)} %get-tuple-element.39.level_ref, ...), custom_call_target="tpu_custom_call" | custom-call | tf_op jit(solution)/shard_map/merge_and_project/pallas_call | solution.py:466
  42.8 2.0 %collective-permute-start.5 = (bf16[8,64,512]{2,1,0:T(8,128)(2,1)S(1)}, bf16[8,64,512]{2,1,0:T(8,128)(2,1)S(1)}, u32[]{:S(2)}, u32[]{:S(2)}) collective-permute-start(bf16[8,64,512]{2,1,0:T(8,128)(2,1)S(1)} %get-tuple-element.44), channel_id=1, source_target_pairs={{0,1},{1,0},{2,3},{3,2},{4,5},{5,4},{6,7},{7,6},{8,9},{9,8},{10,11... | collective-permute-start | bytes 1572872 | tf_op jit(solution)/shard_map/ppermute | solution.py:576
  44.8 1.7 %project.1.one_ref = f32[8,64,512]{2,1,0:T(8,128)S(1)} custom-call(bf16[64,256]{1,0:T(8,128)(2,1)S(1)} %get-tuple-element.42.att_ref, bf16[128,8192]{1,0:T(8,128)(2,1)S(1)} %get-tuple-element.40.upper_ref, bf16[8,128,512]{2,1,0:T(8,128)(2,1)} %get-tuple-element.43.low_hbm), custom_call_target="tpu_custom_call" | custom-call | flops 1073741824 | bytes 2097152 | tf_op jit(solution)/shard_map/project/pallas_call | solution.py:499
  46.5 0.0 collective-permute-done.5.two_ref
  46.5 0.1 add_halves.1
  46.6 3.0 %collective-permute-start.6 = (bf16[2,64,512]{2,1,0:T(8,128)(2,1)S(1)}, bf16[2,64,512]{2,1,0:T(8,128)(2,1)S(1)}, u32[]{:S(2)}, u32[]{:S(2)}) collective-permute-start(bf16[2,64,512]{2,1,0:T(8,128)(2,1)S(1)} %get-tuple-element.46), channel_id=1, source_target_pairs={{0,128},{64,192},{128,0},{192,64},{1,129},{65,193},{129,1},{193,65... | collective-permute-start | bytes 393224 | tf_op jit(solution)/shard_map/ppermute | solution.py:633
  49.6 0.4 collective-permute-start.7
  50.0 2.3 %collective-permute-start.8 = (bf16[2,64,512]{2,1,0:T(8,128)(2,1)S(1)}, bf16[2,64,512]{2,1,0:T(8,128)(2,1)S(1)}, u32[]{:S(2)}, u32[]{:S(2)}) collective-permute-start(bf16[2,64,512]{2,1,0:T(8,128)(2,1)S(1)} %get-tuple-element.48), channel_id=1, source_target_pairs={{0,192},{64,0},{128,64},{192,128},{1,193},{65,1},{129,65},{193,129... | collective-permute-start | bytes 393224 | tf_op jit(solution)/shard_map/ppermute | solution.py:633
  52.3 0.8 %collective-permute-done.6.rest_0_ = bf16[2,64,512]{2,1,0:T(8,128)(2,1)S(1)} collective-permute-done((bf16[2,64,512]{2,1,0:T(8,128)(2,1)S(1)}, bf16[2,64,512]{2,1,0:T(8,128)(2,1)S(1)}, u32[]{:S(2)}, u32[]{:S(2)}) %collective-permute-start.6) | collective-permute-done | bytes 131104 | tf_op jit(solution)/shard_map/ppermute | solution.py:633
  53.1 3.1 %collective-permute-done.7.rest_1_ = bf16[2,64,512]{2,1,0:T(8,128)(2,1)S(1)} collective-permute-done((bf16[2,64,512]{2,1,0:T(8,128)(2,1)S(1)}, bf16[2,64,512]{2,1,0:T(8,128)(2,1)S(1)}, u32[]{:S(2)}, u32[]{:S(2)}) %collective-permute-start.7) | collective-permute-done | bytes 131104 | tf_op jit(solution)/shard_map/ppermute | solution.py:633
  56.2 0.0 collective-permute-done.8.rest_2_
  56.2 0.1 sum_tensor.1
  56.3 1.4 %collective-permute-start.9 = (bf16[64,512]{1,0:T(8,128)(2,1)S(1)}, bf16[64,512]{1,0:T(8,128)(2,1)S(1)}, u32[]{:S(2)}, u32[]{:S(2)}) collective-permute-start(bf16[64,512]{1,0:T(8,128)(2,1)S(1)} %get-tuple-element.50), channel_id=1, source_target_pairs={{0,2},{2,0},{1,3},{3,1},{4,6},{6,4},{5,7},{7,5},{8,10},{10,8},{9,1... | collective-permute-start | bytes 196616 | tf_op jit(solution)/shard_map/ppermute | solution.py:576
  57.7 3.3 %collective-permute-done.9.two_ref = bf16[64,512]{1,0:T(8,128)(2,1)S(1)} collective-permute-done((bf16[64,512]{1,0:T(8,128)(2,1)S(1)}, bf16[64,512]{1,0:T(8,128)(2,1)S(1)}, u32[]{:S(2)}, u32[]{:S(2)}) %collective-permute-start.9) | collective-permute-done | bytes 65568 | tf_op jit(solution)/shard_map/ppermute | solution.py:576
  61.0 0.7 %sum_shares.1 = bf16[32,2,512]{2,1,0:T(2,128)(2,1)} custom-call(f32[64,512]{1,0:T(8,128)S(1)} %get-tuple-element.49.one_ref, bf16[64,512]{1,0:T(8,128)(2,1)S(1)} %collective-permute-done.9.two_ref), custom_call_target="tpu_custom_call" | custom-call | tf_op jit(solution)/shard_map/sum_shares/pallas_call | solution.py:564
  (3 shorter events, 0.0 us)
Async XLA Ops:
  0.0 4.3 %collective-permute-start.1 = (bf16[8,2,1024]{2,1,0:T(2,128)(2,1)}, bf16[8,2,1024]{2,1,0:T(2,128)(2,1)S(1)}, u32[]{:S(2)}, u32[]{:S(2)}) collective-permute-start(bf16[8,2,1024]{2,1,0:T(2,128)(2,1)} %q_hbm.3), channel_id=1, source_target_pairs={{0,1},{1,0},{2,3},{3,2},{4,5},{5,4},{6,7},{7,6},{8,9},{9,8},{10,11... | collective-permute-start | bytes 98312 | tf_op jit(solution)/shard_map/ppermute | solution.py:576
  5.5 18.7 %all-to-all-start = ((bf16[32,16,128]{2,1,0:T(8,128)(2,1)}), bf16[32,16,128]{2,1,0:T(8,128)(2,1)S(1)}, u32[]{:S(2)}, u32[]{:S(2)}) async-start(bf16[32,16,128]{2,1,0:T(8,128)(2,1)} %bitcast.1), calls=%async_computation | async-start | bytes 262144 | tf_op jit(solution)/shard_map/all_to_all | solution.py:602
  14.8 6.5 %copy-start.2 = (s32[1,32]{1,0:T(1,128)S(1)}, s32[1,32]{1,0:T(1,128)}, u32[]{:S(2)}) copy-start(s32[1,32]{1,0:T(1,128)} %place_hbm.1) | copy-start | bytes 388
  14.9 9.4 %copy-start = (bf16[2,1024,128]{2,1,0:T(8,128)(2,1)S(1)}, bf16[2,1024,128]{2,1,0:T(8,128)(2,1)}, u32[]{:S(2)}) copy-start(bf16[2,1024,128]{2,1,0:T(8,128)(2,1)} %k_own) | copy-start | bytes 1572868
  14.9 9.4 %copy-start.1 = (bf16[2,1024,128]{2,1,0:T(8,128)(2,1)S(1)}, bf16[2,1024,128]{2,1,0:T(8,128)(2,1)}, u32[]{:S(2)}) copy-start(bf16[2,1024,128]{2,1,0:T(8,128)(2,1)} %v_own) | copy-start | bytes 1572868
  14.9 9.4 %collective-permute-start.2 = (bf16[2,1024,128]{2,1,0:T(8,128)(2,1)}, bf16[2,1024,128]{2,1,0:T(8,128)(2,1)S(1)}, u32[]{:S(2)}, u32[]{:S(2)}) collective-permute-start(bf16[2,1024,128]{2,1,0:T(8,128)(2,1)} %k_own), channel_id=1, source_target_pairs={{0,1},{1,0},{2,3},{3,2},{4,5},{5,4},{6,7},{7,6},{8,9},{9,8},{10,11... | collective-permute-start | bytes 1572872 | tf_op jit(solution)/shard_map/ppermute | solution.py:576
  15.6 8.7 %collective-permute-start.3 = (bf16[2,1024,128]{2,1,0:T(8,128)(2,1)}, bf16[2,1024,128]{2,1,0:T(8,128)(2,1)S(1)}, u32[]{:S(2)}, u32[]{:S(2)}) collective-permute-start(bf16[2,1024,128]{2,1,0:T(8,128)(2,1)} %v_own), channel_id=1, source_target_pairs={{0,1},{1,0},{2,3},{3,2},{4,5},{5,4},{6,7},{7,6},{8,9},{9,8},{10,11... | collective-permute-start | bytes 1572872 | tf_op jit(solution)/shard_map/ppermute | solution.py:576
  20.8 5.2 %collective-permute-start = (bf16[128,128]{1,0:T(8,128)(2,1)S(1)}, bf16[128,128]{1,0:T(8,128)(2,1)S(1)}, u32[]{:S(2)}, u32[]{:S(2)}) collective-permute-start(bf16[128,128]{1,0:T(8,128)(2,1)S(1)} %get-tuple-element.28), channel_id=1, source_target_pairs={{0,1},{1,0},{2,3},{3,2},{4,5},{5,4},{6,7},{7,6},{8,9},{9,8},{10,11... | collective-permute-start | bytes 98312 | tf_op jit(solution)/shard_map/ppermute | solution.py:576
  26.0 16.0 %all-to-all-start.1 = ((bf16[32,16,128]{2,1,0:T(8,128)(2,1)}), bf16[32,16,128]{2,1,0:T(8,128)(2,1)S(1)}, u32[]{:S(2)}, u32[]{:S(2)}) async-start(bf16[32,16,128]{2,1,0:T(8,128)(2,1)} %bitcast.3), calls=%async_computation.1 | async-start | bytes 262144 | tf_op jit(solution)/shard_map/all_to_all | solution.py:614
  32.6 6.1 %collective-permute-start.4 = (bf16[128,128]{1,0:T(8,128)(2,1)S(1)}, bf16[128,128]{1,0:T(8,128)(2,1)S(1)}, u32[]{:S(2)}, u32[]{:S(2)}) collective-permute-start(bf16[128,128]{1,0:T(8,128)(2,1)S(1)} %pad_maximum_fusion), channel_id=1, source_target_pairs={{0,2},{2,0},{1,3},{3,1},{4,6},{6,4},{5,7},{7,5},{8,10},{10,8},{9,1... | collective-permute-start | bytes 98312 | tf_op jit(solution)/shard_map/ppermute | solution.py:576
  42.8 3.7 %collective-permute-start.5 = (bf16[8,64,512]{2,1,0:T(8,128)(2,1)S(1)}, bf16[8,64,512]{2,1,0:T(8,128)(2,1)S(1)}, u32[]{:S(2)}, u32[]{:S(2)}) collective-permute-start(bf16[8,64,512]{2,1,0:T(8,128)(2,1)S(1)} %get-tuple-element.44), channel_id=1, source_target_pairs={{0,1},{1,0},{2,3},{3,2},{4,5},{5,4},{6,7},{7,6},{8,9},{9,8},{10,11... | collective-permute-start | bytes 1572872 | tf_op jit(solution)/shard_map/ppermute | solution.py:576
  46.6 6.5 %collective-permute-start.6 = (bf16[2,64,512]{2,1,0:T(8,128)(2,1)S(1)}, bf16[2,64,512]{2,1,0:T(8,128)(2,1)S(1)}, u32[]{:S(2)}, u32[]{:S(2)}) collective-permute-start(bf16[2,64,512]{2,1,0:T(8,128)(2,1)S(1)} %get-tuple-element.46), channel_id=1, source_target_pairs={{0,128},{64,192},{128,0},{192,64},{1,129},{65,193},{129,1},{193,65... | collective-permute-start | bytes 393224 | tf_op jit(solution)/shard_map/ppermute | solution.py:633
  49.6 6.6 %collective-permute-start.7 = (bf16[2,64,512]{2,1,0:T(8,128)(2,1)S(1)}, bf16[2,64,512]{2,1,0:T(8,128)(2,1)S(1)}, u32[]{:S(2)}, u32[]{:S(2)}) collective-permute-start(bf16[2,64,512]{2,1,0:T(8,128)(2,1)S(1)} %get-tuple-element.47), channel_id=1, source_target_pairs={{0,64},{64,128},{128,192},{192,0},{1,65},{65,129},{129,193},{193,1... | collective-permute-start | bytes 393224 | tf_op jit(solution)/shard_map/ppermute | solution.py:633
  50.0 6.2 %collective-permute-start.8 = (bf16[2,64,512]{2,1,0:T(8,128)(2,1)S(1)}, bf16[2,64,512]{2,1,0:T(8,128)(2,1)S(1)}, u32[]{:S(2)}, u32[]{:S(2)}) collective-permute-start(bf16[2,64,512]{2,1,0:T(8,128)(2,1)S(1)} %get-tuple-element.48), channel_id=1, source_target_pairs={{0,192},{64,0},{128,64},{192,128},{1,193},{65,1},{129,65},{193,129... | collective-permute-start | bytes 393224 | tf_op jit(solution)/shard_map/ppermute | solution.py:633
  56.3 4.7 %collective-permute-start.9 = (bf16[64,512]{1,0:T(8,128)(2,1)S(1)}, bf16[64,512]{1,0:T(8,128)(2,1)S(1)}, u32[]{:S(2)}, u32[]{:S(2)}) collective-permute-start(bf16[64,512]{1,0:T(8,128)(2,1)S(1)} %get-tuple-element.50), channel_id=1, source_target_pairs={{0,2},{2,0},{1,3},{3,1},{4,6},{6,4},{5,7},{7,5},{8,10},{10,8},{9,1... | collective-permute-start | bytes 196616 | tf_op jit(solution)/shard_map/ppermute | solution.py:576

commit v7 on v6

--- a/solution.py
+++ b/solution.py
@@ -65,21 +65,18 @@
             rows[(h // 2) % 2, i, place : place + tokens, :] = wide[:, h * D : (h + 1) * D]
 
 
-def scatter_rows(q_ref, place_ref, rows, first, core):
-    count, tokens, _ = q_ref.shape
-    for i in range(count):
-        u = place_ref[0, first + i]
-        wide = q_ref[i].astype(F32)
-        for j in range(4):
-            h = 4 * (j // 2) + j % 2
-            one = wide[:, h * D : (h + 1) * D]
-            two = wide[:, (h + 2) * D : (h + 3) * D]
-            rows[u, j * tokens : (j + 1) * tokens, :] = jnp.where(core == 0, one, two)
-
-
-def own_kernel(place_hbm, q_hbm, rows, place_out, place_ref, mine_ref, sem):
-    me_ref = here()
-    xh, core = me_ref[0], me_ref[1]
+def head_rows(wide, tokens, core):
+    pieces = []
+    for j in range(4):
+        h = 4 * (j // 2) + j % 2
+        one = wide[:, h * D : (h + 1) * D]
+        two = wide[:, (h + 2) * D : (h + 3) * D]
+        pieces.append((j * tokens, jnp.where(core == 0, one, two)))
+    return pieces
+
+
+def own_kernel(place_hbm, q_hbm, rows, place_out, pick_ref, place_ref, mine_ref, sem):
+    xh, core, _ = here()
     copies = (
         pltpu.make_async_copy(place_hbm, place_ref, sem.at[0]),
         pltpu.make_async_copy(q_hbm, mine_ref, sem.at[1]),
@@ -90,17 +87,30 @@
     rows[...] = jnp.zeros_like(rows)
     for copy in copies:
         copy.wait()
-    scatter_rows(mine_ref, place_ref, rows, (2 * xh + core) * q_hbm.shape[0], core)
+    count, tokens, _ = q_hbm.shape
+    for i in range(count):
+        u = place_ref[0, (2 * xh + core) * count + i]
+        for first, piece in head_rows(mine_ref[i].astype(F32), tokens, core):
+            rows[u, first : first + tokens, :] = piece
+    lane = lax.broadcasted_iota(jnp.int32, (1, D), 1)
+    wanted = jnp.full((1, D), -1, jnp.int32)
+    for i in range(count):
+        u = place_ref[0, (2 * xh + 1 - core) * count + i]
+        wanted = jnp.where(lane // 8 == i, 8 * u + lane % 8, wanted)
+    row = lax.broadcasted_iota(jnp.int32, pick_ref.shape, 0)
+    pick_ref[...] = jnp.where(row == wanted, 1.0, 0.0).astype(BF16)
 
 
 def own_rows(placement, mine):
+    slots = placement.shape[1]
     return pl.pallas_call(
         own_kernel,
         in_specs=[HBM_SPEC, HBM_SPEC],
-        out_specs=[VMEM_SPEC, VMEM_SPEC],
+        out_specs=[VMEM_SPEC] * 3,
         out_shape=[
-            jax.ShapeDtypeStruct((placement.shape[1], 8, D), F32),
+            jax.ShapeDtypeStruct((slots, 8, D), F32),
             jax.ShapeDtypeStruct(placement.shape, jnp.int32),
+            jax.ShapeDtypeStruct((slots * 8, D), BF16),
         ],
         scratch_shapes=[
             pltpu.SMEM(placement.shape, jnp.int32),
@@ -115,27 +125,30 @@
     )(in_hbm(placement), in_hbm(mine))
 
 
-def route_kernel(place_ref, own_ref, other_ref, out_ref, rows):
-    me_ref = here()
-    xh, core = me_ref[0], me_ref[1]
-    rows[...] = own_ref[...]
-    first = (2 * xh + 1 - core) * other_ref.shape[0]
-    scatter_rows(other_ref, place_ref, rows, first, core)
-    packed = rows[...].reshape(out_ref.shape[0], 16, D).astype(BF16)
+def route_kernel(pick_ref, own_ref, other_ref, out_ref, rows):
+    _, core, _ = here()
+    count, tokens, _ = other_ref.shape
+    rows[count:] = jnp.zeros((rows.shape[0] - count, 8, D), F32)
+    for i in range(count):
+        for first, piece in head_rows(other_ref[i].astype(F32), tokens, core):
+            rows[i, first : first + tokens, :] = piece
+    placed = dot(pick_ref[...], rows[...].reshape(D, D).astype(BF16))
+    packed = own_ref[...].reshape(out_ref.shape[0], 16, D)
+    packed = (packed + placed.reshape(out_ref.shape[0], 16, D)).astype(BF16)
     for j in range(out_ref.shape[1]):
         out_ref[:, j] = packed
 
 
-def route(placement, own, other, indices):
+def route(pick, own, other, indices):
     return pl.pallas_call(
         route_kernel,
-        in_specs=[SMEM_SPEC, VMEM_SPEC, VMEM_SPEC],
+        in_specs=[VMEM_SPEC] * 3,
         out_specs=VMEM_SPEC,
         out_shape=jax.ShapeDtypeStruct((indices, 2, 16, D), BF16),
-        scratch_shapes=[pltpu.VMEM(own.shape, F32)],
+        scratch_shapes=[pltpu.VMEM((D // 8, 8, D), F32)],
         compiler_params=PARAMS,
         name="route_queries",
-    )(placement, own, other)
+    )(pick, own, other)
 
 
 def suffix_kernel(len_hbm, q_hbm, sk_hbm, sv_hbm, k_hbm, v_hbm, *rest):
@@ -594,8 +607,8 @@
     place = placement[0]
     slots = place.shape[0]
     other = swap(q_step, ("core",))
-    own, place_here = own_rows(placement, q_step)
-    routed = route(place_here, own, other, indices)
+    own, place_here, pick = own_rows(placement, q_step)
+    routed = route(pick, own, other, indices)
     routed, prefix_k, prefix_v = lax.optimization_barrier((routed, prefix_k, prefix_v))
     k_other = swap(prefix_k, ("core",))
     v_other = swap(prefix_v, ("core",))

time: 62.5 us -> 62.1 us (level)
  transfers between devices with their start and end apart: 12 -> 12, of which waited for: 6 -> 6; matrix products, arithmetic and copies ran while one was open for 0% -> 0% of each run, Pallas kernels for 21% -> 22%
where the time goes in v7:
time: 62.1 us; the launch traced here: 61.3 us
  starting transfers between devices  32.3 us (52%)
  Pallas kernels  15.5 us (25%)
  waiting for transfers between devices  13.1 us (21%)
    ppermute x7, starting transfers between devices, swap(): return lax.ppermute(value, axes, [(i, size - 1 - i) for i in range(size)])  10.8 us
    all_to_all x1, starting transfers between devices, body(): lax.all_to_all(routed.reshape(indices * 2, 16, D), ('prompt', 'xh'), spli...  9.3 us
    all_to_all x1, starting transfers between devices, body(): lax.all_to_all(parts.reshape(indices * 2, 16, D), ('prompt', 'xh'), split...  6.57 us
    ppermute x3, starting transfers between devices, body(): lax.ppermute(shares[b - 1], 'tensor', [(i, (i + b) % steps) for i in rang...  5.68 us
    pallas_call x1, Pallas kernels, suffix_attention(): pl.pallas_call(suffix_kernel, in_specs=[HBM_SPEC] * 6, out_specs=[VMEM_SP...  5.09 us
    ppermute x3, waiting for transfers between devices, body(): lax.ppermute(shares[b - 1], 'tensor', [(i, (i + b) % steps) for i in rang...  3.96 us
    ppermute x7, waiting for transfers between devices, swap(): return lax.ppermute(value, axes, [(i, size - 1 - i) for i in range(size)])  3.57 us
    pallas_call x1, Pallas kernels, stage_weight(): pl.pallas_call(stage_kernel, in_specs=[HBM_SPEC, pl.BlockSpec(memory_spac...  3.12 us
  transfers between devices with their start and end apart: 12, of which 6 were waited for; matrix products, arithmetic and copies ran while one was open for 0% of the time, Pallas kernels for 22%

profile of v7, /device:TPU:1, one launch (start us, length us, event | category | flops | bytes accessed | tf_op | source)
XLA Modules:
  0.0 61.3 jit_solution(1772258271416582250)
XLA Ops:
  0.0 3.2 %collective-permute-start.1 = (bf16[8,2,1024]{2,1,0:T(2,128)(2,1)}, bf16[8,2,1024]{2,1,0:T(2,128)(2,1)S(1)}, u32[]{:S(2)}, u32[]{:S(2)}) collective-permute-start(bf16[8,2,1024]{2,1,0:T(2,128)(2,1)} %q_hbm.3), channel_id=1, source_target_pairs={{0,1},{1,0},{2,3},{3,2},{4,5},{5,4},{6,7},{7,6},{8,9},{9,8},{10,11... | collective-permute-start | bytes 98312 | tf_op jit(solution)/shard_map/ppermute | solution.py:589
  3.2 0.8 %own_rows.1 = (f32[32,8,128]{2,1,0:T(8,128)S(1)}, s32[1,32]{1,0:T(1,128)S(1)}, bf16[256,128]{1,0:T(8,128)(2,1)S(1)}) custom-call(s32[1,32]{1,0:T(1,128)} %place_hbm.1, bf16[8,2,1024]{2,1,0:T(2,128)(2,1)} %q_hbm.3), custom_call_target="tpu_custom_call" | custom-call | bytes 2097152 | tf_op jit(solution)/shard_map/own_rows/pallas_call | solution.py:106
  4.1 0.2 collective-permute-done.1.other_ref
  4.3 0.8 %route_queries.1 = bf16[16,2,16,128]{3,2,1,0:T(8,128)(2,1)} custom-call(bf16[256,128]{1,0:T(8,128)(2,1)S(1)} %get-tuple-element.30.pick_ref, f32[32,8,128]{2,1,0:T(8,128)S(1)} %get-tuple-element.31.own_ref, bf16[8,2,1024]{2,1,0:T(2,128)(2,1)S(1)} %collective-permute-done.1.other_ref), custom_call_target="tpu_custom_call" | custom-call | tf_op jit(solution)/shard_map/route_queries/pallas_call | solution.py:143
  5.1 9.3 %all-to-all-start = ((bf16[32,16,128]{2,1,0:T(8,128)(2,1)}), bf16[32,16,128]{2,1,0:T(8,128)(2,1)S(1)}, u32[]{:S(2)}, u32[]{:S(2)}) async-start(bf16[32,16,128]{2,1,0:T(8,128)(2,1)} %bitcast.1), calls=%async_computation | async-start | bytes 262144 | tf_op jit(solution)/shard_map/all_to_all | solution.py:615
  14.4 0.0 copy-start.2
  14.5 0.0 copy-start
  14.5 0.0 copy-start.1
  14.5 0.7 %collective-permute-start.2 = (bf16[2,1024,128]{2,1,0:T(8,128)(2,1)}, bf16[2,1024,128]{2,1,0:T(8,128)(2,1)S(1)}, u32[]{:S(2)}, u32[]{:S(2)}) collective-permute-start(bf16[2,1024,128]{2,1,0:T(8,128)(2,1)} %k_own), channel_id=1, source_target_pairs={{0,1},{1,0},{2,3},{3,2},{4,5},{5,4},{6,7},{7,6},{8,9},{9,8},{10,11... | collective-permute-start | bytes 1572872 | tf_op jit(solution)/shard_map/ppermute | solution.py:589
  15.2 0.1 collective-permute-start.3
  15.3 5.1 %suffix_attention.1 = (bf16[64,128]{1,0:T(8,128)(2,1)S(1)}, bf16[128,128]{1,0:T(8,128)(2,1)S(1)}, bf16[64,128]{1,0:T(8,128)(2,1)S(1)}) custom-call(s32[8]{0:T(128)} %len_hbm.1, bf16[8,2,1024]{2,1,0:T(2,128)(2,1)} %q_hbm.3, bf16[8,2,128]{2,1,0:T(2,128)(2,1)} %sk_hbm.1, bf16[8,2,128]{2,1,0:T(2,128)(2,1)} %sv_hbm.1, bf16[8,2048,128]{2,1,0:T(8,128)(2,1)} %k_hbm.1, ...), custom_call_target="tpu_custom_call" | custom-call | flops 8589934592 | bytes 8388608 | tf_op jit(solution)/shard_map/suffix_attention/pallas_call | solution.py:259
  20.4 0.5 collective-permute-start
  20.9 0.0 copy-done.2
  20.9 3.0 %all-to-all-done = bf16[32,16,128]{2,1,0:T(8,128)(2,1)S(1)} async-done(((bf16[32,16,128]{2,1,0:T(8,128)(2,1)}), bf16[32,16,128]{2,1,0:T(8,128)(2,1)S(1)}, u32[]{:S(2)}, u32[]{:S(2)}) %all-to-all-start) | async-done | bytes 131104 | tf_op jit(solution)/shard_map/all_to_all | solution.py:615
  23.9 0.0 collective-permute-done.2.k_other
  23.9 0.0 collective-permute-done.3.v_other
  23.9 0.0 copy-done
  23.9 0.0 copy-done.1
  23.9 1.7 %prefix_attention.1.after_ref = bf16[16,2,16,128]{3,2,1,0:T(8,128)(2,1)} custom-call(bf16[16,2,16,128]{3,2,1,0:T(8,128)(2,1)S(1)} %bitcast.6, bf16[2,1024,128]{2,1,0:T(8,128)(2,1)S(1)} %copy-done, bf16[2,1024,128]{2,1,0:T(8,128)(2,1)S(1)} %collective-permute-done.2.k_other, bf16[2,1024,128]{2,1,0:T(8,128)(2,1)S(1)} %copy-done.1, ...), custom_call_target="tpu_custom_call" | custom-call | tf_op jit(solution)/shard_map/prefix_attention/pallas_call | solution.py:328
  25.6 0.0 collective-permute-done.near_ref
  25.6 6.6 %all-to-all-start.1 = ((bf16[32,16,128]{2,1,0:T(8,128)(2,1)}), bf16[32,16,128]{2,1,0:T(8,128)(2,1)S(1)}, u32[]{:S(2)}, u32[]{:S(2)}) async-start(bf16[32,16,128]{2,1,0:T(8,128)(2,1)} %bitcast.3), calls=%async_computation.1 | async-start | bytes 262144 | tf_op jit(solution)/shard_map/all_to_all | solution.py:627
  32.2 2.8 %collective-permute-start.4 = (bf16[128,128]{1,0:T(8,128)(2,1)S(1)}, bf16[128,128]{1,0:T(8,128)(2,1)S(1)}, u32[]{:S(2)}, u32[]{:S(2)}) collective-permute-start(bf16[128,128]{1,0:T(8,128)(2,1)S(1)} %pad_maximum_fusion), channel_id=1, source_target_pairs={{0,2},{2,0},{1,3},{3,1},{4,6},{6,4},{5,7},{7,5},{8,10},{10,8},{9,1... | collective-permute-start | bytes 98312 | tf_op jit(solution)/shard_map/ppermute | solution.py:589
  35.0 0.1 iota_add_fusion
  35.1 0.1 add.27.col_ref
  35.2 3.1 %stage_weight.1 = (bf16[128,8192]{1,0:T(8,128)(2,1)S(1)}, bf16[8,128,512]{2,1,0:T(8,128)(2,1)S(1)}, bf16[8,128,512]{2,1,0:T(8,128)(2,1)}) custom-call(bf16[256,8192]{1,0:T(8,128)(2,1)} %w_hbm.1, bf16[16,2,16,128]{3,2,1,0:T(8,128)(2,1)} %prefix_attention.1.after_ref), custom_call_target="tpu_custom_call" | custom-call | bytes 10485760 | tf_op jit(solution)/shard_map/stage_weight/pallas_call | solution.py:376
  38.3 0.0 collective-permute-done.4.far_ref
  38.3 0.8 %collect_suffix.1 = (f32[16,8,128]{2,1,0:T(8,128)S(1)}, f32[16,8,128]{2,1,0:T(8,128)S(1)}) custom-call(s32[1,32]{1,0:T(1,128)S(1)} %get-tuple-element.36.place_ref, bf16[64,128]{1,0:T(8,128)(2,1)S(1)} %get-tuple-element.37.keep_ref, bf16[128,128]{1,0:T(8,128)(2,1)S(1)} %collective-permute-done.near_ref, bf16[128,128]{1,0:T(8,128)(2,1)S(1)} %collective-permute-done.4.far_ref), custom_call_target="tpu_custom_call" | custom-call | bytes 1048576 | tf_op jit(solution)/shard_map/collect_suffix/pallas_call | solution.py:428
  39.1 2.6 %all-to-all-done.1 = bf16[32,16,128]{2,1,0:T(8,128)(2,1)S(1)} async-done(((bf16[32,16,128]{2,1,0:T(8,128)(2,1)}), bf16[32,16,128]{2,1,0:T(8,128)(2,1)S(1)}, u32[]{:S(2)}, u32[]{:S(2)}) %all-to-all-start.1) | async-done | bytes 131104 | tf_op jit(solution)/shard_map/all_to_all | solution.py:627
  41.6 0.7 %merge_and_project.1 = (bf16[8,64,512]{2,1,0:T(8,128)(2,1)S(1)}, bf16[64,256]{1,0:T(8,128)(2,1)S(1)}) custom-call(s32[64,1]{1,0:T(8,128)S(1)} %add.27.col_ref, bf16[16,2,16,128]{3,2,1,0:T(8,128)(2,1)S(1)} %bitcast.7, f32[16,8,128]{2,1,0:T(8,128)S(1)} %get-tuple-element.40.value_ref, f32[16,8,128]{2,1,0:T(8,128)S(1)} %get-tuple-element.41.level_ref, ...), custom_call_target="tpu_custom_call" | custom-call | tf_op jit(solution)/shard_map/merge_and_project/pallas_call | solution.py:479
  42.4 2.0 %collective-permute-start.5 = (bf16[8,64,512]{2,1,0:T(8,128)(2,1)S(1)}, bf16[8,64,512]{2,1,0:T(8,128)(2,1)S(1)}, u32[]{:S(2)}, u32[]{:S(2)}) collective-permute-start(bf16[8,64,512]{2,1,0:T(8,128)(2,1)S(1)} %get-tuple-element.46), channel_id=1, source_target_pairs={{0,1},{1,0},{2,3},{3,2},{4,5},{5,4},{6,7},{7,6},{8,9},{9,8},{10,11... | collective-permute-start | bytes 1572872 | tf_op jit(solution)/shard_map/ppermute | solution.py:589
  44.4 1.7 %project.1.one_ref = f32[8,64,512]{2,1,0:T(8,128)S(1)} custom-call(bf16[64,256]{1,0:T(8,128)(2,1)S(1)} %get-tuple-element.44.att_ref, bf16[128,8192]{1,0:T(8,128)(2,1)S(1)} %get-tuple-element.42.upper_ref, bf16[8,128,512]{2,1,0:T(8,128)(2,1)} %get-tuple-element.45.low_hbm), custom_call_target="tpu_custom_call" | custom-call | flops 1073741824 | bytes 2097152 | tf_op jit(solution)/shard_map/project/pallas_call | solution.py:512
  46.1 0.0 collective-permute-done.5.two_ref
  46.1 0.1 add_halves.1
  46.2 3.0 %collective-permute-start.6 = (bf16[2,64,512]{2,1,0:T(8,128)(2,1)S(1)}, bf16[2,64,512]{2,1,0:T(8,128)(2,1)S(1)}, u32[]{:S(2)}, u32[]{:S(2)}) collective-permute-start(bf16[2,64,512]{2,1,0:T(8,128)(2,1)S(1)} %get-tuple-element.48), channel_id=1, source_target_pairs={{0,128},{64,192},{128,0},{192,64},{1,129},{65,193},{129,1},{193,65... | collective-permute-start | bytes 393224 | tf_op jit(solution)/shard_map/ppermute | solution.py:646
  49.2 0.4 collective-permute-start.7
  49.6 2.3 %collective-permute-start.8 = (bf16[2,64,512]{2,1,0:T(8,128)(2,1)S(1)}, bf16[2,64,512]{2,1,0:T(8,128)(2,1)S(1)}, u32[]{:S(2)}, u32[]{:S(2)}) collective-permute-start(bf16[2,64,512]{2,1,0:T(8,128)(2,1)S(1)} %get-tuple-element.50), channel_id=1, source_target_pairs={{0,192},{64,0},{128,64},{192,128},{1,193},{65,1},{129,65},{193,129... | collective-permute-start | bytes 393224 | tf_op jit(solution)/shard_map/ppermute | solution.py:646
  51.9 0.8 %collective-permute-done.6.rest_0_ = bf16[2,64,512]{2,1,0:T(8,128)(2,1)S(1)} collective-permute-done((bf16[2,64,512]{2,1,0:T(8,128)(2,1)S(1)}, bf16[2,64,512]{2,1,0:T(8,128)(2,1)S(1)}, u32[]{:S(2)}, u32[]{:S(2)}) %collective-permute-start.6) | collective-permute-done | bytes 131104 | tf_op jit(solution)/shard_map/ppermute | solution.py:646
  52.7 3.1 %collective-permute-done.7.rest_1_ = bf16[2,64,512]{2,1,0:T(8,128)(2,1)S(1)} collective-permute-done((bf16[2,64,512]{2,1,0:T(8,128)(2,1)S(1)}, bf16[2,64,512]{2,1,0:T(8,128)(2,1)S(1)}, u32[]{:S(2)}, u32[]{:S(2)}) %collective-permute-start.7) | collective-permute-done | bytes 131104 | tf_op jit(solution)/shard_map/ppermute | solution.py:646
  55.8 0.0 collective-permute-done.8.rest_2_
  55.8 0.1 sum_tensor.1
  55.9 1.4 %collective-permute-start.9 = (bf16[64,512]{1,0:T(8,128)(2,1)S(1)}, bf16[64,512]{1,0:T(8,128)(2,1)S(1)}, u32[]{:S(2)}, u32[]{:S(2)}) collective-permute-start(bf16[64,512]{1,0:T(8,128)(2,1)S(1)} %get-tuple-element.52), channel_id=1, source_target_pairs={{0,2},{2,0},{1,3},{3,1},{4,6},{6,4},{5,7},{7,5},{8,10},{10,8},{9,1... | collective-permute-start | bytes 196616 | tf_op jit(solution)/shard_map/ppermute | solution.py:589
  57.3 3.3 %collective-permute-done.9.two_ref = bf16[64,512]{1,0:T(8,128)(2,1)S(1)} collective-permute-done((bf16[64,512]{1,0:T(8,128)(2,1)S(1)}, bf16[64,512]{1,0:T(8,128)(2,1)S(1)}, u32[]{:S(2)}, u32[]{:S(2)}) %collective-permute-start.9) | collective-permute-done | bytes 65568 | tf_op jit(solution)/shard_map/ppermute | solution.py:589
  60.6 0.7 %sum_shares.1 = bf16[32,2,512]{2,1,0:T(2,128)(2,1)} custom-call(f32[64,512]{1,0:T(8,128)S(1)} %get-tuple-element.51.one_ref, bf16[64,512]{1,0:T(8,128)(2,1)S(1)} %collective-permute-done.9.two_ref), custom_call_target="tpu_custom_call" | custom-call | tf_op jit(solution)/shard_map/sum_shares/pallas_call | solution.py:577
  (3 shorter events, 0.0 us)
Async XLA Ops:
  0.0 4.3 %collective-permute-start.1 = (bf16[8,2,1024]{2,1,0:T(2,128)(2,1)}, bf16[8,2,1024]{2,1,0:T(2,128)(2,1)S(1)}, u32[]{:S(2)}, u32[]{:S(2)}) collective-permute-start(bf16[8,2,1024]{2,1,0:T(2,128)(2,1)} %q_hbm.3), channel_id=1, source_target_pairs={{0,1},{1,0},{2,3},{3,2},{4,5},{5,4},{6,7},{7,6},{8,9},{9,8},{10,11... | collective-permute-start | bytes 98312 | tf_op jit(solution)/shard_map/ppermute | solution.py:589
  5.1 18.7 %all-to-all-start = ((bf16[32,16,128]{2,1,0:T(8,128)(2,1)}), bf16[32,16,128]{2,1,0:T(8,128)(2,1)S(1)}, u32[]{:S(2)}, u32[]{:S(2)}) async-start(bf16[32,16,128]{2,1,0:T(8,128)(2,1)} %bitcast.1), calls=%async_computation | async-start | bytes 262144 | tf_op jit(solution)/shard_map/all_to_all | solution.py:615
  14.4 6.5 %copy-start.2 = (s32[1,32]{1,0:T(1,128)S(1)}, s32[1,32]{1,0:T(1,128)}, u32[]{:S(2)}) copy-start(s32[1,32]{1,0:T(1,128)} %place_hbm.1) | copy-start | bytes 388
  14.5 9.4 %copy-start = (bf16[2,1024,128]{2,1,0:T(8,128)(2,1)S(1)}, bf16[2,1024,128]{2,1,0:T(8,128)(2,1)}, u32[]{:S(2)}) copy-start(bf16[2,1024,128]{2,1,0:T(8,128)(2,1)} %k_own) | copy-start | bytes 1572868
  14.5 9.4 %copy-start.1 = (bf16[2,1024,128]{2,1,0:T(8,128)(2,1)S(1)}, bf16[2,1024,128]{2,1,0:T(8,128)(2,1)}, u32[]{:S(2)}) copy-start(bf16[2,1024,128]{2,1,0:T(8,128)(2,1)} %v_own) | copy-start | bytes 1572868
  14.5 9.4 %collective-permute-start.2 = (bf16[2,1024,128]{2,1,0:T(8,128)(2,1)}, bf16[2,1024,128]{2,1,0:T(8,128)(2,1)S(1)}, u32[]{:S(2)}, u32[]{:S(2)}) collective-permute-start(bf16[2,1024,128]{2,1,0:T(8,128)(2,1)} %k_own), channel_id=1, source_target_pairs={{0,1},{1,0},{2,3},{3,2},{4,5},{5,4},{6,7},{7,6},{8,9},{9,8},{10,11... | collective-permute-start | bytes 1572872 | tf_op jit(solution)/shard_map/ppermute | solution.py:589
  15.2 8.7 %collective-permute-start.3 = (bf16[2,1024,128]{2,1,0:T(8,128)(2,1)}, bf16[2,1024,128]{2,1,0:T(8,128)(2,1)S(1)}, u32[]{:S(2)}, u32[]{:S(2)}) collective-permute-start(bf16[2,1024,128]{2,1,0:T(8,128)(2,1)} %v_own), channel_id=1, source_target_pairs={{0,1},{1,0},{2,3},{3,2},{4,5},{5,4},{6,7},{7,6},{8,9},{9,8},{10,11... | collective-permute-start | bytes 1572872 | tf_op jit(solution)/shard_map/ppermute | solution.py:589
  20.4 5.2 %collective-permute-start = (bf16[128,128]{1,0:T(8,128)(2,1)S(1)}, bf16[128,128]{1,0:T(8,128)(2,1)S(1)}, u32[]{:S(2)}, u32[]{:S(2)}) collective-permute-start(bf16[128,128]{1,0:T(8,128)(2,1)S(1)} %get-tuple-element.29), channel_id=1, source_target_pairs={{0,1},{1,0},{2,3},{3,2},{4,5},{5,4},{6,7},{7,6},{8,9},{9,8},{10,11... | collective-permute-start | bytes 98312 | tf_op jit(solution)/shard_map/ppermute | solution.py:589
  25.6 16.0 %all-to-all-start.1 = ((bf16[32,16,128]{2,1,0:T(8,128)(2,1)}), bf16[32,16,128]{2,1,0:T(8,128)(2,1)S(1)}, u32[]{:S(2)}, u32[]{:S(2)}) async-start(bf16[32,16,128]{2,1,0:T(8,128)(2,1)} %bitcast.3), calls=%async_computation.1 | async-start | bytes 262144 | tf_op jit(solution)/shard_map/all_to_all | solution.py:627
  32.2 6.1 %collective-permute-start.4 = (bf16[128,128]{1,0:T(8,128)(2,1)S(1)}, bf16[128,128]{1,0:T(8,128)(2,1)S(1)}, u32[]{:S(2)}, u32[]{:S(2)}) collective-permute-start(bf16[128,128]{1,0:T(8,128)(2,1)S(1)} %pad_maximum_fusion), channel_id=1, source_target_pairs={{0,2},{2,0},{1,3},{3,1},{4,6},{6,4},{5,7},{7,5},{8,10},{10,8},{9,1... | collective-permute-start | bytes 98312 | tf_op jit(solution)/shard_map/ppermute | solution.py:589
  42.4 3.7 %collective-permute-start.5 = (bf16[8,64,512]{2,1,0:T(8,128)(2,1)S(1)}, bf16[8,64,512]{2,1,0:T(8,128)(2,1)S(1)}, u32[]{:S(2)}, u32[]{:S(2)}) collective-permute-start(bf16[8,64,512]{2,1,0:T(8,128)(2,1)S(1)} %get-tuple-element.46), channel_id=1, source_target_pairs={{0,1},{1,0},{2,3},{3,2},{4,5},{5,4},{6,7},{7,6},{8,9},{9,8},{10,11... | collective-permute-start | bytes 1572872 | tf_op jit(solution)/shard_map/ppermute | solution.py:589
  46.2 6.5 %collective-permute-start.6 = (bf16[2,64,512]{2,1,0:T(8,128)(2,1)S(1)}, bf16[2,64,512]{2,1,0:T(8,128)(2,1)S(1)}, u32[]{:S(2)}, u32[]{:S(2)}) collective-permute-start(bf16[2,64,512]{2,1,0:T(8,128)(2,1)S(1)} %get-tuple-element.48), channel_id=1, source_target_pairs={{0,128},{64,192},{128,0},{192,64},{1,129},{65,193},{129,1},{193,65... | collective-permute-start | bytes 393224 | tf_op jit(solution)/shard_map/ppermute | solution.py:646
  49.2 6.6 %collective-permute-start.7 = (bf16[2,64,512]{2,1,0:T(8,128)(2,1)S(1)}, bf16[2,64,512]{2,1,0:T(8,128)(2,1)S(1)}, u32[]{:S(2)}, u32[]{:S(2)}) collective-permute-start(bf16[2,64,512]{2,1,0:T(8,128)(2,1)S(1)} %get-tuple-element.49), channel_id=1, source_target_pairs={{0,64},{64,128},{128,192},{192,0},{1,65},{65,129},{129,193},{193,1... | collective-permute-start | bytes 393224 | tf_op jit(solution)/shard_map/ppermute | solution.py:646
  49.6 6.2 %collective-permute-start.8 = (bf16[2,64,512]{2,1,0:T(8,128)(2,1)S(1)}, bf16[2,64,512]{2,1,0:T(8,128)(2,1)S(1)}, u32[]{:S(2)}, u32[]{:S(2)}) collective-permute-start(bf16[2,64,512]{2,1,0:T(8,128)(2,1)S(1)} %get-tuple-element.50), channel_id=1, source_target_pairs={{0,192},{64,0},{128,64},{192,128},{1,193},{65,1},{129,65},{193,129... | collective-permute-start | bytes 393224 | tf_op jit(solution)/shard_map/ppermute | solution.py:646
  55.9 4.7 %collective-permute-start.9 = (bf16[64,512]{1,0:T(8,128)(2,1)S(1)}, bf16[64,512]{1,0:T(8,128)(2,1)S(1)}, u32[]{:S(2)}, u32[]{:S(2)}) collective-permute-start(bf16[64,512]{1,0:T(8,128)(2,1)S(1)} %get-tuple-element.52), channel_id=1, source_target_pairs={{0,2},{2,0},{1,3},{3,1},{4,6},{6,4},{5,7},{7,5},{8,10},{10,8},{9,1... | collective-permute-start | bytes 196616 | tf_op jit(solution)/shard_map/ppermute | solution.py:589

commit v8 on v7

--- a/solution.py
+++ b/solution.py
@@ -404,7 +404,9 @@
     return pl.ds(pl.multiple_of(block * width, width), width)
 
 
-def collect_kernel(place_ref, keep_ref, near_ref, far_ref, value_ref, level_ref, own):
+def collect_kernel(
+    place_ref, col_ref, keep_ref, near_ref, far_ref, value_ref, level_ref, pick_ref, own
+):
     xh, core, _ = here()
     owners = value_ref.shape[0]
     count = keep_ref.shape[0] // 8
@@ -421,26 +423,33 @@
     value_ref[...] = jnp.where(lower, one, pltpu.roll(two, 4, 1))
     level = join_stat(jnp.where(lower, pltpu.roll(one, 4, 1), two))
     level_ref[...] = jnp.broadcast_to(level, level_ref.shape)
-
-
-def collect_suffix(placement, pieces, owners):
+    lane = lax.broadcasted_iota(jnp.int32, pick_ref.shape[1:], 1)
+    for h in range(2):
+        pick_ref[h] = jnp.where(lane == col_ref[...] + 2 * h, 1.0, 0.0).astype(BF16)
+
+
+def collect_suffix(placement, columns, pieces, owners):
     part = jax.ShapeDtypeStruct((owners, 8, D), F32)
     return pl.pallas_call(
         collect_kernel,
-        in_specs=[SMEM_SPEC] + [VMEM_SPEC] * 3,
-        out_specs=[VMEM_SPEC] * 2,
-        out_shape=[part, part],
+        in_specs=[SMEM_SPEC] + [VMEM_SPEC] * 4,
+        out_specs=[VMEM_SPEC] * 3,
+        out_shape=[
+            part,
+            part,
+            jax.ShapeDtypeStruct((2, columns.shape[0], owners * 8), BF16),
+        ],
         scratch_shapes=[pltpu.VMEM((placement.shape[1], 8, D), F32)],
         cost_estimate=pl.CostEstimate(
             flops=0, bytes_accessed=1024 * 1024, transcendentals=0
         ),
         compiler_params=PARAMS,
         name="collect_suffix",
-    )(placement, *pieces)
+    )(placement, columns, *pieces)
 
 
 def merge_kernel(
-    col_ref, parts_ref, value_ref, level_ref, upper_ref, low_ref, out_ref, att_ref
+    parts_ref, value_ref, level_ref, pick_ref, upper_ref, low_ref, out_ref, att_ref
 ):
     me_ref = here()
     core = me_ref[1]
@@ -462,10 +471,8 @@
         total = total + weight
         numer = numer + value * weight
     merged = (numer / total).astype(BF16).reshape(owners * 8, D)
-    lane = lax.broadcasted_iota(jnp.int32, (out_rows, owners * 8), 1)
     for h in range(2):
-        pick = jnp.where(lane == col_ref[...] + 2 * h, 1.0, 0.0).astype(BF16)
-        att_ref[:, h * D : (h + 1) * D] = dot(pick, merged).astype(BF16)
+        att_ref[:, h * D : (h + 1) * D] = dot(pick_ref[h], merged).astype(BF16)
     half = low_ref.shape[1]
     for b in range(blocks):
         columns = block_columns(me_ref, b, 1 - core, width)
@@ -473,9 +480,8 @@
         out_ref[b] = (value + dot(att_ref[:, half:], low_ref[b])).astype(BF16)
 
 
-def merge_and_project(columns, parts, suffix, upper, low):
+def merge_and_project(out_rows, parts, suffix, upper, low):
     blocks, half, width = low.shape
-    out_rows = columns.shape[0]
     return pl.pallas_call(
         merge_kernel,
         in_specs=[VMEM_SPEC] * 6,
@@ -486,7 +492,7 @@
         ],
         compiler_params=PARAMS,
         name="merge_and_project",
-    )(columns, parts, *suffix, upper, low)
+    )(parts, *suffix, upper, low)
 
 
 def project_kernel(att_ref, upper_ref, low_hbm, out_ref, low_ref, sem):
@@ -632,9 +638,9 @@
         slots * tokens, 1
     )
     away, attention = merge_and_project(
-        columns,
+        slots * tokens,
         returned.reshape(indices, 2, 16, D),
-        collect_suffix(place_here, (keep, near, far), indices),
+        collect_suffix(place_here, columns, (keep, near, far), indices),
         upper,
         low_away,
     )

time: 62.1 us -> 62.1 us (level)
  waiting for transfers between devices: 13.1 us -> 12.4 us
  local copies, waits for them, and re-layouts: 0.1 us -> 0.75 us
    all_to_all x1, waiting for transfers between devices: 2.58 us -> 1.91 us  [body(): lax.all_to_all(parts.reshape(indices * 2, 16, D), ('prompt', 'xh'), split...]
    unnamed x6 -> x10, local copies, waits for them, and re-layouts: 0.02 us -> 0.68 us
where the time goes in v8:
time: 62.1 us; the launch traced here: 61.2 us
  starting transfers between devices  32.3 us (52%)
  Pallas kernels  15.5 us (25%)
  waiting for transfers between devices  12.4 us (20%)
  local copies, waits for them, and re-layouts  0.75 us (1%)
    ppermute x7, starting transfers between devices, swap(): return lax.ppermute(value, axes, [(i, size - 1 - i) for i in range(size)])  10.8 us
    all_to_all x1, starting transfers between devices, body(): lax.all_to_all(routed.reshape(indices * 2, 16, D), ('prompt', 'xh'), spli...  9.3 us
    all_to_all x1, starting transfers between devices, body(): lax.all_to_all(parts.reshape(indices * 2, 16, D), ('prompt', 'xh'), split...  6.57 us
    ppermute x3, starting transfers between devices, body(): lax.ppermute(shares[b - 1], 'tensor', [(i, (i + b) % steps) for i in rang...  5.68 us
    pallas_call x1, Pallas kernels, suffix_attention(): pl.pallas_call(suffix_kernel, in_specs=[HBM_SPEC] * 6, out_specs=[VMEM_SP...  5.09 us
    ppermute x3, waiting for transfers between devices, body(): lax.ppermute(shares[b - 1], 'tensor', [(i, (i + b) % steps) for i in rang...  3.96 us
    ppermute x7, waiting for transfers between devices, swap(): return lax.ppermute(value, axes, [(i, size - 1 - i) for i in range(size)])  3.54 us
    pallas_call x1, Pallas kernels, stage_weight(): pl.pallas_call(stage_kernel, in_specs=[HBM_SPEC, pl.BlockSpec(memory_spac...  3.13 us
  transfers between devices with their start and end apart: 12, of which 6 were waited for; matrix products, arithmetic and copies ran while one was open for 0% of the time, Pallas kernels for 22%

profile of v8, /device:TPU:1, one launch (start us, length us, event | category | flops | bytes accessed | tf_op | source)
XLA Modules:
  0.0 61.2 jit_solution(12917038727577929407)
XLA Ops:
  0.0 3.2 %collective-permute-start.1 = (bf16[8,2,1024]{2,1,0:T(2,128)(2,1)}, bf16[8,2,1024]{2,1,0:T(2,128)(2,1)S(1)}, u32[]{:S(2)}, u32[]{:S(2)}) collective-permute-start(bf16[8,2,1024]{2,1,0:T(2,128)(2,1)} %q_hbm.3), channel_id=1, source_target_pairs={{0,1},{1,0},{2,3},{3,2},{4,5},{5,4},{6,7},{7,6},{8,9},{9,8},{10,11... | collective-permute-start | bytes 98312 | tf_op jit(solution)/shard_map/ppermute | solution.py:595
  3.2 0.8 %own_rows.1 = (f32[32,8,128]{2,1,0:T(8,128)S(1)}, s32[1,32]{1,0:T(1,128)S(1)}, bf16[256,128]{1,0:T(8,128)(2,1)S(1)}) custom-call(s32[1,32]{1,0:T(1,128)} %place_hbm.1, bf16[8,2,1024]{2,1,0:T(2,128)(2,1)} %q_hbm.3), custom_call_target="tpu_custom_call" | custom-call | bytes 2097152 | tf_op jit(solution)/shard_map/own_rows/pallas_call | solution.py:106
  4.1 0.0 copy-start.2
  4.1 0.2 collective-permute-done.1.other_ref
  4.3 0.8 %route_queries.1 = bf16[16,2,16,128]{3,2,1,0:T(8,128)(2,1)} custom-call(bf16[256,128]{1,0:T(8,128)(2,1)S(1)} %get-tuple-element.31.pick_ref, f32[32,8,128]{2,1,0:T(8,128)S(1)} %get-tuple-element.32.own_ref, bf16[8,2,1024]{2,1,0:T(2,128)(2,1)S(1)} %collective-permute-done.1.other_ref), custom_call_target="tpu_custom_call" | custom-call | tf_op jit(solution)/shard_map/route_queries/pallas_call | solution.py:143
  5.1 0.0 copy-done.2
  5.1 9.3 %all-to-all-start = ((bf16[32,16,128]{2,1,0:T(8,128)(2,1)}), bf16[32,16,128]{2,1,0:T(8,128)(2,1)S(1)}, u32[]{:S(2)}, u32[]{:S(2)}) async-start(bf16[32,16,128]{2,1,0:T(8,128)(2,1)} %bitcast), calls=%async_computation | async-start | bytes 262144 | tf_op jit(solution)/shard_map/all_to_all | solution.py:621
  14.4 0.0 copy-start.4
  14.5 0.0 copy-start
  14.5 0.0 copy-start.1
  14.5 0.7 %collective-permute-start.2 = (bf16[2,1024,128]{2,1,0:T(8,128)(2,1)}, bf16[2,1024,128]{2,1,0:T(8,128)(2,1)S(1)}, u32[]{:S(2)}, u32[]{:S(2)}) collective-permute-start(bf16[2,1024,128]{2,1,0:T(8,128)(2,1)} %k_own), channel_id=1, source_target_pairs={{0,1},{1,0},{2,3},{3,2},{4,5},{5,4},{6,7},{7,6},{8,9},{9,8},{10,11... | collective-permute-start | bytes 1572872 | tf_op jit(solution)/shard_map/ppermute | solution.py:595
  15.2 0.1 collective-permute-start.3
  15.3 5.1 %suffix_attention.1 = (bf16[64,128]{1,0:T(8,128)(2,1)S(1)}, bf16[128,128]{1,0:T(8,128)(2,1)S(1)}, bf16[64,128]{1,0:T(8,128)(2,1)S(1)}) custom-call(s32[8]{0:T(128)} %len_hbm.1, bf16[8,2,1024]{2,1,0:T(2,128)(2,1)} %q_hbm.3, bf16[8,2,128]{2,1,0:T(2,128)(2,1)} %sk_hbm.1, bf16[8,2,128]{2,1,0:T(2,128)(2,1)} %sv_hbm.1, bf16[8,2048,128]{2,1,0:T(8,128)(2,1)} %k_hbm.1, ...), custom_call_target="tpu_custom_call" | custom-call | flops 8589934592 | bytes 8388608 | tf_op jit(solution)/shard_map/suffix_attention/pallas_call | solution.py:259
  20.4 0.5 collective-permute-start
  20.9 0.0 copy-done.4
  20.9 3.0 %all-to-all-done = bf16[32,16,128]{2,1,0:T(8,128)(2,1)S(1)} async-done(((bf16[32,16,128]{2,1,0:T(8,128)(2,1)}), bf16[32,16,128]{2,1,0:T(8,128)(2,1)S(1)}, u32[]{:S(2)}, u32[]{:S(2)}) %all-to-all-start) | async-done | bytes 131104 | tf_op jit(solution)/shard_map/all_to_all | solution.py:621
  23.9 0.0 collective-permute-done.2.k_other
  23.9 0.0 collective-permute-done.3.v_other
  23.9 0.0 copy-done
  23.9 0.0 copy-done.1
  23.9 1.7 %prefix_attention.1.after_ref = bf16[16,2,16,128]{3,2,1,0:T(8,128)(2,1)} custom-call(bf16[16,2,16,128]{3,2,1,0:T(8,128)(2,1)S(1)} %bitcast.6, bf16[2,1024,128]{2,1,0:T(8,128)(2,1)S(1)} %copy-done, bf16[2,1024,128]{2,1,0:T(8,128)(2,1)S(1)} %collective-permute-done.2.k_other, bf16[2,1024,128]{2,1,0:T(8,128)(2,1)S(1)} %copy-done.1, ...), custom_call_target="tpu_custom_call" | custom-call | tf_op jit(solution)/shard_map/prefix_attention/pallas_call | solution.py:328
  25.6 0.0 collective-permute-done.near_ref
  25.6 6.6 %all-to-all-start.1 = ((bf16[32,16,128]{2,1,0:T(8,128)(2,1)}), bf16[32,16,128]{2,1,0:T(8,128)(2,1)S(1)}, u32[]{:S(2)}, u32[]{:S(2)}) async-start(bf16[32,16,128]{2,1,0:T(8,128)(2,1)} %bitcast.2), calls=%async_computation.1 | async-start | bytes 262144 | tf_op jit(solution)/shard_map/all_to_all | solution.py:633
  32.2 2.8 %collective-permute-start.4 = (bf16[128,128]{1,0:T(8,128)(2,1)S(1)}, bf16[128,128]{1,0:T(8,128)(2,1)S(1)}, u32[]{:S(2)}, u32[]{:S(2)}) collective-permute-start(bf16[128,128]{1,0:T(8,128)(2,1)S(1)} %pad_maximum_fusion), channel_id=1, source_target_pairs={{0,2},{2,0},{1,3},{3,1},{4,6},{6,4},{5,7},{7,5},{8,10},{10,8},{9,1... | collective-permute-start | bytes 98312 | tf_op jit(solution)/shard_map/ppermute | solution.py:595
  35.0 0.1 iota_add_fusion
  35.1 0.1 add.27.col_ref
  35.2 3.1 %stage_weight.1 = (bf16[128,8192]{1,0:T(8,128)(2,1)S(1)}, bf16[8,128,512]{2,1,0:T(8,128)(2,1)S(1)}, bf16[8,128,512]{2,1,0:T(8,128)(2,1)}) custom-call(bf16[256,8192]{1,0:T(8,128)(2,1)} %w_hbm.1, bf16[16,2,16,128]{3,2,1,0:T(8,128)(2,1)} %prefix_attention.1.after_ref), custom_call_target="tpu_custom_call" | custom-call | bytes 10485760 | tf_op jit(solution)/shard_map/stage_weight/pallas_call | solution.py:376
  38.3 0.0 collective-permute-done.4.far_ref
  38.3 0.0 copy-start.3
  38.3 0.6 %copy-done.3 = s32[1,32]{1,0:T(1,128)S(1)} copy-done((s32[1,32]{1,0:T(1,128)S(1)}, s32[1,32]{1,0:T(1,128)}, u32[]{:S(2)}) %copy-start.3) | copy-done | bytes 152
  39.0 0.8 %collect_suffix.1 = (f32[16,8,128]{2,1,0:T(8,128)S(1)}, f32[16,8,128]{2,1,0:T(8,128)S(1)}, bf16[2,64,128]{2,1,0:T(8,128)(2,1)S(1)}) custom-call(s32[1,32]{1,0:T(1,128)S(1)} %copy-done.3, s32[64,1]{1,0:T(8,128)S(1)} %add.27.col_ref, bf16[64,128]{1,0:T(8,128)(2,1)S(1)} %get-tuple-element.38.keep_ref, bf16[128,128]{1,0:T(8,128)(2,1)S(1)} %collective-permute-done.near_ref, ...), custom_call_target="tpu_custom_call" | custom-call | bytes 1048576 | tf_op jit(solution)/shard_map/collect_suffix/pallas_call | solution.py:433
  39.7 1.9 %all-to-all-done.1 = bf16[32,16,128]{2,1,0:T(8,128)(2,1)S(1)} async-done(((bf16[32,16,128]{2,1,0:T(8,128)(2,1)}), bf16[32,16,128]{2,1,0:T(8,128)(2,1)S(1)}, u32[]{:S(2)}, u32[]{:S(2)}) %all-to-all-start.1) | async-done | bytes 131104 | tf_op jit(solution)/shard_map/all_to_all | solution.py:633
  41.6 0.7 %merge_and_project.1 = (bf16[8,64,512]{2,1,0:T(8,128)(2,1)S(1)}, bf16[64,256]{1,0:T(8,128)(2,1)S(1)}) custom-call(bf16[16,2,16,128]{3,2,1,0:T(8,128)(2,1)S(1)} %bitcast.7, f32[16,8,128]{2,1,0:T(8,128)S(1)} %get-tuple-element.41.value_ref, f32[16,8,128]{2,1,0:T(8,128)S(1)} %get-tuple-element.42.level_ref, bf16[2,64,128]{2,1,0:T(8,128)(2,1)S(1)} %get-tuple-element.43.pick_ref, ...), custom_call_target="tpu_custom_call" | custom-call | tf_op jit(solution)/shard_map/merge_and_project/pallas_call | solution.py:485
  42.4 2.0 %collective-permute-start.5 = (bf16[8,64,512]{2,1,0:T(8,128)(2,1)S(1)}, bf16[8,64,512]{2,1,0:T(8,128)(2,1)S(1)}, u32[]{:S(2)}, u32[]{:S(2)}) collective-permute-start(bf16[8,64,512]{2,1,0:T(8,128)(2,1)S(1)} %get-tuple-element.48), channel_id=1, source_target_pairs={{0,1},{1,0},{2,3},{3,2},{4,5},{5,4},{6,7},{7,6},{8,9},{9,8},{10,11... | collective-permute-start | bytes 1572872 | tf_op jit(solution)/shard_map/ppermute | solution.py:595
  44.4 1.7 %project.1.one_ref = f32[8,64,512]{2,1,0:T(8,128)S(1)} custom-call(bf16[64,256]{1,0:T(8,128)(2,1)S(1)} %get-tuple-element.46.att_ref, bf16[128,8192]{1,0:T(8,128)(2,1)S(1)} %get-tuple-element.44.upper_ref, bf16[8,128,512]{2,1,0:T(8,128)(2,1)} %get-tuple-element.47.low_hbm), custom_call_target="tpu_custom_call" | custom-call | flops 1073741824 | bytes 2097152 | tf_op jit(solution)/shard_map/project/pallas_call | solution.py:518
  46.1 0.0 collective-permute-done.5.two_ref
  46.1 0.1 add_halves.1
  46.2 3.0 %collective-permute-start.6 = (bf16[2,64,512]{2,1,0:T(8,128)(2,1)S(1)}, bf16[2,64,512]{2,1,0:T(8,128)(2,1)S(1)}, u32[]{:S(2)}, u32[]{:S(2)}) collective-permute-start(bf16[2,64,512]{2,1,0:T(8,128)(2,1)S(1)} %get-tuple-element.50), channel_id=1, source_target_pairs={{0,128},{64,192},{128,0},{192,64},{1,129},{65,193},{129,1},{193,65... | collective-permute-start | bytes 393224 | tf_op jit(solution)/shard_map/ppermute | solution.py:652
  49.2 0.4 collective-permute-start.7
  49.6 2.3 %collective-permute-start.8 = (bf16[2,64,512]{2,1,0:T(8,128)(2,1)S(1)}, bf16[2,64,512]{2,1,0:T(8,128)(2,1)S(1)}, u32[]{:S(2)}, u32[]{:S(2)}) collective-permute-start(bf16[2,64,512]{2,1,0:T(8,128)(2,1)S(1)} %get-tuple-element.52), channel_id=1, source_target_pairs={{0,192},{64,0},{128,64},{192,128},{1,193},{65,1},{129,65},{193,129... | collective-permute-start | bytes 393224 | tf_op jit(solution)/shard_map/ppermute | solution.py:652
  51.9 0.8 %collective-permute-done.6.rest_0_ = bf16[2,64,512]{2,1,0:T(8,128)(2,1)S(1)} collective-permute-done((bf16[2,64,512]{2,1,0:T(8,128)(2,1)S(1)}, bf16[2,64,512]{2,1,0:T(8,128)(2,1)S(1)}, u32[]{:S(2)}, u32[]{:S(2)}) %collective-permute-start.6) | collective-permute-done | bytes 131104 | tf_op jit(solution)/shard_map/ppermute | solution.py:652
  52.7 3.1 %collective-permute-done.7.rest_1_ = bf16[2,64,512]{2,1,0:T(8,128)(2,1)S(1)} collective-permute-done((bf16[2,64,512]{2,1,0:T(8,128)(2,1)S(1)}, bf16[2,64,512]{2,1,0:T(8,128)(2,1)S(1)}, u32[]{:S(2)}, u32[]{:S(2)}) %collective-permute-start.7) | collective-permute-done | bytes 131104 | tf_op jit(solution)/shard_map/ppermute | solution.py:652
  55.8 0.0 collective-permute-done.8.rest_2_
  55.8 0.1 sum_tensor.1
  55.9 1.4 %collective-permute-start.9 = (bf16[64,512]{1,0:T(8,128)(2,1)S(1)}, bf16[64,512]{1,0:T(8,128)(2,1)S(1)}, u32[]{:S(2)}, u32[]{:S(2)}) collective-permute-start(bf16[64,512]{1,0:T(8,128)(2,1)S(1)} %get-tuple-element.54), channel_id=1, source_target_pairs={{0,2},{2,0},{1,3},{3,1},{4,6},{6,4},{5,7},{7,5},{8,10},{10,8},{9,1... | collective-permute-start | bytes 196616 | tf_op jit(solution)/shard_map/ppermute | solution.py:595
  57.3 3.3 %collective-permute-done.9.two_ref = bf16[64,512]{1,0:T(8,128)(2,1)S(1)} collective-permute-done((bf16[64,512]{1,0:T(8,128)(2,1)S(1)}, bf16[64,512]{1,0:T(8,128)(2,1)S(1)}, u32[]{:S(2)}, u32[]{:S(2)}) %collective-permute-start.9) | collective-permute-done | bytes 65568 | tf_op jit(solution)/shard_map/ppermute | solution.py:595
  60.6 0.7 %sum_shares.1 = bf16[32,2,512]{2,1,0:T(2,128)(2,1)} custom-call(f32[64,512]{1,0:T(8,128)S(1)} %get-tuple-element.53.one_ref, bf16[64,512]{1,0:T(8,128)(2,1)S(1)} %collective-permute-done.9.two_ref), custom_call_target="tpu_custom_call" | custom-call | tf_op jit(solution)/shard_map/sum_shares/pallas_call | solution.py:583
  (3 shorter events, 0.0 us)
Async XLA Ops:
  0.0 4.3 %collective-permute-start.1 = (bf16[8,2,1024]{2,1,0:T(2,128)(2,1)}, bf16[8,2,1024]{2,1,0:T(2,128)(2,1)S(1)}, u32[]{:S(2)}, u32[]{:S(2)}) collective-permute-start(bf16[8,2,1024]{2,1,0:T(2,128)(2,1)} %q_hbm.3), channel_id=1, source_target_pairs={{0,1},{1,0},{2,3},{3,2},{4,5},{5,4},{6,7},{7,6},{8,9},{9,8},{10,11... | collective-permute-start | bytes 98312 | tf_op jit(solution)/shard_map/ppermute | solution.py:595
  4.1 1.1 %copy-start.2 = (s32[1,32]{1,0:T(1,128)}, s32[1,32]{1,0:T(1,128)S(1)}, u32[]{:S(2)}) copy-start(s32[1,32]{1,0:T(1,128)S(1)} %get-tuple-element.37.place_ref) | copy-start | bytes 388
  5.1 18.7 %all-to-all-start = ((bf16[32,16,128]{2,1,0:T(8,128)(2,1)}), bf16[32,16,128]{2,1,0:T(8,128)(2,1)S(1)}, u32[]{:S(2)}, u32[]{:S(2)}) async-start(bf16[32,16,128]{2,1,0:T(8,128)(2,1)} %bitcast), calls=%async_computation | async-start | bytes 262144 | tf_op jit(solution)/shard_map/all_to_all | solution.py:621
  14.4 6.5 %copy-start.4 = (s32[1,32]{1,0:T(1,128)S(1)}, s32[1,32]{1,0:T(1,128)}, u32[]{:S(2)}) copy-start(s32[1,32]{1,0:T(1,128)} %place_hbm.1) | copy-start | bytes 388
  14.5 9.4 %copy-start = (bf16[2,1024,128]{2,1,0:T(8,128)(2,1)S(1)}, bf16[2,1024,128]{2,1,0:T(8,128)(2,1)}, u32[]{:S(2)}) copy-start(bf16[2,1024,128]{2,1,0:T(8,128)(2,1)} %k_own) | copy-start | bytes 1572868
  14.5 9.4 %copy-start.1 = (bf16[2,1024,128]{2,1,0:T(8,128)(2,1)S(1)}, bf16[2,1024,128]{2,1,0:T(8,128)(2,1)}, u32[]{:S(2)}) copy-start(bf16[2,1024,128]{2,1,0:T(8,128)(2,1)} %v_own) | copy-start | bytes 1572868
  14.5 9.4 %collective-permute-start.2 = (bf16[2,1024,128]{2,1,0:T(8,128)(2,1)}, bf16[2,1024,128]{2,1,0:T(8,128)(2,1)S(1)}, u32[]{:S(2)}, u32[]{:S(2)}) collective-permute-start(bf16[2,1024,128]{2,1,0:T(8,128)(2,1)} %k_own), channel_id=1, source_target_pairs={{0,1},{1,0},{2,3},{3,2},{4,5},{5,4},{6,7},{7,6},{8,9},{9,8},{10,11... | collective-permute-start | bytes 1572872 | tf_op jit(solution)/shard_map/ppermute | solution.py:595
  15.2 8.7 %collective-permute-start.3 = (bf16[2,1024,128]{2,1,0:T(8,128)(2,1)}, bf16[2,1024,128]{2,1,0:T(8,128)(2,1)S(1)}, u32[]{:S(2)}, u32[]{:S(2)}) collective-permute-start(bf16[2,1024,128]{2,1,0:T(8,128)(2,1)} %v_own), channel_id=1, source_target_pairs={{0,1},{1,0},{2,3},{3,2},{4,5},{5,4},{6,7},{7,6},{8,9},{9,8},{10,11... | collective-permute-start | bytes 1572872 | tf_op jit(solution)/shard_map/ppermute | solution.py:595
  20.4 5.2 %collective-permute-start = (bf16[128,128]{1,0:T(8,128)(2,1)S(1)}, bf16[128,128]{1,0:T(8,128)(2,1)S(1)}, u32[]{:S(2)}, u32[]{:S(2)}) collective-permute-start(bf16[128,128]{1,0:T(8,128)(2,1)S(1)} %get-tuple-element.30), channel_id=1, source_target_pairs={{0,1},{1,0},{2,3},{3,2},{4,5},{5,4},{6,7},{7,6},{8,9},{9,8},{10,11... | collective-permute-start | bytes 98312 | tf_op jit(solution)/shard_map/ppermute | solution.py:595
  25.6 16.0 %all-to-all-start.1 = ((bf16[32,16,128]{2,1,0:T(8,128)(2,1)}), bf16[32,16,128]{2,1,0:T(8,128)(2,1)S(1)}, u32[]{:S(2)}, u32[]{:S(2)}) async-start(bf16[32,16,128]{2,1,0:T(8,128)(2,1)} %bitcast.2), calls=%async_computation.1 | async-start | bytes 262144 | tf_op jit(solution)/shard_map/all_to_all | solution.py:633
  32.2 6.1 %collective-permute-start.4 = (bf16[128,128]{1,0:T(8,128)(2,1)S(1)}, bf16[128,128]{1,0:T(8,128)(2,1)S(1)}, u32[]{:S(2)}, u32[]{:S(2)}) collective-permute-start(bf16[128,128]{1,0:T(8,128)(2,1)S(1)} %pad_maximum_fusion), channel_id=1, source_target_pairs={{0,2},{2,0},{1,3},{3,1},{4,6},{6,4},{5,7},{7,5},{8,10},{10,8},{9,1... | collective-permute-start | bytes 98312 | tf_op jit(solution)/shard_map/ppermute | solution.py:595
  38.3 0.7 %copy-start.3 = (s32[1,32]{1,0:T(1,128)S(1)}, s32[1,32]{1,0:T(1,128)}, u32[]{:S(2)}) copy-start(s32[1,32]{1,0:T(1,128)} %copy-done.2) | copy-start | bytes 388
  42.4 3.7 %collective-permute-start.5 = (bf16[8,64,512]{2,1,0:T(8,128)(2,1)S(1)}, bf16[8,64,512]{2,1,0:T(8,128)(2,1)S(1)}, u32[]{:S(2)}, u32[]{:S(2)}) collective-permute-start(bf16[8,64,512]{2,1,0:T(8,128)(2,1)S(1)} %get-tuple-element.48), channel_id=1, source_target_pairs={{0,1},{1,0},{2,3},{3,2},{4,5},{5,4},{6,7},{7,6},{8,9},{9,8},{10,11... | collective-permute-start | bytes 1572872 | tf_op jit(solution)/shard_map/ppermute | solution.py:595
  46.2 6.5 %collective-permute-start.6 = (bf16[2,64,512]{2,1,0:T(8,128)(2,1)S(1)}, bf16[2,64,512]{2,1,0:T(8,128)(2,1)S(1)}, u32[]{:S(2)}, u32[]{:S(2)}) collective-permute-start(bf16[2,64,512]{2,1,0:T(8,128)(2,1)S(1)} %get-tuple-element.50), channel_id=1, source_target_pairs={{0,128},{64,192},{128,0},{192,64},{1,129},{65,193},{129,1},{193,65... | collective-permute-start | bytes 393224 | tf_op jit(solution)/shard_map/ppermute | solution.py:652
  49.2 6.6 %collective-permute-start.7 = (bf16[2,64,512]{2,1,0:T(8,128)(2,1)S(1)}, bf16[2,64,512]{2,1,0:T(8,128)(2,1)S(1)}, u32[]{:S(2)}, u32[]{:S(2)}) collective-permute-start(bf16[2,64,512]{2,1,0:T(8,128)(2,1)S(1)} %get-tuple-element.51), channel_id=1, source_target_pairs={{0,64},{64,128},{128,192},{192,0},{1,65},{65,129},{129,193},{193,1... | collective-permute-start | bytes 393224 | tf_op jit(solution)/shard_map/ppermute | solution.py:652
  49.6 6.2 %collective-permute-start.8 = (bf16[2,64,512]{2,1,0:T(8,128)(2,1)S(1)}, bf16[2,64,512]{2,1,0:T(8,128)(2,1)S(1)}, u32[]{:S(2)}, u32[]{:S(2)}) collective-permute-start(bf16[2,64,512]{2,1,0:T(8,128)(2,1)S(1)} %get-tuple-element.52), channel_id=1, source_target_pairs={{0,192},{64,0},{128,64},{192,128},{1,193},{65,1},{129,65},{193,129... | collective-permute-start | bytes 393224 | tf_op jit(solution)/shard_map/ppermute | solution.py:652
  55.9 4.7 %collective-permute-start.9 = (bf16[64,512]{1,0:T(8,128)(2,1)S(1)}, bf16[64,512]{1,0:T(8,128)(2,1)S(1)}, u32[]{:S(2)}, u32[]{:S(2)}) collective-permute-start(bf16[64,512]{1,0:T(8,128)(2,1)S(1)} %get-tuple-element.54), channel_id=1, source_target_pairs={{0,2},{2,0},{1,3},{3,1},{4,6},{6,4},{5,7},{7,5},{8,10},{10,8},{9,1... | collective-permute-start | bytes 196616 | tf_op jit(solution)/shard_map/ppermute | solution.py:595
